TPU v7x, 32 devices: a whole 2x2x4 slice. The times are simulated.
32 devices in a mesh: grp: 2 (over x), row: 8 (over z, y), col: 2 (over core).
Axes of the slice: x: 2, y: 2, z: 4, core: 2. Of those that a mesh axis runs over, the one named last changes fastest.
Arguments:
- query_window: bfloat16 [16, 8, 128, 1280], P(('grp', 'row'), 'col'), parts along dimension 0, may hold values from -80 to 80
- key_window: bfloat16 [16, 8, 128, 1280], P(('grp', 'row'), 'col'), parts along dimension 0, may hold values from -9 to 9
- value_window: bfloat16 [16, 8, 128, 1280], P(('grp', 'row'), 'col'), parts along dimension 0, may hold values from -6 to 6
- query_index: bfloat16 [16, 8, 128, 1280], P(('grp', 'row'), 'col'), parts along dimension 0, may hold values from -80 to 80
- key_index: bfloat16 [16, 8, 128, 1280], P(('grp', 'row'), 'col'), parts along dimension 0, may hold values from -9 to 9
- proj_weight: bfloat16 [1280, 1024], replicated, may hold values from -0.5 to 0.5
- proj_bias: float32 [1024], replicated, may hold values from -3 to 3
- first_kernel: bfloat16 [3, 3, 256, 256], replicated, may hold values from -0.125 to 0.125
- first_bias: float32 [256], replicated, may hold values from -3 to 3
- second_kernel: bfloat16 [3, 3, 256, 256], replicated, may hold values from -0.125 to 0.125
- second_bias: float32 [256], replicated, may hold values from -3 to 3
Outputs:
- fine_field: bfloat16 [256, 256, 256], P(('grp', 'row'), 'col'), parts along dimension 0
There are 2 independent parts, one for each index of `grp`. A program takes and returns all parts, laid end to end along the dimension named above; an argument that names none is the same for every part. Nothing has to cross between parts.
All inputs are finite; a program needn't handle non-finite values.
Results may differ from a plain program's by a relative error of at most 0.0048.
Values may be sent and summed in bfloat16 or wider, within the bound.
No kernel may reach another device: no remote copies, remote signals or barrier semaphores. Data moves between devices by JAX's collectives and lax.ppermute only.
A program may use at most 64 MiB of HBM per device.

v0:
```python
import math

import jax
import jax.numpy as jnp
from jax import lax
from jax.sharding import PartitionSpec as P

HEADS = 8
HEAD_DIM = 160
CHANNELS = 256
TILE_ROWS = 8
TILE_COLS = 16


def extended(value, sides, width):
    for axis, dim in sides:
        size, length = (lax.axis_size(axis), value.shape[dim])
        up = [(i, (i + 1) % size) for i in range(size - 1)]
        down = [(j, i) for i, j in up]
        last = lax.slice_in_dim(value, length - width, length, axis=dim)
        first = lax.slice_in_dim(value, 0, width, axis=dim)
        before = lax.ppermute(last, axis, up)
        after = lax.ppermute(first, axis, down)
        value = jnp.concatenate([before, value, after], axis=dim)
    return value


def softmax_rows(scores):
    highest = jnp.max(scores, axis=-1, keepdims=True)
    raised = jnp.exp(scores - highest)
    return (raised / jnp.sum(raised, axis=-1, keepdims=True)).astype(jnp.bfloat16)


def window_attend(queries, key_rows, values):
    scores = jnp.einsum(
        "blhd,bmhd->bhlm", queries, key_rows, preferred_element_type=jnp.float32
    ) / math.sqrt(HEAD_DIM)
    weights = softmax_rows(scores)
    return jnp.einsum(
        "bhlm,bmhd->blhd", weights, values, preferred_element_type=jnp.float32
    ).astype(jnp.bfloat16)


def index_attend(queries, key_rows, values):
    scores = jnp.einsum(
        "lbhd,mbhd->bhlm", queries, key_rows, preferred_element_type=jnp.float32
    ) / math.sqrt(HEAD_DIM)
    weights = softmax_rows(scores)
    return jnp.einsum(
        "bhlm,mbhd->lbhd", weights, values, preferred_element_type=jnp.float32
    ).astype(jnp.bfloat16)


def convolve(image, kernel, bias):
    height, breadth, depth = image.shape
    padded = extended(image, (("row", 0), ("col", 1)), 1)
    total = jnp.zeros((height * breadth, kernel.shape[-1]), jnp.float32)
    for row_shift in range(3):
        for col_shift in range(3):
            cells = padded[row_shift : row_shift + height, col_shift : col_shift + breadth].reshape(
                -1, depth
            )
            total = total + jnp.dot(
                cells, kernel[row_shift, col_shift], preferred_element_type=jnp.float32
            )
    return (total + bias).reshape(height, breadth, -1)


def shards(
    query_window,
    key_window,
    value_window,
    query_index,
    key_index,
    proj_weight,
    proj_bias,
    first_kernel,
    first_bias,
    second_kernel,
    second_bias,
):
    rows_dev, cols_dev, tokens_win, features = query_window.shape
    layout = (rows_dev * cols_dev, tokens_win, HEADS, HEAD_DIM)
    window_out = window_attend(
        query_window.reshape(layout), key_window.reshape(layout), value_window.reshape(layout)
    ).reshape(query_window.shape)
    count_row = lax.axis_size("row")
    count_col = lax.axis_size("col")
    owned_tokens = tokens_win // (count_row * count_col)
    moved = (
        lax.all_to_all(query_index, ("row", "col"), split_axis=2, concat_axis=0, tiled=True),
        lax.all_to_all(key_index, ("row", "col"), split_axis=2, concat_axis=0, tiled=True),
        lax.all_to_all(window_out, ("row", "col"), split_axis=2, concat_axis=0, tiled=True),
    )
    owner_shape = moved[0].shape
    across = (-1, owned_tokens, HEADS, HEAD_DIM)
    index_out = index_attend(
        moved[0].reshape(across), moved[1].reshape(across), moved[2].reshape(across)
    )
    index_rows = index_out.reshape(-1, features)
    owner_rows = (
        jnp.dot(index_rows, proj_weight, preferred_element_type=jnp.float32) + proj_bias
    ).astype(jnp.bfloat16)
    last = owner_rows.shape[-1]
    shaped = owner_rows.reshape(tuple(owner_shape[:-1]) + (last,))
    returned = lax.all_to_all(shaped, ("row", "col"), split_axis=0, concat_axis=2, tiled=True)
    projected = returned.reshape(rows_dev * cols_dev * tokens_win, last)
    grouped = projected.reshape(rows_dev, cols_dev, TILE_ROWS, TILE_COLS, 2, 2, CHANNELS)
    shuffled = jnp.transpose(grouped, (0, 2, 4, 1, 3, 5, 6)).reshape(
        rows_dev * TILE_ROWS * 2, cols_dev * TILE_COLS * 2, CHANNELS
    )
    activated = jax.nn.gelu(convolve(shuffled, first_kernel, first_bias)).astype(jnp.bfloat16)
    return convolve(activated, second_kernel, second_bias).astype(jnp.bfloat16)


def solution(mesh):
    in_specs = (
        P(("grp", "row"), "col", None, None),
        P(("grp", "row"), "col", None, None),
        P(("grp", "row"), "col", None, None),
        P(("grp", "row"), "col", None, None),
        P(("grp", "row"), "col", None, None),
        P(),
        P(),
        P(),
        P(),
        P(),
        P(),
    )
    out_specs = P(("grp", "row"), "col", None)
    return jax.shard_map(shards, mesh=mesh, in_specs=in_specs, out_specs=out_specs, check_vma=False)
```

profile of v0, /device:TPU:0, one launch (start us, length us, event | category | flops | bytes accessed | tf_op | source)
XLA Modules:
  0.0 239.0 jit_solution(4875045535725694193)
XLA Ops:
  0.0 2.6 %copy.35 = bf16[1,4,128,1280]{2,3,1,0:T(8,128)(2,1)} copy(bf16[1,4,128,1280]{3,2,1,0:T(8,128)(2,1)} %param.13) | data formatting | bytes 2621440 | tf_op args[2]
  2.6 2.4 %copy.33 = bf16[1,4,128,1280]{2,3,1,0:T(8,128)(2,1)} copy(bf16[1,4,128,1280]{3,2,1,0:T(8,128)(2,1)} %param.11) | data formatting | bytes 2621440 | tf_op args[0]
  5.0 2.4 %copy.34 = bf16[1,4,128,1280]{2,3,1,0:T(8,128)(2,1)} copy(bf16[1,4,128,1280]{3,2,1,0:T(8,128)(2,1)} %param.12) | data formatting | bytes 2621440 | tf_op args[1]
  7.4 2.5 %fusion.114 = f32[4,8,128,128]{2,3,1,0:T(8,128)S(1)} fusion(bf16[4,128,8,160]{1,3,2,0:T(8,128)(2,1)} %bitcast.137, bf16[4,128,8,160]{1,3,2,0:T(8,128)(2,1)} %bitcast.138), kind=kOutput, calls=%fused_computation.150 | convolution fusion | flops 167772160 | bytes 4718592 | tf_op jit(solution)/shard_map/blhd,bmhd->bhlm/dot_general | solution.py:35
  9.9 1.3 copy-done.4
  11.2 0.5 fusion.112
  11.8 3.9 %convolution_convert_fusion = bf16[4,8,128,160]{2,3,1,0:T(8,128)(2,1)} fusion(bf16[4,128,8,160]{1,3,2,0:T(8,128)(2,1)} %bitcast.160, f32[4,8,128]{2,1,0:T(8,128)S(1)} %fusion.112, f32[4,8,128,128]{2,3,1,0:T(8,128)} %copy-done.4), kind=kOutput, calls=%fused_computation.58 | convolution fusion | flops 170528896 | bytes 4734976 | tf_op jit(solution)/shard_map/bhlm,bmhd->blhd/dot_general | solution.py:39
  15.7 3.7 %copy.37 = bf16[1,4,128,1280]{3,1,0,2:T(4,128)(2,1)} copy(bf16[1,4,128,1280]{2,3,1,0:T(8,128)(2,1)} %bitcast.161) | data formatting | bytes 2621440 | tf_op jit(solution)/shard_map/reshape | solution.py:86
  19.4 7.4 %all-to-all-start = ((bf16[1,4,128,1280]{3,1,0,2:T(4,128)(2,1)}), bf16[1,4,128,1280]{3,1,0,2:T(4,128)(2,1)}, u32[]{:S(2)}, u32[]{:S(2)}) async-start(bf16[1,4,128,1280]{3,1,0,2:T(4,128)(2,1)} %copy.37), calls=%async_computation | async-start | bytes 2621440 | tf_op jit(solution)/shard_map/all_to_all | solution.py:93
  26.9 3.4 %copy.42 = bf16[1,4,128,1280]{3,1,0,2:T(4,128)(2,1)} copy(bf16[1,4,128,1280]{3,2,1,0:T(8,128)(2,1)} %param.15) | data formatting | bytes 2621440 | tf_op args[4]
  30.3 24.1 %all-to-all-done = bf16[1,4,128,1280]{3,1,0,2:T(4,128)(2,1)} async-done(((bf16[1,4,128,1280]{3,1,0,2:T(4,128)(2,1)}), bf16[1,4,128,1280]{3,1,0,2:T(4,128)(2,1)}, u32[]{:S(2)}, u32[]{:S(2)}) %all-to-all-start) | async-done | bytes 1310752 | tf_op jit(solution)/shard_map/all_to_all | solution.py:93
  54.3 8.1 %all-to-all-start.2 = ((bf16[1,4,128,1280]{3,1,0,2:T(4,128)(2,1)}), bf16[1,4,128,1280]{3,1,0,2:T(4,128)(2,1)}, u32[]{:S(2)}, u32[]{:S(2)}) async-start(bf16[1,4,128,1280]{3,1,0,2:T(4,128)(2,1)} %copy.42), calls=%async_computation.2 | async-start | bytes 2621440 | tf_op jit(solution)/shard_map/all_to_all | solution.py:92
  62.4 3.4 %copy.40 = bf16[1,4,128,1280]{3,1,0,2:T(4,128)(2,1)} copy(bf16[1,4,128,1280]{3,2,1,0:T(8,128)(2,1)} %param.14) | data formatting | bytes 2621440 | tf_op args[3]
  65.8 24.1 %all-to-all-done.2 = bf16[1,4,128,1280]{3,1,0,2:T(4,128)(2,1)} async-done(((bf16[1,4,128,1280]{3,1,0,2:T(4,128)(2,1)}), bf16[1,4,128,1280]{3,1,0,2:T(4,128)(2,1)}, u32[]{:S(2)}, u32[]{:S(2)}) %all-to-all-start.2) | async-done | bytes 1310752 | tf_op jit(solution)/shard_map/all_to_all | solution.py:92
  89.9 8.1 %all-to-all-start.1 = ((bf16[1,4,128,1280]{3,1,0,2:T(4,128)(2,1)}), bf16[1,4,128,1280]{3,1,0,2:T(4,128)(2,1)}, u32[]{:S(2)}, u32[]{:S(2)}) async-start(bf16[1,4,128,1280]{3,1,0,2:T(4,128)(2,1)} %copy.40), calls=%async_computation.1 | async-start | bytes 2621440 | tf_op jit(solution)/shard_map/all_to_all | solution.py:91
  97.9 1.4 copy.67
  99.4 1.2 copy.39
  100.6 4.8 %reshape.99 = bf16[64,8,8,160]{3,2,1,0:T(8,128)(2,1)} reshape(bf16[16,1,4,8,1280]{4,3,2,0,1:T(8,128)(2,1)} %copy.39) | data formatting | bytes 2621440 | tf_op jit(solution)/shard_map/reshape | solution.py:98
  105.4 2.5 %copy.65 = bf16[1,4,16,8,1280]{4,3,1,2,0:T(8,128)(2,1)} copy(bf16[1,4,16,8,1280]{4,1,3,2,0:T(4,128)(2,1)} %bitcast.9) | data formatting | bytes 2621440 | tf_op jit(solution)/shard_map/all_to_all | solution.py:92
  108.0 4.8 %reshape.101 = bf16[64,8,8,160]{3,2,1,0:T(8,128)(2,1)} reshape(bf16[16,1,4,8,1280]{4,3,2,0,1:T(8,128)(2,1)} %bitcast.140) | data formatting | bytes 2621440 | tf_op jit(solution)/shard_map/reshape | solution.py:98
  112.8 12.6 %all-to-all-done.1 = bf16[1,4,128,1280]{3,1,0,2:T(4,128)(2,1)} async-done(((bf16[1,4,128,1280]{3,1,0,2:T(4,128)(2,1)}), bf16[1,4,128,1280]{3,1,0,2:T(4,128)(2,1)}, u32[]{:S(2)}, u32[]{:S(2)}) %all-to-all-start.1) | async-done | bytes 1310752 | tf_op jit(solution)/shard_map/all_to_all | solution.py:91
  125.4 2.5 %copy.66 = bf16[1,4,16,8,1280]{4,3,1,2,0:T(8,128)(2,1)} copy(bf16[1,4,16,8,1280]{4,1,3,2,0:T(4,128)(2,1)} %bitcast.7) | data formatting | bytes 2621440 | tf_op jit(solution)/shard_map/all_to_all | solution.py:91
  127.9 4.8 %reshape.100 = bf16[64,8,8,160]{3,2,1,0:T(8,128)(2,1)} reshape(bf16[16,1,4,8,1280]{4,3,2,0,1:T(8,128)(2,1)} %bitcast.141) | data formatting | bytes 2621440 | tf_op jit(solution)/shard_map/reshape | solution.py:98
  132.8 4.6 %fusion.26 = f32[8,8,64,64]{2,3,1,0:T(8,128)S(1)} fusion(bf16[64,8,8,160]{3,2,1,0:T(8,128)(2,1)} %reshape.101, bf16[64,8,8,160]{3,2,1,0:T(8,128)(2,1)} %reshape.100), kind=kOutput, calls=%fused_computation.41 | convolution fusion | flops 83886080 | bytes 3670016 | tf_op jit(solution)/shard_map/lbhd,mbhd->bhlm/dot_general | solution.py:45
  137.4 1.3 copy-done.3
  138.7 0.6 fusion.113
  139.4 5.6 %convert_bitcast_fusion = bf16[64,8,8,160]{3,0,2,1:T(8,128)(2,1)} fusion(bf16[64,8,8,160]{3,2,1,0:T(8,128)(2,1)} %reshape.99, f32[8,8,64]{2,1,0:T(8,128)S(1)} %fusion.113, f32[8,8,64,64]{2,3,1,0:T(8,128)} %copy-done.3), kind=kOutput, calls=%fused_computation.45 | convolution fusion | flops 85594176 | bytes 3686400 | tf_op jit(solution)/shard_map/bhlm,mbhd->lbhd/dot_general | solution.py:49
  145.0 4.1 %copy.48 = bf16[64,8,8,160]{3,2,1,0:T(8,128)(2,1)} copy(bf16[64,8,8,160]{3,0,2,1:T(8,128)(2,1)} %convert_bitcast_fusion) | data formatting | bytes 2621440 | tf_op jit(solution)/shard_map/convert_element_type | solution.py:51
  149.1 4.6 %reshape.102 = bf16[512,1280]{1,0:T(8,128)(2,1)} reshape(bf16[64,8,8,160]{3,2,1,0:T(8,128)(2,1)} %copy.48) | data formatting | bytes 2621440 | tf_op jit(solution)/shard_map/reshape | solution.py:100
  153.7 2.8 %add_convert_fusion = bf16[512,1024]{1,0:T(8,128)(2,1)S(1)} fusion(bf16[512,1280]{1,0:T(8,128)(2,1)} %reshape.102, bf16[1280,1024]{1,0:T(8,128)(2,1)S(1)} %copy-done, f32[1024]{0:T(1024)S(1)} %copy-done.9), kind=kOutput, calls=%fused_computation.44 | convolution fusion | flops 1343225856 | bytes 4984832 | tf_op jit(solution)/shard_map/dot_general | solution.py:102
  156.6 32.7 %all_to_all.60 = bf16[16,4,8,1024]{3,2,1,0:T(8,128)(2,1)S(1)} all-to-all(bf16[16,4,8,1024]{3,2,1,0:T(8,128)(2,1)S(1)} %bitcast.162), channel_id=1, replica_groups=mesh['grp'=2,'row'=8,'col'=2] {'row','col'}, dimensions={0} | all-to-all | bytes 2097152 | tf_op jit(solution)/shard_map/all_to_all | solution.py:106
  189.3 1.6 reshape_reshape.6
  190.9 2.4 copy.50
  193.3 0.4 reshape.104
  193.7 3.2 %collective-permute-start = (bf16[1,128,256]{2,1,0:T(8,128)(2,1)S(1)}, bf16[1,128,256]{2,1,0:T(8,128)(2,1)S(1)}, u32[]{:S(2)}, u32[]{:S(2)}) collective-permute-start(bf16[1,128,256]{2,1,0:T(8,128)(2,1)S(1)} %get-tuple-element.34), channel_id=1, source_target_pairs={{0,2},{2,4},{4,6},{6,8},{8,10},{10,12},{12,14},{1,3},{3,5},{5,7},{... | collective-permute-start | bytes 196616 | tf_op jit(solution)/shard_map/ppermute | solution.py:22
  196.9 1.2 reshape_reshape.7
  198.2 1.3 collective-permute-start.1
  199.5 5.4 %collective-permute-done.1 = bf16[1,128,256]{2,1,0:T(8,128)(2,1)S(1)} collective-permute-done((bf16[1,128,256]{2,1,0:T(8,128)(2,1)S(1)}, bf16[1,128,256]{2,1,0:T(8,128)(2,1)S(1)}, u32[]{:S(2)}, u32[]{:S(2)}) %collective-permute-start.1) | collective-permute-done | bytes 65568 | tf_op jit(solution)/shard_map/ppermute | solution.py:23
  205.2 1.7 collective-permute-start.2
  206.9 1.3 collective-permute-start.3
  209.1 0.9 collective-permute-done.3
  210.0 3.7 %pad_maximum_fusion.5 = (bf16[16,128,256]{2,1,0:T(8,128)(2,1)S(1)}, bf16[16,128,256]{2,1,0:T(8,128)(2,1)S(1)}, bf16[16,128,256]{2,1,0:T(8,128)(2,1)S(1)}, bf16[1...) fusion(bf16[18,128,256]{2,1,0:T(8,128)(2,1)S(1)} %constant_dynamic-update-slice_, ...), kind=kLoop, calls=%fused_computation.76 | loop fusion | flops 12582912 | bytes 7489536 | tf_op jit(solution)/shard_map/concatenate | solution.py:24
  214.1 0.4 convolution_add_fusion.12
  215.0 0.4 convolution_add_fusion.10
  215.4 0.8 copy-done.2
  216.2 0.4 convolution_add_fusion.9
  217.3 0.7 fusion.6
  218.0 0.7 fusion.15
  218.7 1.3 collective-permute-start.5
  220.0 5.0 %collective-permute-start.4 = (bf16[1,128,256]{2,1,0:T(8,128)(2,1)S(1)}, bf16[1,128,256]{2,1,0:T(8,128)(2,1)S(1)}, u32[]{:S(2)}, u32[]{:S(2)}) collective-permute-start(bf16[1,128,256]{2,1,0:T(8,128)(2,1)S(1)} %get-tuple-element.28), channel_id=1, source_target_pairs={{0,2},{2,4},{4,6},{6,8},{8,10},{10,12},{12,14},{1,3},{3,5},{5,7},{... | collective-permute-start | bytes 196616 | tf_op jit(solution)/shard_map/ppermute | solution.py:22
  225.0 0.4 collective-permute-done.5
  225.5 1.6 collective-permute-done.4
  227.1 1.6 collective-permute-start.6
  228.7 1.6 collective-permute-start.7
  230.8 0.9 collective-permute-done.7
  231.7 0.8 maximum_maximum_fusion
  232.6 1.0 fusion.107
  233.6 0.4 fusion.46
  234.0 0.4 convolution_add_fusion.6
  234.9 0.5 convolution_add_fusion.4
  235.3 0.9 convolution_add_fusion.3
  236.2 0.5 convolution_add_fusion.2
  236.7 0.4 convolution_add_fusion.1
  237.3 1.5 fusion.7
  (36 shorter events, 4.3 us)
Async XLA Ops:
  0.0 153.7 %copy-start = (bf16[1280,1024]{1,0:T(8,128)(2,1)S(1)}, bf16[1280,1024]{1,0:T(8,128)(2,1)}, u32[]{:S(2)}) copy-start(bf16[1280,1024]{1,0:T(8,128)(2,1)} %param.16) | copy-start | bytes 7864324
  9.9 1.3 copy-start.4
  19.4 34.9 %all-to-all-start = ((bf16[1,4,128,1280]{3,1,0,2:T(4,128)(2,1)}), bf16[1,4,128,1280]{3,1,0,2:T(4,128)(2,1)}, u32[]{:S(2)}, u32[]{:S(2)}) async-start(bf16[1,4,128,1280]{3,1,0,2:T(4,128)(2,1)} %copy.37), calls=%async_computation | async-start | bytes 2621440 | tf_op jit(solution)/shard_map/all_to_all | solution.py:93
  54.3 35.5 %all-to-all-start.2 = ((bf16[1,4,128,1280]{3,1,0,2:T(4,128)(2,1)}), bf16[1,4,128,1280]{3,1,0,2:T(4,128)(2,1)}, u32[]{:S(2)}, u32[]{:S(2)}) async-start(bf16[1,4,128,1280]{3,1,0,2:T(4,128)(2,1)} %copy.42), calls=%async_computation.2 | async-start | bytes 2621440 | tf_op jit(solution)/shard_map/all_to_all | solution.py:92
  89.9 35.5 %all-to-all-start.1 = ((bf16[1,4,128,1280]{3,1,0,2:T(4,128)(2,1)}), bf16[1,4,128,1280]{3,1,0,2:T(4,128)(2,1)}, u32[]{:S(2)}, u32[]{:S(2)}) async-start(bf16[1,4,128,1280]{3,1,0,2:T(4,128)(2,1)} %copy.40), calls=%async_computation.1 | async-start | bytes 2621440 | tf_op jit(solution)/shard_map/all_to_all | solution.py:91
  137.4 1.3 copy-start.3
  149.1 4.6 %copy-start.9 = (f32[1024]{0:T(1024)S(1)}, f32[1024]{0:T(1024)}, u32[]{:S(2)}) copy-start(f32[1024]{0:T(1024)} %param.17) | copy-start | bytes 12292
  193.7 5.7 %collective-permute-start = (bf16[1,128,256]{2,1,0:T(8,128)(2,1)S(1)}, bf16[1,128,256]{2,1,0:T(8,128)(2,1)S(1)}, u32[]{:S(2)}, u32[]{:S(2)}) collective-permute-start(bf16[1,128,256]{2,1,0:T(8,128)(2,1)S(1)} %get-tuple-element.34), channel_id=1, source_target_pairs={{0,2},{2,4},{4,6},{6,8},{8,10},{10,12},{12,14},{1,3},{3,5},{5,7},{... | collective-permute-start | bytes 196616 | tf_op jit(solution)/shard_map/ppermute | solution.py:22
  198.2 6.7 %collective-permute-start.1 = (bf16[1,128,256]{2,1,0:T(8,128)(2,1)S(1)}, bf16[1,128,256]{2,1,0:T(8,128)(2,1)S(1)}, u32[]{:S(2)}, u32[]{:S(2)}) collective-permute-start(bf16[1,128,256]{2,1,0:T(8,128)(2,1)S(1)} %get-tuple-element.33), channel_id=1, source_target_pairs={{2,0},{4,2},{6,4},{8,6},{10,8},{12,10},{14,12},{3,1},{5,3},{7,5},{... | collective-permute-start | bytes 196616 | tf_op jit(solution)/shard_map/ppermute | solution.py:23
  199.5 8.7 %copy-start.5 = (bf16[3,3,256,256]{3,2,1,0:T(8,128)(2,1)S(1)}, bf16[3,3,256,256]{3,2,1,0:T(8,128)(2,1)}, u32[]{:S(2)}) copy-start(bf16[3,3,256,256]{3,2,1,0:T(8,128)(2,1)} %param.18) | copy-start | bytes 3538948
  205.2 3.9 %collective-permute-start.2 = (bf16[18,1,256]{2,1,0:T(2,128)(2,1)S(1)}, bf16[18,1,256]{2,1,0:T(2,128)(2,1)S(1)}, u32[]{:S(2)}, u32[]{:S(2)}) collective-permute-start(bf16[18,1,256]{2,1,0:T(2,128)(2,1)S(1)} %get-tuple-element.24), channel_id=1, source_target_pairs={{0,1},{2,3},{4,5},{6,7},{8,9},{10,11},{12,13},{14,15},{16,17},{18,... | collective-permute-start | bytes 27656 | tf_op jit(solution)/shard_map/ppermute | solution.py:22
  206.9 3.1 %collective-permute-start.3 = (bf16[18,1,256]{2,1,0:T(2,128)(2,1)S(1)}, bf16[18,1,256]{2,1,0:T(2,128)(2,1)S(1)}, u32[]{:S(2)}, u32[]{:S(2)}) collective-permute-start(bf16[18,1,256]{2,1,0:T(2,128)(2,1)S(1)} %get-tuple-element.25), channel_id=1, source_target_pairs={{1,0},{3,2},{5,4},{7,6},{9,8},{11,10},{13,12},{15,14},{17,16},{19,... | collective-permute-start | bytes 27656 | tf_op jit(solution)/shard_map/ppermute | solution.py:23
  215.0 1.2 copy-start.2
  216.6 0.7 copy-start.7
  218.7 6.8 %collective-permute-start.5 = (bf16[1,128,256]{2,1,0:T(8,128)(2,1)S(1)}, bf16[1,128,256]{2,1,0:T(8,128)(2,1)S(1)}, u32[]{:S(2)}, u32[]{:S(2)}) collective-permute-start(bf16[1,128,256]{2,1,0:T(8,128)(2,1)S(1)} %get-tuple-element.29), channel_id=1, source_target_pairs={{2,0},{4,2},{6,4},{8,6},{10,8},{12,10},{14,12},{3,1},{5,3},{7,5},{... | collective-permute-start | bytes 196616 | tf_op jit(solution)/shard_map/ppermute | solution.py:23
  220.0 10.4 %copy-start.6 = (bf16[3,3,256,256]{3,2,1,0:T(8,128)(2,1)S(1)}, bf16[3,3,256,256]{3,2,1,0:T(8,128)(2,1)}, u32[]{:S(2)}) copy-start(bf16[3,3,256,256]{3,2,1,0:T(8,128)(2,1)} %param.20) | copy-start | bytes 3538948
  220.0 7.0 %collective-permute-start.4 = (bf16[1,128,256]{2,1,0:T(8,128)(2,1)S(1)}, bf16[1,128,256]{2,1,0:T(8,128)(2,1)S(1)}, u32[]{:S(2)}, u32[]{:S(2)}) collective-permute-start(bf16[1,128,256]{2,1,0:T(8,128)(2,1)S(1)} %get-tuple-element.28), channel_id=1, source_target_pairs={{0,2},{2,4},{4,6},{6,8},{8,10},{10,12},{12,14},{1,3},{3,5},{5,7},{... | collective-permute-start | bytes 196616 | tf_op jit(solution)/shard_map/ppermute | solution.py:22
  227.1 3.8 %collective-permute-start.6 = (bf16[18,1,256]{2,1,0:T(2,128)(2,1)S(1)}, bf16[18,1,256]{2,1,0:T(2,128)(2,1)S(1)}, u32[]{:S(2)}, u32[]{:S(2)}) collective-permute-start(bf16[18,1,256]{2,1,0:T(2,128)(2,1)S(1)} %get-tuple-element.19), channel_id=1, source_target_pairs={{0,1},{2,3},{4,5},{6,7},{8,9},{10,11},{12,13},{14,15},{16,17},{18,... | collective-permute-start | bytes 27656 | tf_op jit(solution)/shard_map/ppermute | solution.py:22
  228.7 3.1 %collective-permute-start.7 = (bf16[18,1,256]{2,1,0:T(2,128)(2,1)S(1)}, bf16[18,1,256]{2,1,0:T(2,128)(2,1)S(1)}, u32[]{:S(2)}, u32[]{:S(2)}) collective-permute-start(bf16[18,1,256]{2,1,0:T(2,128)(2,1)S(1)} %get-tuple-element.20), channel_id=1, source_target_pairs={{1,0},{3,2},{5,4},{7,6},{9,8},{11,10},{13,12},{15,14},{17,16},{19,... | collective-permute-start | bytes 27656 | tf_op jit(solution)/shard_map/ppermute | solution.py:23
  236.7 0.7 copy-start.8
  237.1 1.9 copy-start.1
where the time goes:
time: 242 us; the launch traced here: 239 us
  waiting for transfers between devices  69.9 us (29%)
  local copies, waits for them, and re-layouts  59.7 us (25%)
  starting transfers between devices  40.5 us (17%)
  blocking collectives  32.7 us (14%)
  matrix products  29 us (12%)
  other arithmetic  6.8 us (3%)
    all_to_all x1, blocking collectives, shards(): lax.all_to_all(shaped, ('row', 'col'), split_axis=0, concat_axis=2, tiled...  32.7 us
    all_to_all x1, waiting for transfers between devices, shards(): lax.all_to_all(key_index, ('row', 'col'), split_axis=2, concat_axis=0, ti...  24.1 us
    all_to_all x1, waiting for transfers between devices, shards(): lax.all_to_all(window_out, ('row', 'col'), split_axis=2, concat_axis=0, t...  24.1 us
    unnamed x26, local copies, waits for them, and re-layouts  18.4 us
    all_to_all x1, waiting for transfers between devices, shards(): lax.all_to_all(query_index, ('row', 'col'), split_axis=2, concat_axis=0,...  12.6 us
    ppermute x4, starting transfers between devices, extended(): before = lax.ppermute(last, axis, up)  11.5 us
    dot_general x18, matrix products, convolve(): jnp.dot(cells, kernel[row_shift, col_shift], preferred_element_type=jnp.f...  9.55 us
    all_to_all x1, starting transfers between devices, shards(): lax.all_to_all(query_index, ('row', 'col'), split_axis=2, concat_axis=0,...  8.07 us
  transfers between devices with their start and end apart: 11, of which 8 were waited for; matrix products, arithmetic and copies ran while one was open for 10% of the time, Pallas kernels for 0%

commit v1 on v0

v1 whole, which is shorter than its diff:
```python
import functools
import math

import jax
import jax.numpy as jnp
from jax import lax
from jax.experimental import pallas as pl
from jax.experimental.pallas import tpu as pltpu
from jax.sharding import PartitionSpec as P

HEADS = 8
HEAD_DIM = 160
CHANNELS = 256
TILE_ROWS = 8
TILE_COLS = 16
LANES = 128
EDGE = 16
SPAN = 2 * LANES
VMEM_BYTES = 40 * 1024 * 1024


def params(steps=0):
    return pltpu.CompilerParams(
        dimension_semantics=("arbitrary",) * steps if steps else None,
        vmem_limit_bytes=VMEM_BYTES,
    )


def head_start(head):
    return head * HEAD_DIM // LANES * LANES


def head_mask(head):
    lane = lax.broadcasted_iota(jnp.int32, (1, SPAN), 1) + head_start(head)
    return (lane >= head * HEAD_DIM) & (lane < (head + 1) * HEAD_DIM)


def joined_heads(mixed):
    tiles = []
    lane = lax.broadcasted_iota(jnp.int32, (1, LANES), 1)
    for tile in range(HEADS * HEAD_DIM // LANES):
        base = tile * LANES
        first, last = base // HEAD_DIM, (base + LANES - 1) // HEAD_DIM
        pieces = []
        for head in (first, last):
            at = base - head_start(head)
            pieces.append(mixed[head][:, at : at + LANES])
        if first == last:
            tiles.append(pieces[0])
        else:
            tiles.append(jnp.where(lane < last * HEAD_DIM - base, pieces[0], pieces[1]))
    return jnp.concatenate(tiles, axis=1)


def softmax_rows(scores):
    raised = jnp.exp(scores - jnp.max(scores, axis=-1, keepdims=True))
    return (raised / jnp.sum(raised, axis=-1, keepdims=True)).astype(jnp.bfloat16)


def window_kernel(query, key_rows, value, out):
    mixed = []
    for head in range(HEADS):
        lanes = pl.ds(head_start(head), SPAN)
        masked = jnp.where(head_mask(head), query[0, :, lanes], 0)
        scores = lax.dot_general(
            masked, key_rows[0, :, lanes], (((1,), (1,)), ((), ())),
            preferred_element_type=jnp.float32,
        ) * (1.0 / math.sqrt(HEAD_DIM))
        mixed.append(
            jnp.dot(softmax_rows(scores), value[0, :, lanes], preferred_element_type=jnp.float32)
        )
    out[0] = joined_heads(mixed).astype(jnp.bfloat16)


def window_attend(query, key_rows, value):
    windows, tokens, features = query.shape
    block = pl.BlockSpec((1, tokens, features), lambda w: (w, 0, 0))
    return pl.pallas_call(
        window_kernel,
        grid=(windows,),
        in_specs=[block] * 3,
        out_specs=block,
        out_shape=jax.ShapeDtypeStruct(query.shape, jnp.bfloat16),
        compiler_params=params(1),
    )(query, key_rows, value)


def weights_kernel(tokens, query, key_rows, out):
    rows = query.shape[0]
    head = pl.program_id(0)
    start = head * HEAD_DIM // LANES * LANES
    lanes = pl.ds(pl.multiple_of(start, LANES), SPAN)
    lane = lax.broadcasted_iota(jnp.int32, (1, SPAN), 1) + start
    inside = (lane >= head * HEAD_DIM) & (lane < (head + 1) * HEAD_DIM)
    masked = jnp.where(inside, query[:, lanes], 0)
    scores = lax.dot_general(
        masked, key_rows[:, lanes], (((1,), (1,)), ((), ())),
        preferred_element_type=jnp.float32,
    ) * (1.0 / math.sqrt(HEAD_DIM))
    token_row = lax.broadcasted_iota(jnp.int32, (rows, 1), 0) % tokens
    token_col = lax.broadcasted_iota(jnp.int32, (1, rows), 1) % tokens
    out[0] = softmax_rows(jnp.where(token_row == token_col, scores, -jnp.inf))


def index_weights(query, key_rows, tokens):
    rows, features = query.shape
    whole = pl.BlockSpec((rows, features), lambda h: (0, 0))
    return pl.pallas_call(
        functools.partial(weights_kernel, tokens),
        grid=(HEADS,),
        in_specs=[whole] * 2,
        out_specs=pl.BlockSpec((1, rows, rows), lambda h: (h, 0, 0)),
        out_shape=jax.ShapeDtypeStruct((HEADS, rows, rows), jnp.bfloat16),
        compiler_params=params(1),
    )(query, key_rows)


def project_kernel(weights, value, proj_weight, proj_bias, out):
    mixed = []
    for head in range(HEADS):
        lanes = pl.ds(head_start(head), SPAN)
        mixed.append(
            jnp.dot(weights[head], value[:, lanes], preferred_element_type=jnp.float32)
        )
    joined = joined_heads(mixed).astype(jnp.bfloat16)
    total = jnp.dot(joined, proj_weight[...], preferred_element_type=jnp.float32)
    out[...] = (total + proj_bias[...]).astype(jnp.bfloat16)


def project(weights, value, proj_weight, proj_bias):
    rows, features = value.shape
    width = proj_weight.shape[1]
    block = rows // 2
    return pl.pallas_call(
        project_kernel,
        grid=(rows // block,),
        in_specs=[
            pl.BlockSpec((HEADS, block, rows), lambda r: (0, r, 0)),
            pl.BlockSpec((rows, features), lambda r: (0, 0)),
            pl.BlockSpec((features, width), lambda r: (0, 0)),
            pl.BlockSpec((1, width), lambda r: (0, 0)),
        ],
        out_specs=pl.BlockSpec((block, width), lambda r: (r, 0)),
        out_shape=jax.ShapeDtypeStruct((rows, width), jnp.bfloat16),
        compiler_params=params(1),
    )(weights, value, proj_weight, proj_bias.reshape(1, width))


def conv_kernel(
    rows, cols, image, above, below, left, right, keep,
    first_kernel, first_bias, second_kernel, second_bias, out,
    taken, even, odd, acted, woven,
):
    pitch = cols + EDGE
    depth = CHANNELS
    place = lax.broadcasted_iota(jnp.int32, (EDGE, 1), 0)
    half = 2 * depth

    def gap_of(row):
        block = jnp.zeros((EDGE, half), jnp.float32)
        if row >= 1:
            token, sub = (row - 1) // 2, (row - 1) % 2
            block = jnp.where(
                place == 0,
                right[token : token + 1, sub * half : (sub + 1) * half].astype(jnp.float32),
                block,
            )
        if row < 2 * (rows + 2):
            token, sub = row // 2, row % 2
            block = jnp.where(
                place == EDGE - 1,
                left[token : token + 1, sub * half : (sub + 1) * half].astype(jnp.float32),
                block,
            )
        return block

    taken[0:EDGE, 0:depth] = jnp.zeros((EDGE, depth), jnp.bfloat16)
    for i in range(rows + 2):
        if i == 0:
            body = above[...]
        elif i == rows + 1:
            body = below[...]
        else:
            body = image[pl.ds((i - 1) * cols, cols), :]
        body = body.astype(jnp.float32)
        for p in range(2):
            lanes = slice(p * half, (p + 1) * half)
            y = 2 * i + p
            line = jnp.concatenate([gap_of(y), body[:, lanes], gap_of(y + 1)], axis=0)
            length = line.shape[0]
            base = y * pitch
            taken[base : base + length, depth : 3 * depth] = line.astype(jnp.bfloat16)
            later = pltpu.roll(line[:, depth:], 1, 0)
            sooner = pltpu.roll(line[:, :depth], length - 1, 0)
            taken[base + EDGE : base + length, 0:depth] = later[EDGE:].astype(jnp.bfloat16)
            taken[base : base + pitch, 3 * depth :] = sooner[:pitch].astype(jnp.bfloat16)
    last = 2 * (rows + 2) * pitch
    taken[last : last + EDGE, 3 * depth :] = jnp.zeros((EDGE, depth), jnp.bfloat16)

    lines = 2 * rows
    total = (lines + 2) * pitch + EDGE
    even[0:EDGE] = jnp.zeros((EDGE, depth), jnp.float32)
    odd[0:EDGE] = jnp.zeros((EDGE, depth), jnp.float32)
    even[EDGE + total :] = jnp.zeros((EDGE, depth), jnp.float32)
    odd[EDGE + total :] = jnp.zeros((EDGE, depth), jnp.float32)

    def taps(source, kernel, at, size, q):
        found = None
        for r in range(3):
            part = jnp.dot(
                source[pl.ds(at + r * pitch, size), q * depth : (q + 3) * depth], kernel[r],
                preferred_element_type=jnp.float32,
            )
            found = part if found is None else found + part
        return found

    pieces = 3
    step = -(-total // pieces // EDGE) * EDGE
    for at in range(0, total, step):
        size = min(step, total - at)
        kept = keep[at : at + size, :] > 0.0
        kept = jnp.concatenate([kept] * (depth // LANES), axis=1)
        for q, held in ((0, even), (1, odd)):
            value = taps(taken, first_kernel, at, size, q) + first_bias[...]
            value = jax.nn.gelu(value)
            held[EDGE + at : EDGE + at + size] = jnp.where(kept, value, 0.0)
    acted[:, depth : 2 * depth] = even[EDGE : EDGE + total].astype(jnp.bfloat16)
    acted[:, 2 * depth : 3 * depth] = odd[EDGE : EDGE + total].astype(jnp.bfloat16)
    acted[:, 0:depth] = odd[EDGE - 1 : EDGE - 1 + total].astype(jnp.bfloat16)
    acted[:, 3 * depth :] = even[EDGE + 1 : EDGE + 1 + total].astype(jnp.bfloat16)

    group = max(lines // 4, 1)
    for at in range(0, lines, group):
        size = group * pitch - EDGE
        for q in range(2):
            value = taps(acted, second_kernel, EDGE + at * pitch, size, q) + second_bias[...]
            for y in range(group):
                for lane in range(depth // LANES):
                    woven[lane, pl.ds((at + y) * 2 * cols + q, cols, stride=2), :] = value[
                        y * pitch : y * pitch + cols, lane * LANES : (lane + 1) * LANES
                    ]
    for lane in range(depth // LANES):
        out[:, lane * LANES : (lane + 1) * LANES] = woven[lane].astype(jnp.bfloat16)


def convolve_twice(image, above, below, left, right, keep, first_kernel, first_bias, second_kernel, second_bias):
    rows, cols, width = image.shape
    pitch = cols + EDGE
    total = (2 * rows + 2) * pitch + EDGE
    depth = CHANNELS
    found = pl.pallas_call(
        functools.partial(conv_kernel, rows, cols),
        out_shape=jax.ShapeDtypeStruct((4 * rows * cols, depth), jnp.bfloat16),
        in_specs=[pl.BlockSpec(memory_space=pltpu.VMEM)] * 10,
        out_specs=pl.BlockSpec(memory_space=pltpu.VMEM),
        scratch_shapes=[
            pltpu.VMEM(((2 * rows + 4) * pitch + EDGE, 4 * depth), jnp.bfloat16),
            pltpu.VMEM((total + 2 * EDGE, depth), jnp.float32),
            pltpu.VMEM((total + 2 * EDGE, depth), jnp.float32),
            pltpu.VMEM((total, 4 * depth), jnp.bfloat16),
            pltpu.VMEM((depth // LANES, 4 * rows * cols, LANES), jnp.float32),
        ],
        compiler_params=params(),
    )(
        image.reshape(rows * cols, width), above, below, left, right, keep,
        first_kernel.reshape(3, 3 * depth, depth), first_bias.reshape(1, depth),
        second_kernel.reshape(3, 3 * depth, depth), second_bias.reshape(1, depth),
    )
    return found.reshape(2 * rows, 2 * cols, depth)


def kept_rows(rows, cols):
    pitch = cols + EDGE
    lines = 2 * rows
    total = (lines + 2) * pitch + EDGE
    row, col = lax.axis_index("row"), lax.axis_index("col")
    top, bottom = row == 0, row == lax.axis_size("row") - 1
    start, end = col == 0, col == lax.axis_size("col") - 1
    flat = jnp.arange(total)
    line, place = flat // pitch - 1, flat % pitch - EDGE
    wrapped = place == -EDGE
    line = jnp.where(wrapped, line - 1, line)
    place = jnp.where(wrapped, cols, place)
    outside = (
        ((line < 0) & top) | ((line >= lines) & bottom)
        | ((place < 0) & start) | ((place >= cols) & end)
    )
    return jnp.broadcast_to(jnp.where(outside, 0.0, 1.0)[:, None], (total, LANES)).astype(jnp.float32)


def shifted(value, axis, by):
    size = lax.axis_size(axis)
    pairs = [(i, i + by) for i in range(size) if 0 <= i + by < size]
    return lax.ppermute(value, axis, pairs)


def shards(
    query_window, key_window, value_window, query_index, key_index,
    proj_weight, proj_bias, first_kernel, first_bias, second_kernel, second_bias,
):
    rows_dev, cols_dev, tokens_win, features = query_window.shape
    windows = rows_dev * cols_dev
    axes = ("row", "col")
    owners = lax.axis_size("row") * lax.axis_size("col")
    owned = tokens_win // owners

    def dealt(value):
        return jnp.swapaxes(value.reshape(windows, owners, owned, features), 0, 1)

    def exchanged(value):
        return lax.all_to_all(value, axes, split_axis=0, concat_axis=0, tiled=True)

    pair = exchanged(jnp.concatenate([dealt(query_index), dealt(key_index)], axis=1))
    flat = (windows, tokens_win, features)
    window_out = window_attend(
        query_window.reshape(flat), key_window.reshape(flat), value_window.reshape(flat)
    )
    keep = kept_rows(rows_dev * TILE_ROWS, cols_dev * TILE_COLS)
    values = exchanged(dealt(window_out)).reshape(-1, features)
    queries = pair[:, :windows].reshape(-1, features)
    key_rows = pair[:, windows:].reshape(-1, features)
    weights = index_weights(queries, key_rows, owned)
    projected = project(weights, values, proj_weight, proj_bias)
    width = projected.shape[-1]
    returned = exchanged(projected.reshape(owners, windows, owned, width))
    tokens = jnp.swapaxes(returned, 0, 1).reshape(rows_dev, cols_dev, TILE_ROWS, TILE_COLS, width)
    image = jnp.transpose(tokens, (0, 2, 1, 3, 4)).reshape(
        rows_dev * TILE_ROWS, cols_dev * TILE_COLS, width
    )
    above = shifted(image[-1:], "row", 1)
    below = shifted(image[:1], "row", -1)
    tall = jnp.concatenate([above[:, -1], image[:, -1], below[:, -1]], axis=0)
    left = shifted(tall, "col", 1)
    tall = jnp.concatenate([above[:, 0], image[:, 0], below[:, 0]], axis=0)
    right = shifted(tall, "col", -1)
    return convolve_twice(
        image, above[0], below[0], left, right, keep,
        first_kernel, first_bias, second_kernel, second_bias,
    )


def solution(mesh):
    spread = P(("grp", "row"), "col", None, None)
    in_specs = (spread,) * 5 + (P(),) * 6
    out_specs = P(("grp", "row"), "col", None)
    return jax.shard_map(shards, mesh=mesh, in_specs=in_specs, out_specs=out_specs, check_vma=False)
```

time: 242 us -> 171 us (0.71)
  local copies, waits for them, and re-layouts: 59.7 us -> 17.1 us
  blocking collectives: 32.7 us -> 0 us
  matrix products: 29 us -> 0 us
  waiting for transfers between devices: 69.9 us -> 91.9 us
  Pallas kernels: 0 us -> 20.8 us
  other arithmetic: 6.8 us -> 1.85 us
    all_to_all x1 -> x0, blocking collectives: 32.7 us -> none  [shards(): lax.all_to_all(shaped, ('row', 'col'), split_axis=0, concat_axis=2, tiled...]
    dot_general x23 -> x0, matrix products: 29 us -> none  [the longest x18 9.55 us: convolve(): jnp.dot(cells, kernel[row_shift, col_shift], preferred_element_type=jnp.f...]
    reshape x6 -> x0, local copies, waits for them, and re-layouts: 23.3 us -> none  [the longest x1 4.85 us: shards(): moved[2].reshape(across)]
    all_to_all x3, waiting for transfers between devices: 60.7 us -> 83.7 us  [exchanged(): return lax.all_to_all(value, axes, split_axis=0, concat_axis=0, tiled=True)]
    pallas_call x0 -> x4, Pallas kernels: none -> 20.8 us  [the longest x1 8.47 us: convolve_twice(): pl.pallas_call(functools.partial(conv_kernel, rows, cols), out_shape=jax....]
    all_to_all x5 -> x1, local copies, waits for them, and re-layouts: 7.83 us -> 0.08 us  [exchanged(): return lax.all_to_all(value, axes, split_axis=0, concat_axis=0, tiled=True)]
    ppermute x8 -> x4, starting transfers between devices: 16.9 us -> 9.33 us  [shifted(): return lax.ppermute(value, axis, pairs)]
    unnamed x26, local copies, waits for them, and re-layouts: 18.4 us -> 11.4 us
  transfers between devices with their start and end apart: 11 -> 7, of which waited for: 8 -> 6; matrix products, arithmetic and copies ran while one was open for 10% -> 2% of each run, Pallas kernels for 0% -> 5%
where the time goes in v1:
time: 171 us; the launch traced here: 170 us
  waiting for transfers between devices  91.9 us (54%)
  starting transfers between devices  38.2 us (22%)
  Pallas kernels  20.8 us (12%)
  local copies, waits for them, and re-layouts  17.1 us (10%)
  other arithmetic  1.85 us (1%)
    all_to_all x3, waiting for transfers between devices, exchanged(): return lax.all_to_all(value, axes, split_axis=0, concat_axis=0, tiled=True)  83.7 us
    all_to_all x3, starting transfers between devices, exchanged(): return lax.all_to_all(value, axes, split_axis=0, concat_axis=0, tiled=True)  28.9 us
    unnamed x26, local copies, waits for them, and re-layouts  11.4 us
    ppermute x4, starting transfers between devices, shifted(): return lax.ppermute(value, axis, pairs)  9.33 us
    pallas_call x1, Pallas kernels, convolve_twice(): pl.pallas_call(functools.partial(conv_kernel, rows, cols), out_shape=jax....  8.47 us
    ppermute x4, waiting for transfers between devices, shifted(): return lax.ppermute(value, axis, pairs)  8.26 us
    pallas_call x1, Pallas kernels, index_weights(): pl.pallas_call(functools.partial(weights_kernel, tokens), grid=(HEADS,),...  4.74 us
    pallas_call x1, Pallas kernels, window_attend(): pl.pallas_call(window_kernel, grid=(windows,), in_specs=[block] * 3, out_...  4.48 us
  transfers between devices with their start and end apart: 7, of which 6 were waited for; matrix products, arithmetic and copies ran while one was open for 2% of the time, Pallas kernels for 5%

profile of v1, /device:TPU:0, one launch (start us, length us, event | category | flops | bytes accessed | tf_op | source)
XLA Modules:
  0.0 170.2 jit_solution(14519236962291506277)
XLA Ops:
  0.0 0.0 copy-start
  0.0 1.3 copy-done
  1.3 1.6 copy_bitcast_fusion.1
  2.9 1.8 %pad_maximum_fusion = bf16[16,8,8,1280]{3,2,1,0:T(8,128)(2,1)} fusion(bf16[16,4,8,1280]{3,2,1,0:T(8,128)(2,1)S(1)} %get-tuple-element.15, bf16[16,4,8,1280]{3,2,1,0:T(8,128)(2,1)S(1)} %get-tuple-element.16), kind=kLoop, calls=%fused_computation | loop fusion | flops 1310720 | bytes 5242880 | tf_op jit(solution)/shard_map/concatenate | solution.py:313
  4.7 0.0 copy-start.5
  4.7 7.6 %all-to-all-start = ((bf16[16,8,8,1280]{3,2,1,0:T(8,128)(2,1)}), bf16[16,8,8,1280]{3,2,1,0:T(8,128)(2,1)}, u32[]{:S(2)}, u32[]{:S(2)}) async-start(bf16[16,8,8,1280]{3,2,1,0:T(8,128)(2,1)} %pad_maximum_fusion), calls=%async_computation | async-start | bytes 5242880 | tf_op jit(solution)/shard_map/all_to_all | solution.py:311
  12.3 0.0 copy-done.5
  12.3 0.0 copy-start.6
  12.3 1.3 copy-done.6
  13.6 0.0 copy-start.7
  13.6 1.3 copy-done.7
  14.9 4.5 %shard_map.110 = bf16[4,128,1280]{2,1,0:T(8,128)(2,1)S(1)} custom-call(bf16[4,128,1280]{2,1,0:T(8,128)(2,1)S(1)} %bitcast.56, bf16[4,128,1280]{2,1,0:T(8,128)(2,1)S(1)} %bitcast.57, bf16[4,128,1280]{2,1,0:T(8,128)(2,1)S(1)} %bitcast.58), custom_call_target="tpu_custom_call" | custom-call | tf_op jit(solution)/shard_map/pallas_call | solution.py:78
  19.4 1.2 copy_bitcast_fusion
  20.7 41.9 %all-to-all-done = bf16[16,8,8,1280]{3,2,1,0:T(8,128)(2,1)} async-done(((bf16[16,8,8,1280]{3,2,1,0:T(8,128)(2,1)}), bf16[16,8,8,1280]{3,2,1,0:T(8,128)(2,1)}, u32[]{:S(2)}, u32[]{:S(2)}) %all-to-all-start) | async-done | bytes 2621472 | tf_op jit(solution)/shard_map/all_to_all | solution.py:311
  62.6 13.3 %all-to-all-start.1 = ((bf16[16,4,8,1280]{3,2,1,0:T(8,128)(2,1)}), bf16[16,4,8,1280]{3,2,1,0:T(8,128)(2,1)S(1)}, u32[]{:S(2)}, u32[]{:S(2)}) async-start(bf16[16,4,8,1280]{3,2,1,0:T(8,128)(2,1)} %copy_bitcast_fusion), calls=%async_computation.1 | async-start | bytes 2621440 | tf_op jit(solution)/shard_map/all_to_all | solution.py:311
  75.9 1.9 %fusion.8 = (bf16[16,4,8,1280]{3,2,1,0:T(8,128)(2,1)S(1)}, bf16[16,4,8,1280]{3,2,1,0:T(8,128)(2,1)S(1)}) fusion(bf16[16,8,8,1280]{3,2,1,0:T(8,128)(2,1)} %all-to-all-done), kind=kLoop, calls=%fused_computation.27 | loop fusion | bytes 5242880 | tf_op jit(solution)/shard_map/slice | solution.py:321
  77.8 0.0 copy-start.10
  77.8 4.7 %shard_map.109.weights = bf16[8,512,512]{2,1,0:T(8,128)(2,1)S(1)} custom-call(bf16[512,1280]{1,0:T(8,128)(2,1)S(1)} %bitcast.52, bf16[512,1280]{1,0:T(8,128)(2,1)S(1)} %bitcast.51), custom_call_target="tpu_custom_call" | custom-call | tf_op jit(solution)/shard_map/pallas_call | solution.py:108
  82.6 0.0 copy-start.1
  82.6 1.9 %copy-done.1 = bf16[8,512,512]{2,1,0:T(8,128)(2,1)} copy-done((bf16[8,512,512]{2,1,0:T(8,128)(2,1)}, bf16[8,512,512]{2,1,0:T(8,128)(2,1)S(1)}, u32[]{:S(2)}) %copy-start.1) | copy-done | bytes 4194328
  84.5 18.8 %all-to-all-done.1 = bf16[16,4,8,1280]{3,2,1,0:T(8,128)(2,1)S(1)} async-done(((bf16[16,4,8,1280]{3,2,1,0:T(8,128)(2,1)}), bf16[16,4,8,1280]{3,2,1,0:T(8,128)(2,1)S(1)}, u32[]{:S(2)}, u32[]{:S(2)}) %all-to-all-start.1) | async-done | bytes 1310752 | tf_op jit(solution)/shard_map/all_to_all | solution.py:311
  103.3 0.0 copy-done.10
  103.3 0.0 copy-start.2
  103.3 2.2 %copy-done.2 = bf16[8,512,512]{2,1,0:T(8,128)(2,1)S(1)} copy-done((bf16[8,512,512]{2,1,0:T(8,128)(2,1)S(1)}, bf16[8,512,512]{2,1,0:T(8,128)(2,1)}, u32[]{:S(2)}) %copy-start.2) | copy-done | bytes 4194328
  105.5 0.0 copy-start.4
  105.5 1.7 %copy-done.4 = bf16[1280,1024]{1,0:T(8,128)(2,1)S(1)} copy-done((bf16[1280,1024]{1,0:T(8,128)(2,1)S(1)}, bf16[1280,1024]{1,0:T(8,128)(2,1)}, u32[]{:S(2)}) %copy-start.4) | copy-done | bytes 2621464
  107.3 3.1 %shard_map.111 = bf16[512,1024]{1,0:T(8,128)(2,1)S(1)} custom-call(bf16[8,512,512]{2,1,0:T(8,128)(2,1)S(1)} %copy-done.2, bf16[512,1280]{1,0:T(8,128)(2,1)S(1)} %bitcast.53, bf16[1280,1024]{1,0:T(8,128)(2,1)S(1)} %copy-done.4, f32[1,1024]{1,0:T(1,128)S(1)} %bitcast.63), custom_call_target="tpu_custom_call" | custom-call | tf_op jit(solution)/shard_map/pallas_call | solution.py:134
  110.4 0.0 copy-start.3
  110.4 1.0 copy-done.3
  111.3 8.0 %all-to-all-start.2 = ((bf16[16,4,8,1024]{3,2,1,0:T(8,128)(2,1)}), bf16[16,4,8,1024]{3,2,1,0:T(8,128)(2,1)S(1)}, u32[]{:S(2)}, u32[]{:S(2)}) async-start(bf16[16,4,8,1024]{3,2,1,0:T(8,128)(2,1)} %bitcast.55), calls=%async_computation.2 | async-start | bytes 2097152 | tf_op jit(solution)/shard_map/all_to_all | solution.py:311
  119.4 22.9 %all-to-all-done.2 = bf16[16,4,8,1024]{3,2,1,0:T(8,128)(2,1)S(1)} async-done(((bf16[16,4,8,1024]{3,2,1,0:T(8,128)(2,1)}), bf16[16,4,8,1024]{3,2,1,0:T(8,128)(2,1)S(1)}, u32[]{:S(2)}, u32[]{:S(2)}) %all-to-all-start.2) | async-done | bytes 1048608 | tf_op jit(solution)/shard_map/all_to_all | solution.py:311
  142.3 0.1 copy.25
  142.4 0.6 copy.27
  143.0 3.7 %collective-permute-start = (bf16[1,64,1024]{2,1,0:T(8,128)(2,1)S(1)}, bf16[1,64,1024]{2,1,0:T(8,128)(2,1)S(1)}, u32[]{:S(2)}, u32[]{:S(2)}) collective-permute-start(bf16[1,64,1024]{2,1,0:T(8,128)(2,1)S(1)} %bitcast.71), channel_id=1, source_target_pairs={{0,2},{2,4},{4,6},{6,8},{8,10},{10,12},{12,14},{1,3},{3,5},{5,7},{... | collective-permute-start | bytes 393224 | tf_op jit(solution)/shard_map/ppermute | solution.py:294
  146.7 1.3 collective-permute-start.1
  148.1 2.4 %collective-permute-done = bf16[1,64,1024]{2,1,0:T(8,128)(2,1)S(1)} collective-permute-done((bf16[1,64,1024]{2,1,0:T(8,128)(2,1)S(1)}, bf16[1,64,1024]{2,1,0:T(8,128)(2,1)S(1)}, u32[]{:S(2)}, u32[]{:S(2)}) %collective-permute-start) | collective-permute-done | bytes 131104 | tf_op jit(solution)/shard_map/ppermute | solution.py:294
  150.4 5.2 %collective-permute-done.1 = bf16[1,64,1024]{2,1,0:T(8,128)(2,1)S(1)} collective-permute-done((bf16[1,64,1024]{2,1,0:T(8,128)(2,1)S(1)}, bf16[1,64,1024]{2,1,0:T(8,128)(2,1)S(1)}, u32[]{:S(2)}, u32[]{:S(2)}) %collective-permute-start.1) | collective-permute-done | bytes 131104 | tf_op jit(solution)/shard_map/ppermute | solution.py:294
  155.7 1.3 collective-permute-start.3
  157.0 3.0 %collective-permute-start.2 = (bf16[10,1024]{1,0:T(8,128)(2,1)S(1)}, bf16[10,1024]{1,0:T(8,128)(2,1)S(1)}, u32[]{:S(2)}, u32[]{:S(2)}) collective-permute-start(bf16[10,1024]{1,0:T(8,128)(2,1)S(1)} %pad_maximum_fusion.1), channel_id=1, source_target_pairs={{0,1},{2,3},{4,5},{6,7},{8,9},{10,11},{12,13},{14,15},{16,17},{18,... | collective-permute-start | bytes 61448 | tf_op jit(solution)/shard_map/ppermute | solution.py:294
  160.1 0.0 copy-start.8
  160.1 0.0 copy-start.9
  160.1 0.0 copy-start.11
  160.1 0.0 copy-start.12
  160.1 0.1 copy.26
  160.2 0.0 collective-permute-done.3.right
  160.2 0.7 collective-permute-done.2.left
  160.9 0.2 broadcast_in_dim.21.keep
  161.2 0.2 copy-done.8
  161.4 0.4 copy-done.9
  161.7 0.0 copy-done.11
  161.7 0.0 copy-done.12
  161.7 8.5 %shard_map.112 = bf16[2048,256]{1,0:T(8,128)(2,1)} custom-call(bf16[512,1024]{1,0:T(8,128)(2,1)S(1)} %bitcast.54, bf16[64,1024]{1,0:T(8,128)(2,1)S(1)} %bitcast.61, bf16[64,1024]{1,0:T(8,128)(2,1)S(1)} %bitcast.62, bf16[10,1024]{1,0:T(8,128)(2,1)S(1)} %collective-permute-done.2.left, bf16[10,1024]{1,0:T(8,128)(2,1)S(1)} %collective-permute-done.3.right, ...), custom_call_target="tpu_custom_call" | custom-call | tf_op jit(solution)/shard_map/pallas_call | solution.py:251
  (7 shorter events, 0.1 us)
Async XLA Ops:
  0.0 1.3 copy-start
  4.7 7.6 %copy-start.5 = (bf16[1,4,128,1280]{3,2,1,0:T(8,128)(2,1)S(1)}, bf16[1,4,128,1280]{3,2,1,0:T(8,128)(2,1)}, u32[]{:S(2)}) copy-start(bf16[1,4,128,1280]{3,2,1,0:T(8,128)(2,1)} %param.11) | copy-start | bytes 3932164
  4.7 57.9 %all-to-all-start = ((bf16[16,8,8,1280]{3,2,1,0:T(8,128)(2,1)}), bf16[16,8,8,1280]{3,2,1,0:T(8,128)(2,1)}, u32[]{:S(2)}, u32[]{:S(2)}) async-start(bf16[16,8,8,1280]{3,2,1,0:T(8,128)(2,1)} %pad_maximum_fusion), calls=%async_computation | async-start | bytes 5242880 | tf_op jit(solution)/shard_map/all_to_all | solution.py:311
  12.3 1.3 copy-start.6
  13.6 1.3 copy-start.7
  62.6 40.7 %all-to-all-start.1 = ((bf16[16,4,8,1280]{3,2,1,0:T(8,128)(2,1)}), bf16[16,4,8,1280]{3,2,1,0:T(8,128)(2,1)S(1)}, u32[]{:S(2)}, u32[]{:S(2)}) async-start(bf16[16,4,8,1280]{3,2,1,0:T(8,128)(2,1)} %copy_bitcast_fusion), calls=%async_computation.1 | async-start | bytes 2621440 | tf_op jit(solution)/shard_map/all_to_all | solution.py:311
  77.8 25.5 %copy-start.10 = (f32[1024]{0:T(1024)S(1)}, f32[1024]{0:T(1024)}, u32[]{:S(2)}) copy-start(f32[1024]{0:T(1024)} %param.17) | copy-start | bytes 12292
  82.6 1.9 %copy-start.1 = (bf16[8,512,512]{2,1,0:T(8,128)(2,1)}, bf16[8,512,512]{2,1,0:T(8,128)(2,1)S(1)}, u32[]{:S(2)}) copy-start(bf16[8,512,512]{2,1,0:T(8,128)(2,1)S(1)} %shard_map.109.weights) | copy-start | bytes 12582916
  103.3 2.2 %copy-start.2 = (bf16[8,512,512]{2,1,0:T(8,128)(2,1)S(1)}, bf16[8,512,512]{2,1,0:T(8,128)(2,1)}, u32[]{:S(2)}) copy-start(bf16[8,512,512]{2,1,0:T(8,128)(2,1)} %copy-done.1) | copy-start | bytes 12582916
  105.5 1.7 %copy-start.4 = (bf16[1280,1024]{1,0:T(8,128)(2,1)S(1)}, bf16[1280,1024]{1,0:T(8,128)(2,1)}, u32[]{:S(2)}) copy-start(bf16[1280,1024]{1,0:T(8,128)(2,1)} %proj_weight.1) | copy-start | bytes 7864324
  110.4 1.0 copy-start.3
  111.3 31.0 %all-to-all-start.2 = ((bf16[16,4,8,1024]{3,2,1,0:T(8,128)(2,1)}), bf16[16,4,8,1024]{3,2,1,0:T(8,128)(2,1)S(1)}, u32[]{:S(2)}, u32[]{:S(2)}) async-start(bf16[16,4,8,1024]{3,2,1,0:T(8,128)(2,1)} %bitcast.55), calls=%async_computation.2 | async-start | bytes 2097152 | tf_op jit(solution)/shard_map/all_to_all | solution.py:311
  143.0 7.4 %collective-permute-start = (bf16[1,64,1024]{2,1,0:T(8,128)(2,1)S(1)}, bf16[1,64,1024]{2,1,0:T(8,128)(2,1)S(1)}, u32[]{:S(2)}, u32[]{:S(2)}) collective-permute-start(bf16[1,64,1024]{2,1,0:T(8,128)(2,1)S(1)} %bitcast.71), channel_id=1, source_target_pairs={{0,2},{2,4},{4,6},{6,8},{8,10},{10,12},{12,14},{1,3},{3,5},{5,7},{... | collective-permute-start | bytes 393224 | tf_op jit(solution)/shard_map/ppermute | solution.py:294
  146.7 8.9 %collective-permute-start.1 = (bf16[1,64,1024]{2,1,0:T(8,128)(2,1)S(1)}, bf16[1,64,1024]{2,1,0:T(8,128)(2,1)S(1)}, u32[]{:S(2)}, u32[]{:S(2)}) collective-permute-start(bf16[1,64,1024]{2,1,0:T(8,128)(2,1)S(1)} %bitcast.70), channel_id=1, source_target_pairs={{2,0},{4,2},{6,4},{8,6},{10,8},{12,10},{14,12},{3,1},{5,3},{7,5},{... | collective-permute-start | bytes 393224 | tf_op jit(solution)/shard_map/ppermute | solution.py:294
  155.7 4.5 %collective-permute-start.3 = (bf16[10,1024]{1,0:T(8,128)(2,1)S(1)}, bf16[10,1024]{1,0:T(8,128)(2,1)S(1)}, u32[]{:S(2)}, u32[]{:S(2)}) collective-permute-start(bf16[10,1024]{1,0:T(8,128)(2,1)S(1)} %pad_maximum_fusion.2), channel_id=1, source_target_pairs={{1,0},{3,2},{5,4},{7,6},{9,8},{11,10},{13,12},{15,14},{17,16},{19,... | collective-permute-start | bytes 61448 | tf_op jit(solution)/shard_map/ppermute | solution.py:294
  157.0 3.9 %collective-permute-start.2 = (bf16[10,1024]{1,0:T(8,128)(2,1)S(1)}, bf16[10,1024]{1,0:T(8,128)(2,1)S(1)}, u32[]{:S(2)}, u32[]{:S(2)}) collective-permute-start(bf16[10,1024]{1,0:T(8,128)(2,1)S(1)} %pad_maximum_fusion.1), channel_id=1, source_target_pairs={{0,1},{2,3},{4,5},{6,7},{8,9},{10,11},{12,13},{14,15},{16,17},{18,... | collective-permute-start | bytes 61448 | tf_op jit(solution)/shard_map/ppermute | solution.py:294
  160.1 1.3 copy-start.8
  160.1 1.6 copy-start.9
  160.1 1.6 copy-start.11
  160.1 1.6 copy-start.12

commit v2 on v1

--- a/solution.py
+++ b/solution.py
@@ -38,7 +38,7 @@
 def joined_heads(mixed):
     tiles = []
     lane = lax.broadcasted_iota(jnp.int32, (1, LANES), 1)
-    for tile in range(HEADS * HEAD_DIM // LANES):
+    for tile in range(len(mixed) * HEAD_DIM // LANES):
         base = tile * LANES
         first, last = base // HEAD_DIM, (base + LANES - 1) // HEAD_DIM
         pieces = []
@@ -69,85 +69,113 @@
         mixed.append(
             jnp.dot(softmax_rows(scores), value[0, :, lanes], preferred_element_type=jnp.float32)
         )
-    out[0] = joined_heads(mixed).astype(jnp.bfloat16)
-
-
-def window_attend(query, key_rows, value):
+    joined = joined_heads(mixed).astype(jnp.bfloat16)
+    parts, features = out.shape[0], out.shape[-1]
+    for part in range(parts):
+        out[part, 0] = joined[:, part * features : (part + 1) * features]
+
+
+def window_attend(query, key_rows, value, parts):
     windows, tokens, features = query.shape
+    result = (parts, windows, tokens, features // parts)
     block = pl.BlockSpec((1, tokens, features), lambda w: (w, 0, 0))
     return pl.pallas_call(
         window_kernel,
         grid=(windows,),
         in_specs=[block] * 3,
-        out_specs=block,
-        out_shape=jax.ShapeDtypeStruct(query.shape, jnp.bfloat16),
+        out_specs=pl.BlockSpec((parts, 1, tokens, features // parts), lambda w: (0, w, 0, 0)),
+        out_shape=jax.ShapeDtypeStruct(result, jnp.bfloat16),
         compiler_params=params(1),
     )(query, key_rows, value)
 
 
-def weights_kernel(tokens, query, key_rows, out):
-    rows = query.shape[0]
+def weights_kernel(tokens, query_near, query_far, key_near, key_far, out):
     head = pl.program_id(0)
     start = head * HEAD_DIM // LANES * LANES
     lanes = pl.ds(pl.multiple_of(start, LANES), SPAN)
     lane = lax.broadcasted_iota(jnp.int32, (1, SPAN), 1) + start
     inside = (lane >= head * HEAD_DIM) & (lane < (head + 1) * HEAD_DIM)
-    masked = jnp.where(inside, query[:, lanes], 0)
+    query = jnp.concatenate([query_near[:, lanes], query_far[:, lanes]], axis=0)
+    key_rows = jnp.concatenate([key_near[:, lanes], key_far[:, lanes]], axis=0)
     scores = lax.dot_general(
-        masked, key_rows[:, lanes], (((1,), (1,)), ((), ())),
+        jnp.where(inside, query, 0), key_rows, (((1,), (1,)), ((), ())),
         preferred_element_type=jnp.float32,
     ) * (1.0 / math.sqrt(HEAD_DIM))
+    rows = query.shape[0]
     token_row = lax.broadcasted_iota(jnp.int32, (rows, 1), 0) % tokens
     token_col = lax.broadcasted_iota(jnp.int32, (1, rows), 1) % tokens
     out[0] = softmax_rows(jnp.where(token_row == token_col, scores, -jnp.inf))
 
 
-def index_weights(query, key_rows, tokens):
-    rows, features = query.shape
+def index_weights(query_near, query_far, key_near, key_far, tokens):
+    rows, features = query_near.shape
+    heads = features // HEAD_DIM
     whole = pl.BlockSpec((rows, features), lambda h: (0, 0))
     return pl.pallas_call(
         functools.partial(weights_kernel, tokens),
-        grid=(HEADS,),
-        in_specs=[whole] * 2,
-        out_specs=pl.BlockSpec((1, rows, rows), lambda h: (h, 0, 0)),
-        out_shape=jax.ShapeDtypeStruct((HEADS, rows, rows), jnp.bfloat16),
+        grid=(heads,),
+        in_specs=[whole] * 4,
+        out_specs=pl.BlockSpec((1, 2 * rows, 2 * rows), lambda h: (h, 0, 0)),
+        out_shape=jax.ShapeDtypeStruct((heads, 2 * rows, 2 * rows), jnp.bfloat16),
         compiler_params=params(1),
-    )(query, key_rows)
-
-
-def project_kernel(weights, value, proj_weight, proj_bias, out):
+    )(query_near, query_far, key_near, key_far)
+
+
+def mix_kernel(weights, *refs):
+    pieces, (near, far) = refs[:-2], refs[-2:]
+    inner, cores, _, features = pieces[0].shape
+    value = jnp.concatenate(
+        [piece[j, core] for core in range(cores) for piece in pieces for j in range(inner)], axis=0
+    )
     mixed = []
-    for head in range(HEADS):
-        lanes = pl.ds(head_start(head), SPAN)
-        mixed.append(
-            jnp.dot(weights[head], value[:, lanes], preferred_element_type=jnp.float32)
-        )
+    for head in range(features // HEAD_DIM):
+        lanes = slice(head_start(head), head_start(head) + SPAN)
+        mixed.append(jnp.dot(weights[head], value[:, lanes], preferred_element_type=jnp.float32))
     joined = joined_heads(mixed).astype(jnp.bfloat16)
+    half = value.shape[0] // 2
+    near[...] = joined[:half]
+    far[...] = joined[half:]
+
+
+def index_mix(weights, pieces):
+    rows, features = weights.shape[1], pieces[0].shape[-1]
+    result = jax.ShapeDtypeStruct((rows // 2, features), jnp.bfloat16)
+    return pl.pallas_call(
+        mix_kernel,
+        in_specs=[pl.BlockSpec(memory_space=pltpu.VMEM)] * (1 + len(pieces)),
+        out_specs=[pl.BlockSpec(memory_space=pltpu.VMEM)] * 2,
+        out_shape=[result, result],
+        compiler_params=params(),
+    )(weights, *pieces)
+
+
+def project_kernel(near, far, proj_weight, proj_bias, out):
+    joined = jnp.concatenate([near[...], far[...]], axis=1)
     total = jnp.dot(joined, proj_weight[...], preferred_element_type=jnp.float32)
     out[...] = (total + proj_bias[...]).astype(jnp.bfloat16)
 
 
-def project(weights, value, proj_weight, proj_bias):
-    rows, features = value.shape
-    width = proj_weight.shape[1]
-    block = rows // 2
+def project(near, far, proj_weight, proj_bias):
     return pl.pallas_call(
         project_kernel,
-        grid=(rows // block,),
-        in_specs=[
-            pl.BlockSpec((HEADS, block, rows), lambda r: (0, r, 0)),
-            pl.BlockSpec((rows, features), lambda r: (0, 0)),
-            pl.BlockSpec((features, width), lambda r: (0, 0)),
-            pl.BlockSpec((1, width), lambda r: (0, 0)),
-        ],
-        out_specs=pl.BlockSpec((block, width), lambda r: (r, 0)),
-        out_shape=jax.ShapeDtypeStruct((rows, width), jnp.bfloat16),
-        compiler_params=params(1),
-    )(weights, value, proj_weight, proj_bias.reshape(1, width))
+        in_specs=[pl.BlockSpec(memory_space=pltpu.VMEM)] * 4,
+        out_specs=pl.BlockSpec(memory_space=pltpu.VMEM),
+        out_shape=jax.ShapeDtypeStruct((near.shape[0], proj_weight.shape[1]), jnp.bfloat16),
+        compiler_params=params(),
+    )(near, far, proj_weight, proj_bias.reshape(1, -1))
+
+
+def line_of(line, rows):
+    quarter = rows // 4
+    if line < quarter:
+        return 0, line
+    if line < 3 * quarter:
+        return 1, line - quarter
+    return 0, line - 2 * quarter
 
 
 def conv_kernel(
-    rows, cols, image, above, below, left, right, keep,
+    rows, cols, outer, middle, above, below, left, right, keep,
     first_kernel, first_bias, second_kernel, second_bias, out,
     taken, even, odd, acted, woven,
 ):
@@ -181,7 +209,8 @@
         elif i == rows + 1:
             body = below[...]
         else:
-            body = image[pl.ds((i - 1) * cols, cols), :]
+            part, at = line_of(i - 1, rows)
+            body = (outer, middle)[part][pl.ds(at * cols, cols), :]
         body = body.astype(jnp.float32)
         for p in range(2):
             lanes = slice(p * half, (p + 1) * half)
@@ -243,15 +272,15 @@
         out[:, lane * LANES : (lane + 1) * LANES] = woven[lane].astype(jnp.bfloat16)
 
 
-def convolve_twice(image, above, below, left, right, keep, first_kernel, first_bias, second_kernel, second_bias):
-    rows, cols, width = image.shape
+def convolve_twice(outer, middle, above, below, left, right, keep, first_kernel, first_bias, second_kernel, second_bias):
+    rows, cols, width = (2 * outer.shape[0],) + outer.shape[1:]
     pitch = cols + EDGE
     total = (2 * rows + 2) * pitch + EDGE
     depth = CHANNELS
     found = pl.pallas_call(
         functools.partial(conv_kernel, rows, cols),
         out_shape=jax.ShapeDtypeStruct((4 * rows * cols, depth), jnp.bfloat16),
-        in_specs=[pl.BlockSpec(memory_space=pltpu.VMEM)] * 10,
+        in_specs=[pl.BlockSpec(memory_space=pltpu.VMEM)] * 11,
         out_specs=pl.BlockSpec(memory_space=pltpu.VMEM),
         scratch_shapes=[
             pltpu.VMEM(((2 * rows + 4) * pitch + EDGE, 4 * depth), jnp.bfloat16),
@@ -262,7 +291,7 @@
         ],
         compiler_params=params(),
     )(
-        image.reshape(rows * cols, width), above, below, left, right, keep,
+        outer.reshape(-1, width), middle.reshape(-1, width), above, below, left, right, keep,
         first_kernel.reshape(3, 3 * depth, depth), first_bias.reshape(1, depth),
         second_kernel.reshape(3, 3 * depth, depth), second_bias.reshape(1, depth),
     )
@@ -294,47 +323,115 @@
     return lax.ppermute(value, axis, pairs)
 
 
+def across(value, axis, by, unit=1):
+    size = lax.axis_size(axis)
+    return lax.ppermute(value, axis, [(i, (i + by * unit) % size) for i in range(size)])
+
+
+def paired(value, axis):
+    return lax.ppermute(value, axis, [(i, i ^ 1) for i in range(lax.axis_size(axis))])
+
+
+def picked(value, index, axis=0):
+    return lax.dynamic_index_in_dim(value, index, axis, keepdims=False)
+
+
 def shards(
     query_window, key_window, value_window, query_index, key_index,
     proj_weight, proj_bias, first_kernel, first_bias, second_kernel, second_bias,
 ):
     rows_dev, cols_dev, tokens_win, features = query_window.shape
     windows = rows_dev * cols_dev
-    axes = ("row", "col")
-    owners = lax.axis_size("row") * lax.axis_size("col")
-    owned = tokens_win // owners
-
-    def dealt(value):
-        return jnp.swapaxes(value.reshape(windows, owners, owned, features), 0, 1)
-
-    def exchanged(value):
-        return lax.all_to_all(value, axes, split_axis=0, concat_axis=0, tiled=True)
-
-    pair = exchanged(jnp.concatenate([dealt(query_index), dealt(key_index)], axis=1))
     flat = (windows, tokens_win, features)
+    inner, cores = 2, lax.axis_size("col")
+    outer = lax.axis_size("row") // inner
+    row, core = lax.axis_index("row"), lax.axis_index("col")
+    z, y = row // inner, row % inner
+    chunk = tokens_win // 2
+    owned = chunk // (outer * inner)
+    slab = inner * owned
+    half = features // cores
+
+    def slab_of(value, part, place):
+        at = place * slab
+        if part == 0:
+            at = jnp.where(at < chunk // 2, at, at + chunk)
+        else:
+            at = at + chunk // 2
+        cut = lax.dynamic_slice_in_dim(value, at, slab, axis=value.ndim - 2)
+        return cut.reshape(cut.shape[:-2] + (inner, owned, cut.shape[-1]))
+
+    query, key_rows = query_index.reshape(flat), key_index.reshape(flat)
+    sent = []
+    for k in range(outer):
+        place = (z + k) % outer
+        block = jnp.stack(
+            [slab_of(value, part, place) for part in range(2) for value in (query, key_rows)]
+        )
+        sent.append(across(block, "row", k, inner) if k else block)
+    near = [picked(block, y, 2) for block in sent]
+    far = [paired(picked(block, 1 - y, 2), "row") for block in sent]
+    pair = jnp.stack([jnp.stack([a, b], axis=1) for a, b in zip(near, far)], axis=1)
+    pair = pair.reshape(2, 2, -1, features)
+    own_half = lax.dynamic_slice_in_dim(pair, core * half, half, axis=3)
+    other_half = lax.dynamic_slice_in_dim(pair, (1 - core) * half, half, axis=3)
+    weights = []
+    for part in range(2):
+        here, there = own_half[part], paired(other_half[part], "col")
+        weights.append(index_weights(here[0], there[0], here[1], there[1], owned))
+
     window_out = window_attend(
-        query_window.reshape(flat), key_window.reshape(flat), value_window.reshape(flat)
-    )
+        query_window.reshape(flat), key_window.reshape(flat), value_window.reshape(flat), cores
+    )
+    window_out = jnp.stack([picked(window_out, core), paired(picked(window_out, 1 - core), "col")])
+    ordered = jnp.concatenate([proj_weight, proj_weight], axis=0)
+    ordered = lax.dynamic_slice_in_dim(ordered, core * half, features, axis=0)
     keep = kept_rows(rows_dev * TILE_ROWS, cols_dev * TILE_COLS)
-    values = exchanged(dealt(window_out)).reshape(-1, features)
-    queries = pair[:, :windows].reshape(-1, features)
-    key_rows = pair[:, windows:].reshape(-1, features)
-    weights = index_weights(queries, key_rows, owned)
-    projected = project(weights, values, proj_weight, proj_bias)
-    width = projected.shape[-1]
-    returned = exchanged(projected.reshape(owners, windows, owned, width))
-    tokens = jnp.swapaxes(returned, 0, 1).reshape(rows_dev, cols_dev, TILE_ROWS, TILE_COLS, width)
-    image = jnp.transpose(tokens, (0, 2, 1, 3, 4)).reshape(
-        rows_dev * TILE_ROWS, cols_dev * TILE_COLS, width
-    )
-    above = shifted(image[-1:], "row", 1)
-    below = shifted(image[:1], "row", -1)
-    tall = jnp.concatenate([above[:, -1], image[:, -1], below[:, -1]], axis=0)
-    left = shifted(tall, "col", 1)
-    tall = jnp.concatenate([above[:, 0], image[:, 0], below[:, 0]], axis=0)
-    right = shifted(tall, "col", -1)
+
+    images = []
+    for part in range(2):
+        blocks = jnp.stack([slab_of(window_out, part, (z + k) % outer) for k in range(outer)])
+        here, there = picked(blocks, y, 3), paired(picked(blocks, 1 - y, 3), "row")
+        pieces = []
+        for k in range(outer):
+            piece = jnp.stack([here[k], there[k]]).reshape(inner, cores, windows * owned, half)
+            pieces.append(across(piece, "row", k, inner) if k else piece)
+        mixed_near, mixed_far = index_mix(weights[part], pieces)
+        projected = project(mixed_near, paired(mixed_far, "col"), ordered, proj_bias)
+        width = projected.shape[-1]
+        projected = projected.reshape(outer, inner, windows, owned, width)
+        here, there = projected[:, 0], paired(projected[:, 1], "row")
+        returned = []
+        for k in range(outer):
+            piece = jnp.stack([here[k], there[k]])
+            returned.append(across(piece, "row", -k, inner) if k else piece)
+        returned = jnp.stack(returned)
+        placed = jnp.stack([picked(returned, (place - z) % outer) for place in range(outer)])
+        placed = jnp.where(y == 0, placed, placed[:, ::-1])
+        tokens = jnp.transpose(placed, (2, 0, 1, 3, 4)).reshape(
+            rows_dev, cols_dev, TILE_ROWS // 2, TILE_COLS, width
+        )
+        images.append(
+            jnp.transpose(tokens, (0, 2, 1, 3, 4)).reshape(-1, cols_dev * TILE_COLS, width)
+        )
+    image_outer, image_middle = images
+    above = shifted(image_outer[-1:], "row", 1)
+    below = shifted(image_outer[:1], "row", -1)
+    quarter = image_outer.shape[0] // 2
+
+    def column(at):
+        return jnp.concatenate(
+            [
+                above[:, at], image_outer[:quarter, at], image_middle[:, at],
+                image_outer[quarter:, at], below[:, at],
+            ],
+            axis=0,
+        )
+
+    left = shifted(column(-1), "col", 1)
+    right = shifted(column(0), "col", -1)
     return convolve_twice(
-        image, above[0], below[0], left, right, keep,
+        image_outer, image_middle, above[0], below[0], left, right, keep,
         first_kernel, first_bias, second_kernel, second_bias,
     )
 

time: 171 us -> 187 us (1.094)
  starting transfers between devices: 38.2 us -> 80 us
  waiting for transfers between devices: 91.9 us -> 59.7 us
  other arithmetic: 1.85 us -> 6.48 us
  Pallas kernels: 20.8 us -> 23.4 us
  local copies, waits for them, and re-layouts: 17.1 us -> 15 us
    all_to_all x3 -> x0, waiting for transfers between devices: 83.7 us -> none  [exchanged(): return lax.all_to_all(value, axes, split_axis=0, concat_axis=0, tiled=True)]
    ppermute x0 -> x28, starting transfers between devices: none -> 69.5 us  [the longest x15 58.4 us: across(): lax.ppermute(value, axis, [(i, (i + by * unit) % size) for i in range(siz...]
    ppermute x0 -> x28, waiting for transfers between devices: none -> 57.2 us  [the longest x15 47.2 us: across(): lax.ppermute(value, axis, [(i, (i + by * unit) % size) for i in range(siz...]
    all_to_all x3 -> x0, starting transfers between devices: 28.9 us -> none  [exchanged(): return lax.all_to_all(value, axes, split_axis=0, concat_axis=0, tiled=True)]
    unnamed x26, local copies, waits for them, and re-layouts: 11.4 us -> 4.81 us
    another operation x0 -> x8, local copies, waits for them, and re-layouts: none -> 5.88 us  [the longest x4 4.14 us: shards(): jnp.stack([a, b], axis=1)]
    ppermute x4, waiting for transfers between devices: 8.26 us -> 2.46 us  [shifted(): return lax.ppermute(value, axis, pairs)]
    another operation x0 -> x33, other arithmetic: none -> 2.7 us  [the longest x4 1.17 us: shards(): jnp.stack([slab_of(value, part, place) for part in range(2) for value in...]
  transfers between devices with their start and end apart: 7 -> 32, of which waited for: 6 -> 12; matrix products, arithmetic and copies ran while one was open for 2% -> 8% of each run, Pallas kernels for 5% -> 6%
where the time goes in v2:
time: 187 us; the launch traced here: 185 us
  starting transfers between devices  80 us (43%)
  waiting for transfers between devices  59.7 us (32%)
  Pallas kernels  23.4 us (13%)
  local copies, waits for them, and re-layouts  15 us (8%)
  other arithmetic  6.48 us (3%)
    ppermute x15, starting transfers between devices, across(): lax.ppermute(value, axis, [(i, (i + by * unit) % size) for i in range(siz...  58.4 us
    ppermute x15, waiting for transfers between devices, across(): lax.ppermute(value, axis, [(i, (i + by * unit) % size) for i in range(siz...  47.2 us
    ppermute x13, starting transfers between devices, paired(): lax.ppermute(value, axis, [(i, i ^ 1) for i in range(lax.axis_size(axis))])  11 us
    ppermute x4, starting transfers between devices, shifted(): return lax.ppermute(value, axis, pairs)  10.5 us
    ppermute x13, waiting for transfers between devices, paired(): lax.ppermute(value, axis, [(i, i ^ 1) for i in range(lax.axis_size(axis))])  10 us
    pallas_call x1, Pallas kernels, convolve_twice(): pl.pallas_call(functools.partial(conv_kernel, rows, cols), out_shape=jax....  8.47 us
    unnamed x26, local copies, waits for them, and re-layouts  4.81 us
    pallas_call x2, Pallas kernels, index_weights(): pl.pallas_call(functools.partial(weights_kernel, tokens), grid=(heads,),...  4.74 us
  transfers between devices with their start and end apart: 32, of which 12 were waited for; matrix products, arithmetic and copies ran while one was open for 8% of the time, Pallas kernels for 6%

profile of v2, /device:TPU:0, one launch (start us, length us, event | category | flops | bytes accessed | tf_op | source)
XLA Modules:
  0.0 185.4 jit_solution(1152656540375186774)
XLA Ops:
  0.0 1.3 copy-done
  1.3 1.3 copy-done.1
  2.6 1.3 copy-done.2
  4.0 4.5 %shard_map.110 = bf16[2,4,128,640]{3,2,1,0:T(8,128)(2,1)S(1)} custom-call(bf16[4,128,1280]{2,1,0:T(8,128)(2,1)S(1)} %bitcast.227, bf16[4,128,1280]{2,1,0:T(8,128)(2,1)S(1)} %bitcast.228, bf16[4,128,1280]{2,1,0:T(8,128)(2,1)S(1)} %bitcast.229), custom_call_target="tpu_custom_call" | custom-call | tf_op jit(solution)/shard_map/pallas_call | solution.py:82
  8.5 1.0 constant_dynamic-slice_fusion.8
  9.5 0.5 collective-permute-start.8
  10.1 1.6 dynamic-slice_bitcast_fusion.31
  11.8 0.8 dynamic-slice_bitcast_fusion.16
  12.6 3.0 %collective-permute-start = (bf16[4,4,8,1280]{3,2,1,0:T(8,128)(2,1)}, bf16[4,4,8,1280]{3,2,1,0:T(8,128)(2,1)S(1)}, u32[]{:S(2)}, u32[]{:S(2)}) collective-permute-start(bf16[4,4,8,1280]{3,2,1,0:T(8,128)(2,1)} %get-tuple-element.58), channel_id=1, source_target_pairs={{0,2},{2,0},{4,6},{6,4},{8,10},{10,8},{12,14},{14,12},{1,3},{3,1},... | collective-permute-start | bytes 983048 | tf_op jit(solution)/shard_map/ppermute | solution.py:332
  15.5 0.9 pad_maximum_fusion.2
  16.5 1.6 collective-permute-start.1
  18.1 2.7 %collective-permute-start.3 = (bf16[4,4,2,8,1280]{4,3,2,1,0:T(8,128)(2,1)S(1)}, bf16[4,4,2,8,1280]{4,3,2,1,0:T(8,128)(2,1)}, u32[]{:S(2)}, u32[]{:S(2)}) collective-permute-start(bf16[4,4,2,8,1280]{4,3,2,1,0:T(8,128)(2,1)S(1)} %pad_maximum_fusion.3), channel_id=1, source_target_pairs={{0,8},{2,10},{4,12},{6,14},{8,0},{10,2},{12,4},{14,6},{1,9},{3,11}... | collective-permute-start | bytes 1966088 | tf_op jit(solution)/shard_map/ppermute | solution.py:328
  20.9 1.4 collective-permute-start.5
  22.3 1.3 collective-permute-done
  24.0 1.8 collective-permute-start.19
  25.8 10.5 %collective-permute-done.1 = bf16[4,4,2,8,1280]{4,3,2,1,0:T(8,128)(2,1)} collective-permute-done((bf16[4,4,2,8,1280]{4,3,2,1,0:T(8,128)(2,1)}, bf16[4,4,2,8,1280]{4,3,2,1,0:T(8,128)(2,1)}, u32[]{:S(2)}, u32[]{:S(2)}) %collective-permute-start.1) | collective-permute-done | bytes 655392 | tf_op jit(solution)/shard_map/ppermute | solution.py:328
  36.4 1.1 dynamic-slice_bitcast_fusion.14
  37.5 0.3 collective-permute-start.2
  37.8 25.4 %collective-permute-done.3 = bf16[4,4,2,8,1280]{4,3,2,1,0:T(8,128)(2,1)} collective-permute-done((bf16[4,4,2,8,1280]{4,3,2,1,0:T(8,128)(2,1)S(1)}, bf16[4,4,2,8,1280]{4,3,2,1,0:T(8,128)(2,1)}, u32[]{:S(2)}, u32[]{:S(2)}) %collective-permute-start.3) | collective-permute-done | bytes 655392 | tf_op jit(solution)/shard_map/ppermute | solution.py:328
  63.2 1.1 dynamic-slice_bitcast_fusion.12
  64.3 0.6 collective-permute-start.4
  64.9 1.1 dynamic-slice_bitcast_fusion.10
  66.0 1.6 collective-permute-start.6
  67.8 0.6 collective-permute-start.9
  68.5 15.6 %collective-permute-start.22 = (bf16[2,2,32,640]{3,2,1,0:T(8,128)(2,1)S(1)}, bf16[2,2,32,640]{3,2,1,0:T(8,128)(2,1)S(1)}, u32[]{:S(2)}, u32[]{:S(2)}) collective-permute-start(bf16[2,2,32,640]{3,2,1,0:T(8,128)(2,1)S(1)} %pad_maximum_fusion.18), channel_id=1, source_target_pairs={{0,12},{2,14},{4,0},{6,2},{8,4},{10,6},{12,8},{14,10},{1,13},{3,15... | collective-permute-start | bytes 491528 | tf_op jit(solution)/shard_map/ppermute | solution.py:328
  84.3 3.4 %collective-permute-start.20 = (bf16[2,2,32,640]{3,2,1,0:T(8,128)(2,1)S(1)}, bf16[2,2,32,640]{3,2,1,0:T(8,128)(2,1)S(1)}, u32[]{:S(2)}, u32[]{:S(2)}) collective-permute-start(bf16[2,2,32,640]{3,2,1,0:T(8,128)(2,1)S(1)} %pad_maximum_fusion.16), channel_id=1, source_target_pairs={{0,4},{2,6},{4,8},{6,10},{8,12},{10,14},{12,0},{14,2},{1,5},{3,7},... | collective-permute-start | bytes 491528 | tf_op jit(solution)/shard_map/ppermute | solution.py:328
  87.8 0.3 pad_maximum_fusion
  88.4 0.5 collective-permute-start.7
  89.2 1.3 collective-permute-done.18
  90.4 12.4 %collective-permute-start.12 = (bf16[2,2,32,640]{3,2,1,0:T(8,128)(2,1)S(1)}, bf16[2,2,32,640]{3,2,1,0:T(8,128)(2,1)S(1)}, u32[]{:S(2)}, u32[]{:S(2)}) collective-permute-start(bf16[2,2,32,640]{3,2,1,0:T(8,128)(2,1)S(1)} %pad_maximum_fusion.14), channel_id=1, source_target_pairs={{0,12},{2,14},{4,0},{6,2},{8,4},{10,6},{12,8},{14,10},{1,13},{3,15... | collective-permute-start | bytes 491528 | tf_op jit(solution)/shard_map/ppermute | solution.py:328
  102.9 2.4 %shard_map.113.weights = bf16[4,512,512]{2,1,0:T(8,128)(2,1)S(1)} custom-call(bf16[256,640]{1,0:T(8,128)(2,1)S(1)} %get-tuple-element.14.query_near, bf16[256,640]{1,0:T(8,128)(2,1)S(1)} %get-tuple-element.50.query_far, bf16[256,640]{1,0:T(8,128)(2,1)S(1)} %get-tuple-element.13.key_near, bf16[256,640]{1,0:T(8,128)(2,1)S(1)} %get-tuple-element.49.key_far), custom_call_target="tpu_custom_call" | custom-call | tf_op jit(solution)/shard_map/pallas_call | solution.py:114
  105.3 0.6 collective-permute-start.10
  105.9 1.4 shard_map.114
  107.4 2.4 %shard_map.109.weights = bf16[4,512,512]{2,1,0:T(8,128)(2,1)S(1)} custom-call(bf16[256,640]{1,0:T(8,128)(2,1)S(1)} %get-tuple-element.16.query_near, bf16[256,640]{1,0:T(8,128)(2,1)S(1)} %get-tuple-element.56.query_far, bf16[256,640]{1,0:T(8,128)(2,1)S(1)} %get-tuple-element.15.key_near, bf16[256,640]{1,0:T(8,128)(2,1)S(1)} %get-tuple-element.55.key_far), custom_call_target="tpu_custom_call" | custom-call | tf_op jit(solution)/shard_map/pallas_call | solution.py:114
  109.8 8.4 %collective-permute-done.11.refs_2_ = bf16[2,2,32,640]{3,2,1,0:T(8,128)(2,1)S(1)} collective-permute-done((bf16[2,2,32,640]{3,2,1,0:T(8,128)(2,1)S(1)}, bf16[2,2,32,640]{3,2,1,0:T(8,128)(2,1)S(1)}, u32[]{:S(2)}, u32[]{:S(2)}) %collective-permute-start.11) | collective-permute-done | bytes 163872 | tf_op jit(solution)/shard_map/ppermute | solution.py:328
  118.2 1.4 shard_map.111
  119.6 0.7 copy-done.5
  120.4 3.5 %fusion.proj_weight = bf16[1280,1024]{1,0:T(8,128)(2,1)S(1)} fusion(s32[]{:T(128)S(6)} %select_n.269, bf16[1280,1024]{1,0:T(8,128)(2,1)S(1)} %copy-done.10), kind=kLoop, calls=%fused_computation.2 | loop fusion | flops 5242880 | bytes 5242884 | tf_op jit(solution)/shard_map/concatenate | solution.py:387
  124.1 0.9 shard_map.115
  125.0 0.6 collective-permute-start.24
  125.5 1.8 shard_map.112
  127.5 1.6 collective-permute-start.14
  129.1 5.1 %collective-permute-done.24 = bf16[4,4,8,1024]{3,2,1,0:T(8,128)(2,1)S(1)} collective-permute-done((bf16[4,4,8,1024]{3,2,1,0:T(8,128)(2,1)S(1)}, bf16[4,4,8,1024]{3,2,1,0:T(8,128)(2,1)S(1)}, u32[]{:S(2)}, u32[]{:S(2)}) %collective-permute-start.24) | collective-permute-done | bytes 262176 | tf_op jit(solution)/shard_map/ppermute | solution.py:332
  134.3 2.7 %collective-permute-start.26 = (bf16[2,4,8,1024]{3,2,1,0:T(8,128)(2,1)S(1)}, bf16[2,4,8,1024]{3,2,1,0:T(8,128)(2,1)S(1)}, u32[]{:S(2)}, u32[]{:S(2)}) collective-permute-start(bf16[2,4,8,1024]{3,2,1,0:T(8,128)(2,1)S(1)} %pad_maximum_fusion.23), channel_id=1, source_target_pairs={{0,8},{2,10},{4,12},{6,14},{8,0},{10,2},{12,4},{14,6},{1,9},{3,11}... | collective-permute-start | bytes 393224 | tf_op jit(solution)/shard_map/ppermute | solution.py:328
  137.0 2.3 %collective-permute-done.14 = bf16[4,4,8,1024]{3,2,1,0:T(8,128)(2,1)S(1)} collective-permute-done((bf16[4,4,8,1024]{3,2,1,0:T(8,128)(2,1)S(1)}, bf16[4,4,8,1024]{3,2,1,0:T(8,128)(2,1)S(1)}, u32[]{:S(2)}, u32[]{:S(2)}) %collective-permute-start.14) | collective-permute-done | bytes 262176 | tf_op jit(solution)/shard_map/ppermute | solution.py:332
  139.5 2.7 %collective-permute-start.16 = (bf16[2,4,8,1024]{3,2,1,0:T(8,128)(2,1)S(1)}, bf16[2,4,8,1024]{3,2,1,0:T(8,128)(2,1)S(1)}, u32[]{:S(2)}, u32[]{:S(2)}) collective-permute-start(bf16[2,4,8,1024]{3,2,1,0:T(8,128)(2,1)S(1)} %pad_maximum_fusion.20), channel_id=1, source_target_pairs={{0,8},{2,10},{4,12},{6,14},{8,0},{10,2},{12,4},{14,6},{1,9},{3,11}... | collective-permute-start | bytes 393224 | tf_op jit(solution)/shard_map/ppermute | solution.py:328
  142.2 2.1 %collective-permute-start.17 = (bf16[2,4,8,1024]{3,2,1,0:T(8,128)(2,1)S(1)}, bf16[2,4,8,1024]{3,2,1,0:T(8,128)(2,1)S(1)}, u32[]{:S(2)}, u32[]{:S(2)}) collective-permute-start(bf16[2,4,8,1024]{3,2,1,0:T(8,128)(2,1)S(1)} %pad_maximum_fusion.21), channel_id=1, source_target_pairs={{0,4},{2,6},{4,8},{6,10},{8,12},{10,14},{12,0},{14,2},{1,5},{3,7},... | collective-permute-start | bytes 393224 | tf_op jit(solution)/shard_map/ppermute | solution.py:328
  144.3 1.1 collective-permute-done.15
  145.4 13.2 %collective-permute-start.27 = (bf16[2,4,8,1024]{3,2,1,0:T(8,128)(2,1)S(1)}, bf16[2,4,8,1024]{3,2,1,0:T(8,128)(2,1)S(1)}, u32[]{:S(2)}, u32[]{:S(2)}) collective-permute-start(bf16[2,4,8,1024]{3,2,1,0:T(8,128)(2,1)S(1)} %pad_maximum_fusion.24), channel_id=1, source_target_pairs={{0,4},{2,6},{4,8},{6,10},{8,12},{10,14},{12,0},{14,2},{1,5},{3,7},... | collective-permute-start | bytes 393224 | tf_op jit(solution)/shard_map/ppermute | solution.py:328
  158.6 0.8 collective-permute-done.16
  159.8 0.4 copy.21
  160.3 0.8 collective-permute-done.27
  161.5 0.4 copy.19
  162.0 1.4 collective-permute-start.29
  163.4 4.6 %collective-permute-start.28 = (bf16[1,64,1024]{2,1,0:T(8,128)(2,1)S(1)}, bf16[1,64,1024]{2,1,0:T(8,128)(2,1)S(1)}, u32[]{:S(2)}, u32[]{:S(2)}) collective-permute-start(bf16[1,64,1024]{2,1,0:T(8,128)(2,1)S(1)} %bitcast.249), channel_id=1, source_target_pairs={{0,2},{2,4},{4,6},{6,8},{8,10},{10,12},{12,14},{1,3},{3,5},{5,7},{... | collective-permute-start | bytes 393224 | tf_op jit(solution)/shard_map/ppermute | solution.py:323
  168.0 1.0 collective-permute-done.29
  169.0 1.5 collective-permute-done.28
  170.5 0.2 concatenate.19
  170.6 1.3 collective-permute-start.31
  171.9 0.2 concatenate.18
  172.1 3.2 %collective-permute-start.30 = (bf16[10,1024]{1,0:T(8,128)(2,1)S(1)}, bf16[10,1024]{1,0:T(8,128)(2,1)S(1)}, u32[]{:S(2)}, u32[]{:S(2)}) collective-permute-start(bf16[10,1024]{1,0:T(8,128)(2,1)S(1)} %concatenate.18), channel_id=1, source_target_pairs={{0,1},{2,3},{4,5},{6,7},{8,9},{10,11},{12,13},{14,15},{16,17},{18,... | collective-permute-start | bytes 61448 | tf_op jit(solution)/shard_map/ppermute | solution.py:323
  175.4 1.2 copy.20
  176.6 0.2 broadcast_in_dim.21.keep
  176.9 8.5 %shard_map.116 = bf16[2048,256]{1,0:T(8,128)(2,1)} custom-call(bf16[256,1024]{1,0:T(8,128)(2,1)S(1)} %bitcast.221, bf16[256,1024]{1,0:T(8,128)(2,1)S(1)} %bitcast.222, bf16[64,1024]{1,0:T(8,128)(2,1)S(1)} %bitcast.233, bf16[64,1024]{1,0:T(8,128)(2,1)S(1)} %bitcast.232, bf16[10,1024]{1,0:T(8,128)(2,1)S(1)} %collective-permute-done.30.left, ...), custom_call_target="tpu_custom_call" | custom-call | tf_op jit(solution)/shard_map/pallas_call | solution.py:280
  (105 shorter events, 3.2 us)
Async XLA Ops:
  0.0 1.3 copy-start
  1.3 1.3 copy-start.1
  2.6 1.3 copy-start.2
  8.5 1.6 copy-start.12
  9.5 14.2 %collective-permute-start.8 = (bf16[4,128,640]{2,1,0:T(8,128)(2,1)}, bf16[4,128,640]{2,1,0:T(8,128)(2,1)S(1)}, u32[]{:S(2)}, u32[]{:S(2)}) collective-permute-start(bf16[4,128,640]{2,1,0:T(8,128)(2,1)} %get-tuple-element.28), channel_id=1, source_target_pairs={{0,1},{1,0},{2,3},{3,2},{4,5},{5,4},{6,7},{7,6},{8,9},{9,8},{10,11... | collective-permute-start | bytes 1966088 | tf_op jit(solution)/shard_map/ppermute | solution.py:332
  12.6 11.0 %collective-permute-start = (bf16[4,4,8,1280]{3,2,1,0:T(8,128)(2,1)}, bf16[4,4,8,1280]{3,2,1,0:T(8,128)(2,1)S(1)}, u32[]{:S(2)}, u32[]{:S(2)}) collective-permute-start(bf16[4,4,8,1280]{3,2,1,0:T(8,128)(2,1)} %get-tuple-element.58), channel_id=1, source_target_pairs={{0,2},{2,0},{4,6},{6,4},{8,10},{10,8},{12,14},{14,12},{1,3},{3,1},... | collective-permute-start | bytes 983048 | tf_op jit(solution)/shard_map/ppermute | solution.py:332
  16.5 19.9 %collective-permute-start.1 = (bf16[4,4,2,8,1280]{4,3,2,1,0:T(8,128)(2,1)}, bf16[4,4,2,8,1280]{4,3,2,1,0:T(8,128)(2,1)}, u32[]{:S(2)}, u32[]{:S(2)}) collective-permute-start(bf16[4,4,2,8,1280]{4,3,2,1,0:T(8,128)(2,1)} %pad_maximum_fusion.2), channel_id=1, source_target_pairs={{0,4},{2,6},{4,8},{6,10},{8,12},{10,14},{12,0},{14,2},{1,5},{3,7},... | collective-permute-start | bytes 1966088 | tf_op jit(solution)/shard_map/ppermute | solution.py:328
  18.1 45.1 %collective-permute-start.3 = (bf16[4,4,2,8,1280]{4,3,2,1,0:T(8,128)(2,1)S(1)}, bf16[4,4,2,8,1280]{4,3,2,1,0:T(8,128)(2,1)}, u32[]{:S(2)}, u32[]{:S(2)}) collective-permute-start(bf16[4,4,2,8,1280]{4,3,2,1,0:T(8,128)(2,1)S(1)} %pad_maximum_fusion.3), channel_id=1, source_target_pairs={{0,8},{2,10},{4,12},{6,14},{8,0},{10,2},{12,4},{14,6},{1,9},{3,11}... | collective-permute-start | bytes 1966088 | tf_op jit(solution)/shard_map/ppermute | solution.py:328
  20.9 44.0 %collective-permute-start.5 = (bf16[4,4,2,8,1280]{4,3,2,1,0:T(8,128)(2,1)S(1)}, bf16[4,4,2,8,1280]{4,3,2,1,0:T(8,128)(2,1)}, u32[]{:S(2)}, u32[]{:S(2)}) collective-permute-start(bf16[4,4,2,8,1280]{4,3,2,1,0:T(8,128)(2,1)S(1)} %pad_maximum_fusion.4), channel_id=1, source_target_pairs={{0,12},{2,14},{4,0},{6,2},{8,4},{10,6},{12,8},{14,10},{1,13},{3,15... | collective-permute-start | bytes 1966088 | tf_op jit(solution)/shard_map/ppermute | solution.py:328
  24.0 44.4 %collective-permute-start.19 = (bf16[4,2,4,8,640]{4,3,2,1,0:T(8,128)(2,1)S(1)}, bf16[4,2,4,8,640]{4,3,2,1,0:T(8,128)(2,1)S(1)}, u32[]{:S(2)}, u32[]{:S(2)}) collective-permute-start(bf16[4,2,4,8,640]{4,3,2,1,0:T(8,128)(2,1)S(1)} %dynamic-slice_bitcast_fusion.7), channel_id=1, source_target_pairs={{0,2},{2,0},{4,6},{6,4},{8,10},{10,8},{12,14},{14,12},{1,3},{3,1},... | collective-permute-start | bytes 983048 | tf_op jit(solution)/shard_map/ppermute | solution.py:332
  37.5 46.6 %collective-permute-start.2 = (bf16[4,4,8,1280]{3,2,1,0:T(8,128)(2,1)S(1)}, bf16[4,4,8,1280]{3,2,1,0:T(8,128)(2,1)S(1)}, u32[]{:S(2)}, u32[]{:S(2)}) collective-permute-start(bf16[4,4,8,1280]{3,2,1,0:T(8,128)(2,1)S(1)} %get-tuple-element.60), channel_id=1, source_target_pairs={{0,2},{2,0},{4,6},{6,4},{8,10},{10,8},{12,14},{14,12},{1,3},{3,1},... | collective-permute-start | bytes 983048 | tf_op jit(solution)/shard_map/ppermute | solution.py:332
  64.3 20.0 %collective-permute-start.4 = (bf16[4,4,8,1280]{3,2,1,0:T(8,128)(2,1)S(1)}, bf16[4,4,8,1280]{3,2,1,0:T(8,128)(2,1)S(1)}, u32[]{:S(2)}, u32[]{:S(2)}) collective-permute-start(bf16[4,4,8,1280]{3,2,1,0:T(8,128)(2,1)S(1)} %get-tuple-element.62), channel_id=1, source_target_pairs={{0,2},{2,0},{4,6},{6,4},{8,10},{10,8},{12,14},{14,12},{1,3},{3,1},... | collective-permute-start | bytes 983048 | tf_op jit(solution)/shard_map/ppermute | solution.py:332
  66.0 21.7 %collective-permute-start.6 = (bf16[4,4,8,1280]{3,2,1,0:T(8,128)(2,1)S(1)}, bf16[4,4,8,1280]{3,2,1,0:T(8,128)(2,1)S(1)}, u32[]{:S(2)}, u32[]{:S(2)}) collective-permute-start(bf16[4,4,8,1280]{3,2,1,0:T(8,128)(2,1)S(1)} %get-tuple-element.64), channel_id=1, source_target_pairs={{0,2},{2,0},{4,6},{6,4},{8,10},{10,8},{12,14},{14,12},{1,3},{3,1},... | collective-permute-start | bytes 983048 | tf_op jit(solution)/shard_map/ppermute | solution.py:332
  67.8 20.6 %collective-permute-start.9 = (bf16[4,2,4,8,640]{4,3,2,1,0:T(8,128)(2,1)S(1)}, bf16[4,2,4,8,640]{4,3,2,1,0:T(8,128)(2,1)S(1)}, u32[]{:S(2)}, u32[]{:S(2)}) collective-permute-start(bf16[4,2,4,8,640]{4,3,2,1,0:T(8,128)(2,1)S(1)} %dynamic-slice_bitcast_fusion.8), channel_id=1, source_target_pairs={{0,2},{2,0},{4,6},{6,4},{8,10},{10,8},{12,14},{14,12},{1,3},{3,1},... | collective-permute-start | bytes 983048 | tf_op jit(solution)/shard_map/ppermute | solution.py:332
  68.5 36.8 %collective-permute-start.22 = (bf16[2,2,32,640]{3,2,1,0:T(8,128)(2,1)S(1)}, bf16[2,2,32,640]{3,2,1,0:T(8,128)(2,1)S(1)}, u32[]{:S(2)}, u32[]{:S(2)}) collective-permute-start(bf16[2,2,32,640]{3,2,1,0:T(8,128)(2,1)S(1)} %pad_maximum_fusion.18), channel_id=1, source_target_pairs={{0,12},{2,14},{4,0},{6,2},{8,4},{10,6},{12,8},{14,10},{1,13},{3,15... | collective-permute-start | bytes 491528 | tf_op jit(solution)/shard_map/ppermute | solution.py:328
  84.1 21.2 %collective-permute-start.21 = (bf16[2,2,32,640]{3,2,1,0:T(8,128)(2,1)S(1)}, bf16[2,2,32,640]{3,2,1,0:T(8,128)(2,1)S(1)}, u32[]{:S(2)}, u32[]{:S(2)}) collective-permute-start(bf16[2,2,32,640]{3,2,1,0:T(8,128)(2,1)S(1)} %pad_maximum_fusion.17), channel_id=1, source_target_pairs={{0,8},{2,10},{4,12},{6,14},{8,0},{10,2},{12,4},{14,6},{1,9},{3,11}... | collective-permute-start | bytes 491528 | tf_op jit(solution)/shard_map/ppermute | solution.py:328
  84.3 21.6 %collective-permute-start.20 = (bf16[2,2,32,640]{3,2,1,0:T(8,128)(2,1)S(1)}, bf16[2,2,32,640]{3,2,1,0:T(8,128)(2,1)S(1)}, u32[]{:S(2)}, u32[]{:S(2)}) collective-permute-start(bf16[2,2,32,640]{3,2,1,0:T(8,128)(2,1)S(1)} %pad_maximum_fusion.16), channel_id=1, source_target_pairs={{0,4},{2,6},{4,8},{6,10},{8,12},{10,14},{12,0},{14,2},{1,5},{3,7},... | collective-permute-start | bytes 491528 | tf_op jit(solution)/shard_map/ppermute | solution.py:328
  88.3 2.2 %collective-permute-start.18 = (bf16[2,256,640]{2,1,0:T(8,128)(2,1)S(1)}, bf16[2,256,640]{2,1,0:T(8,128)(2,1)S(1)}, u32[]{:S(2)}, u32[]{:S(2)}) collective-permute-start(bf16[2,256,640]{2,1,0:T(8,128)(2,1)S(1)} %get-tuple-element.17), channel_id=1, source_target_pairs={{0,1},{1,0},{2,3},{3,2},{4,5},{5,4},{6,7},{7,6},{8,9},{9,8},{10,11... | collective-permute-start | bytes 1966088 | tf_op jit(solution)/shard_map/ppermute | solution.py:332
  88.4 19.0 %collective-permute-start.7 = (bf16[2,256,640]{2,1,0:T(8,128)(2,1)S(1)}, bf16[2,256,640]{2,1,0:T(8,128)(2,1)S(1)}, u32[]{:S(2)}, u32[]{:S(2)}) collective-permute-start(bf16[2,256,640]{2,1,0:T(8,128)(2,1)S(1)} %get-tuple-element.18), channel_id=1, source_target_pairs={{0,1},{1,0},{2,3},{3,2},{4,5},{5,4},{6,7},{7,6},{8,9},{9,8},{10,11... | collective-permute-start | bytes 1966088 | tf_op jit(solution)/shard_map/ppermute | solution.py:332
  90.4 19.4 %collective-permute-start.12 = (bf16[2,2,32,640]{3,2,1,0:T(8,128)(2,1)S(1)}, bf16[2,2,32,640]{3,2,1,0:T(8,128)(2,1)S(1)}, u32[]{:S(2)}, u32[]{:S(2)}) collective-permute-start(bf16[2,2,32,640]{3,2,1,0:T(8,128)(2,1)S(1)} %pad_maximum_fusion.14), channel_id=1, source_target_pairs={{0,12},{2,14},{4,0},{6,2},{8,4},{10,6},{12,8},{14,10},{1,13},{3,15... | collective-permute-start | bytes 491528 | tf_op jit(solution)/shard_map/ppermute | solution.py:328
  105.2 13.0 %collective-permute-start.11 = (bf16[2,2,32,640]{3,2,1,0:T(8,128)(2,1)S(1)}, bf16[2,2,32,640]{3,2,1,0:T(8,128)(2,1)S(1)}, u32[]{:S(2)}, u32[]{:S(2)}) collective-permute-start(bf16[2,2,32,640]{3,2,1,0:T(8,128)(2,1)S(1)} %pad_maximum_fusion.13), channel_id=1, source_target_pairs={{0,8},{2,10},{4,12},{6,14},{8,0},{10,2},{12,4},{14,6},{1,9},{3,11}... | collective-permute-start | bytes 491528 | tf_op jit(solution)/shard_map/ppermute | solution.py:328
  105.3 12.9 %collective-permute-start.10 = (bf16[2,2,32,640]{3,2,1,0:T(8,128)(2,1)S(1)}, bf16[2,2,32,640]{3,2,1,0:T(8,128)(2,1)S(1)}, u32[]{:S(2)}, u32[]{:S(2)}) collective-permute-start(bf16[2,2,32,640]{3,2,1,0:T(8,128)(2,1)S(1)} %pad_maximum_fusion.12), channel_id=1, source_target_pairs={{0,4},{2,6},{4,8},{6,10},{8,12},{10,14},{12,0},{14,2},{1,5},{3,7},... | collective-permute-start | bytes 491528 | tf_op jit(solution)/shard_map/ppermute | solution.py:328
  107.3 16.7 %collective-permute-start.23 = (bf16[256,640]{1,0:T(8,128)(2,1)}, bf16[256,640]{1,0:T(8,128)(2,1)S(1)}, u32[]{:S(2)}, u32[]{:S(2)}) collective-permute-start(bf16[256,640]{1,0:T(8,128)(2,1)} %get-tuple-element.12), channel_id=1, source_target_pairs={{0,1},{1,0},{2,3},{3,2},{4,5},{5,4},{6,7},{7,6},{8,9},{9,8},{10,11... | collective-permute-start | bytes 983048 | tf_op jit(solution)/shard_map/ppermute | solution.py:332
  109.8 10.7 %copy-start.10 = (bf16[1280,1024]{1,0:T(8,128)(2,1)S(1)}, bf16[1280,1024]{1,0:T(8,128)(2,1)}, u32[]{:S(2)}) copy-start(bf16[1280,1024]{1,0:T(8,128)(2,1)} %param.16) | copy-start | bytes 7864324
  119.6 0.7 copy-start.5
  120.4 3.6 %copy-start.7 = (f32[1024]{0:T(1024)S(1)}, f32[1024]{0:T(1024)}, u32[]{:S(2)}) copy-start(f32[1024]{0:T(1024)} %param.17) | copy-start | bytes 12292
  120.4 5.2 %collective-permute-start.13 = (bf16[256,640]{1,0:T(8,128)(2,1)}, bf16[256,640]{1,0:T(8,128)(2,1)}, u32[]{:S(2)}, u32[]{:S(2)}) collective-permute-start(bf16[256,640]{1,0:T(8,128)(2,1)} %get-tuple-element.10), channel_id=1, source_target_pairs={{0,1},{1,0},{2,3},{3,2},{4,5},{5,4},{6,7},{7,6},{8,9},{9,8},{10,11... | collective-permute-start | bytes 983048 | tf_op jit(solution)/shard_map/ppermute | solution.py:332
  124.0 1.5 copy-start.6
  125.0 9.2 %collective-permute-start.24 = (bf16[4,4,8,1024]{3,2,1,0:T(8,128)(2,1)S(1)}, bf16[4,4,8,1024]{3,2,1,0:T(8,128)(2,1)S(1)}, u32[]{:S(2)}, u32[]{:S(2)}) collective-permute-start(bf16[4,4,8,1024]{3,2,1,0:T(8,128)(2,1)S(1)} %slice_bitcast_fusion.4), channel_id=1, source_target_pairs={{0,2},{2,0},{4,6},{6,4},{8,10},{10,8},{12,14},{14,12},{1,3},{3,1},... | collective-permute-start | bytes 786440 | tf_op jit(solution)/shard_map/ppermute | solution.py:332
  127.5 11.9 %collective-permute-start.14 = (bf16[4,4,8,1024]{3,2,1,0:T(8,128)(2,1)S(1)}, bf16[4,4,8,1024]{3,2,1,0:T(8,128)(2,1)S(1)}, u32[]{:S(2)}, u32[]{:S(2)}) collective-permute-start(bf16[4,4,8,1024]{3,2,1,0:T(8,128)(2,1)S(1)} %slice_bitcast_fusion.5), channel_id=1, source_target_pairs={{0,2},{2,0},{4,6},{6,4},{8,10},{10,8},{12,14},{14,12},{1,3},{3,1},... | collective-permute-start | bytes 786440 | tf_op jit(solution)/shard_map/ppermute | solution.py:332
  134.2 26.1 %collective-permute-start.25 = (bf16[2,4,8,1024]{3,2,1,0:T(8,128)(2,1)S(1)}, bf16[2,4,8,1024]{3,2,1,0:T(8,128)(2,1)S(1)}, u32[]{:S(2)}, u32[]{:S(2)}) collective-permute-start(bf16[2,4,8,1024]{3,2,1,0:T(8,128)(2,1)S(1)} %pad_maximum_fusion.22), channel_id=1, source_target_pairs={{0,12},{2,14},{4,0},{6,2},{8,4},{10,6},{12,8},{14,10},{1,13},{3,15... | collective-permute-start | bytes 393224 | tf_op jit(solution)/shard_map/ppermute | solution.py:328
  134.3 26.0 %collective-permute-start.26 = (bf16[2,4,8,1024]{3,2,1,0:T(8,128)(2,1)S(1)}, bf16[2,4,8,1024]{3,2,1,0:T(8,128)(2,1)S(1)}, u32[]{:S(2)}, u32[]{:S(2)}) collective-permute-start(bf16[2,4,8,1024]{3,2,1,0:T(8,128)(2,1)S(1)} %pad_maximum_fusion.23), channel_id=1, source_target_pairs={{0,8},{2,10},{4,12},{6,14},{8,0},{10,2},{12,4},{14,6},{1,9},{3,11}... | collective-permute-start | bytes 393224 | tf_op jit(solution)/shard_map/ppermute | solution.py:328
  139.4 6.1 %collective-permute-start.15 = (bf16[2,4,8,1024]{3,2,1,0:T(8,128)(2,1)S(1)}, bf16[2,4,8,1024]{3,2,1,0:T(8,128)(2,1)S(1)}, u32[]{:S(2)}, u32[]{:S(2)}) collective-permute-start(bf16[2,4,8,1024]{3,2,1,0:T(8,128)(2,1)S(1)} %pad_maximum_fusion.19), channel_id=1, source_target_pairs={{0,12},{2,14},{4,0},{6,2},{8,4},{10,6},{12,8},{14,10},{1,13},{3,15... | collective-permute-start | bytes 393224 | tf_op jit(solution)/shard_map/ppermute | solution.py:328
  139.5 19.9 %collective-permute-start.16 = (bf16[2,4,8,1024]{3,2,1,0:T(8,128)(2,1)S(1)}, bf16[2,4,8,1024]{3,2,1,0:T(8,128)(2,1)S(1)}, u32[]{:S(2)}, u32[]{:S(2)}) collective-permute-start(bf16[2,4,8,1024]{3,2,1,0:T(8,128)(2,1)S(1)} %pad_maximum_fusion.20), channel_id=1, source_target_pairs={{0,8},{2,10},{4,12},{6,14},{8,0},{10,2},{12,4},{14,6},{1,9},{3,11}... | collective-permute-start | bytes 393224 | tf_op jit(solution)/shard_map/ppermute | solution.py:328
  142.2 17.3 %collective-permute-start.17 = (bf16[2,4,8,1024]{3,2,1,0:T(8,128)(2,1)S(1)}, bf16[2,4,8,1024]{3,2,1,0:T(8,128)(2,1)S(1)}, u32[]{:S(2)}, u32[]{:S(2)}) collective-permute-start(bf16[2,4,8,1024]{3,2,1,0:T(8,128)(2,1)S(1)} %pad_maximum_fusion.21), channel_id=1, source_target_pairs={{0,4},{2,6},{4,8},{6,10},{8,12},{10,14},{12,0},{14,2},{1,5},{3,7},... | collective-permute-start | bytes 393224 | tf_op jit(solution)/shard_map/ppermute | solution.py:328
  145.4 15.7 %collective-permute-start.27 = (bf16[2,4,8,1024]{3,2,1,0:T(8,128)(2,1)S(1)}, bf16[2,4,8,1024]{3,2,1,0:T(8,128)(2,1)S(1)}, u32[]{:S(2)}, u32[]{:S(2)}) collective-permute-start(bf16[2,4,8,1024]{3,2,1,0:T(8,128)(2,1)S(1)} %pad_maximum_fusion.24), channel_id=1, source_target_pairs={{0,4},{2,6},{4,8},{6,10},{8,12},{10,14},{12,0},{14,2},{1,5},{3,7},... | collective-permute-start | bytes 393224 | tf_op jit(solution)/shard_map/ppermute | solution.py:328
  161.5 15.4 %copy-start.3 = (bf16[3,3,256,256]{3,2,1,0:T(8,128)(2,1)S(1)}, bf16[3,3,256,256]{3,2,1,0:T(8,128)(2,1)}, u32[]{:S(2)}) copy-start(bf16[3,3,256,256]{3,2,1,0:T(8,128)(2,1)} %param.18) | copy-start | bytes 3538948
  161.5 15.4 %copy-start.4 = (bf16[3,3,256,256]{3,2,1,0:T(8,128)(2,1)S(1)}, bf16[3,3,256,256]{3,2,1,0:T(8,128)(2,1)}, u32[]{:S(2)}) copy-start(bf16[3,3,256,256]{3,2,1,0:T(8,128)(2,1)} %param.20) | copy-start | bytes 3538948
  161.5 15.4 %copy-start.8 = (f32[256]{0:T(256)S(1)}, f32[256]{0:T(256)}, u32[]{:S(2)}) copy-start(f32[256]{0:T(256)} %param.19) | copy-start | bytes 3076
  161.5 15.4 %copy-start.9 = (f32[256]{0:T(256)S(1)}, f32[256]{0:T(256)}, u32[]{:S(2)}) copy-start(f32[256]{0:T(256)} %param.21) | copy-start | bytes 3076
  161.9 8.5 %copy-start.11 = (bf16[4,4,2,8,1024]{4,1,3,2,0:T(4,128)(2,1)}, bf16[4,4,2,8,1024]{4,1,3,2,0:T(4,128)(2,1)S(1)}, u32[]{:S(2)}) copy-start(bf16[4,4,2,8,1024]{4,1,3,2,0:T(4,128)(2,1)S(1)} %copy.19) | copy-start | bytes 1572868
  162.0 7.0 %collective-permute-start.29 = (bf16[1,64,1024]{2,1,0:T(8,128)(2,1)S(1)}, bf16[1,64,1024]{2,1,0:T(8,128)(2,1)S(1)}, u32[]{:S(2)}, u32[]{:S(2)}) collective-permute-start(bf16[1,64,1024]{2,1,0:T(8,128)(2,1)S(1)} %bitcast.250), channel_id=1, source_target_pairs={{2,0},{4,2},{6,4},{8,6},{10,8},{12,10},{14,12},{3,1},{5,3},{7,5},{... | collective-permute-start | bytes 393224 | tf_op jit(solution)/shard_map/ppermute | solution.py:323
  163.4 7.1 %collective-permute-start.28 = (bf16[1,64,1024]{2,1,0:T(8,128)(2,1)S(1)}, bf16[1,64,1024]{2,1,0:T(8,128)(2,1)S(1)}, u32[]{:S(2)}, u32[]{:S(2)}) collective-permute-start(bf16[1,64,1024]{2,1,0:T(8,128)(2,1)S(1)} %bitcast.249), channel_id=1, source_target_pairs={{0,2},{2,4},{4,6},{6,8},{8,10},{10,12},{12,14},{1,3},{3,5},{5,7},{... | collective-permute-start | bytes 393224 | tf_op jit(solution)/shard_map/ppermute | solution.py:323
  170.6 6.0 %collective-permute-start.31 = (bf16[10,1024]{1,0:T(8,128)(2,1)S(1)}, bf16[10,1024]{1,0:T(8,128)(2,1)S(1)}, u32[]{:S(2)}, u32[]{:S(2)}) collective-permute-start(bf16[10,1024]{1,0:T(8,128)(2,1)S(1)} %concatenate.19), channel_id=1, source_target_pairs={{1,0},{3,2},{5,4},{7,6},{9,8},{11,10},{13,12},{15,14},{17,16},{19,... | collective-permute-start | bytes 61448 | tf_op jit(solution)/shard_map/ppermute | solution.py:323
  172.1 4.5 %collective-permute-start.30 = (bf16[10,1024]{1,0:T(8,128)(2,1)S(1)}, bf16[10,1024]{1,0:T(8,128)(2,1)S(1)}, u32[]{:S(2)}, u32[]{:S(2)}) collective-permute-start(bf16[10,1024]{1,0:T(8,128)(2,1)S(1)} %concatenate.18), channel_id=1, source_target_pairs={{0,1},{2,3},{4,5},{6,7},{8,9},{10,11},{12,13},{14,15},{16,17},{18,... | collective-permute-start | bytes 61448 | tf_op jit(solution)/shard_map/ppermute | solution.py:323

commit v3 on v2

--- a/solution.py
+++ b/solution.py
@@ -15,6 +15,7 @@
 TILE_COLS = 16
 LANES = 128
 EDGE = 16
+PIECE = 8
 SPAN = 2 * LANES
 VMEM_BYTES = 40 * 1024 * 1024
 
@@ -89,80 +90,165 @@
     )(query, key_rows, value)
 
 
-def weights_kernel(tokens, query_near, query_far, key_near, key_far, out):
+def token_of(place, part, owned, places):
+    chunk = owned * places
+    if part:
+        return chunk // 2 + place * owned
+    return place * owned if place * owned < chunk // 2 else chunk + place * owned
+
+
+def deal_kernel(query, key_rows, out, held, packed, arrived, left):
+    places, cores, parts, kinds, block, half = out.shape
+    windows = query.shape[0]
+    owned = block // windows
+    copies = [
+        pltpu.make_async_copy(source, held.at[kind], arrived.at[kind])
+        for kind, source in enumerate((query, key_rows))
+    ]
+    for copy in copies:
+        copy.start()
+    for copy in copies:
+        copy.wait()
+    copies = []
+    for place in range(places):
+        for part in range(parts):
+            rows = pl.ds(token_of(place, part, owned, places), owned)
+            for kind in range(kinds):
+                for window in range(windows):
+                    for core in range(cores):
+                        packed[place, core, part, kind, pl.ds(window * owned, owned), :] = held[
+                            kind, window, rows, core * half : (core + 1) * half
+                        ]
+        copy = pltpu.make_async_copy(packed.at[place], out.at[place], left.at[place])
+        copy.start()
+        copies.append(copy)
+    for copy in copies:
+        copy.wait()
+
+
+def dealt(query, key_rows, places, cores):
+    windows, tokens, features = query.shape
+    result = (places, cores, 2, 2, windows * tokens // (2 * places), features // cores)
+    return pl.pallas_call(
+        deal_kernel,
+        in_specs=[pl.BlockSpec(memory_space=pltpu.HBM)] * 2,
+        out_specs=pl.BlockSpec(memory_space=pltpu.HBM),
+        out_shape=pltpu.HBM(result, query.dtype),
+        scratch_shapes=[
+            pltpu.VMEM((2,) + query.shape, query.dtype),
+            pltpu.VMEM(result, query.dtype),
+            pltpu.SemaphoreType.DMA((2,)),
+            pltpu.SemaphoreType.DMA((places,)),
+        ],
+        compiler_params=params(),
+    )(
+        pltpu.with_memory_space_constraint(query, pltpu.HBM),
+        pltpu.with_memory_space_constraint(key_rows, pltpu.HBM),
+    )
+
+
+def weights_kernel(tokens, core, pair, out):
+    places, cores, _, _, block, _ = pair.shape
     head = pl.program_id(0)
     start = head * HEAD_DIM // LANES * LANES
     lanes = pl.ds(pl.multiple_of(start, LANES), SPAN)
     lane = lax.broadcasted_iota(jnp.int32, (1, SPAN), 1) + start
     inside = (lane >= head * HEAD_DIM) & (lane < (head + 1) * HEAD_DIM)
-    query = jnp.concatenate([query_near[:, lanes], query_far[:, lanes]], axis=0)
-    key_rows = jnp.concatenate([key_near[:, lanes], key_far[:, lanes]], axis=0)
+    held = jnp.float32 if block % EDGE else jnp.bfloat16
+
+    def gathered(kind):
+        return jnp.concatenate(
+            [
+                pair[place, core[0] ^ far, 0, kind, :, lanes].astype(held)
+                for far in range(cores)
+                for place in range(places)
+            ],
+            axis=0,
+        ).astype(jnp.bfloat16)
+
     scores = lax.dot_general(
-        jnp.where(inside, query, 0), key_rows, (((1,), (1,)), ((), ())),
+        jnp.where(inside, gathered(0), 0), gathered(1), (((1,), (1,)), ((), ())),
         preferred_element_type=jnp.float32,
     ) * (1.0 / math.sqrt(HEAD_DIM))
-    rows = query.shape[0]
+    rows = scores.shape[0]
     token_row = lax.broadcasted_iota(jnp.int32, (rows, 1), 0) % tokens
     token_col = lax.broadcasted_iota(jnp.int32, (1, rows), 1) % tokens
     out[0] = softmax_rows(jnp.where(token_row == token_col, scores, -jnp.inf))
 
 
-def index_weights(query_near, query_far, key_near, key_far, tokens):
-    rows, features = query_near.shape
+def index_weights(core, pair, part, tokens):
+    places, cores, _, kinds, block, features = pair.shape
     heads = features // HEAD_DIM
-    whole = pl.BlockSpec((rows, features), lambda h: (0, 0))
+    rows = places * cores * block
     return pl.pallas_call(
         functools.partial(weights_kernel, tokens),
         grid=(heads,),
-        in_specs=[whole] * 4,
-        out_specs=pl.BlockSpec((1, 2 * rows, 2 * rows), lambda h: (h, 0, 0)),
-        out_shape=jax.ShapeDtypeStruct((heads, 2 * rows, 2 * rows), jnp.bfloat16),
+        in_specs=[
+            pl.BlockSpec(memory_space=pltpu.SMEM),
+            pl.BlockSpec((places, cores, 1, kinds, block, features), lambda h: (0, 0, part, 0, 0, 0)),
+        ],
+        out_specs=pl.BlockSpec((1, rows, rows), lambda h: (h, 0, 0)),
+        out_shape=jax.ShapeDtypeStruct((heads, rows, rows), jnp.bfloat16),
         compiler_params=params(1),
-    )(query_near, query_far, key_near, key_far)
-
-
-def mix_kernel(weights, *refs):
-    pieces, (near, far) = refs[:-2], refs[-2:]
-    inner, cores, _, features = pieces[0].shape
-    value = jnp.concatenate(
-        [piece[j, core] for core in range(cores) for piece in pieces for j in range(inner)], axis=0
-    )
+    )(core.reshape(1), pair)
+
+
+def mix_kernel(place, weights, *refs):
+    pieces, (near, far, value) = refs[:-3], refs[-3:]
+    inner, cores, rows, features = pieces[0].shape
+    half = value.shape[0] // cores
+    for k, piece in enumerate(pieces):
+        for j in range(inner):
+            at = pl.multiple_of((place[0] ^ (k * inner + j)) * rows, rows)
+            for core in range(cores):
+                value[pl.ds(core * half + at, rows), :] = piece[j, core].astype(value.dtype)
     mixed = []
     for head in range(features // HEAD_DIM):
         lanes = slice(head_start(head), head_start(head) + SPAN)
-        mixed.append(jnp.dot(weights[head], value[:, lanes], preferred_element_type=jnp.float32))
+        mixed.append(
+            jnp.dot(
+                weights[head], value[:, lanes].astype(jnp.bfloat16),
+                preferred_element_type=jnp.float32,
+            )
+        )
     joined = joined_heads(mixed).astype(jnp.bfloat16)
-    half = value.shape[0] // 2
     near[...] = joined[:half]
     far[...] = joined[half:]
 
 
-def index_mix(weights, pieces):
+def index_mix(place, weights, pieces):
     rows, features = weights.shape[1], pieces[0].shape[-1]
     result = jax.ShapeDtypeStruct((rows // 2, features), jnp.bfloat16)
+    held = jnp.float32 if pieces[0].shape[2] % EDGE else jnp.bfloat16
     return pl.pallas_call(
         mix_kernel,
-        in_specs=[pl.BlockSpec(memory_space=pltpu.VMEM)] * (1 + len(pieces)),
+        in_specs=[pl.BlockSpec(memory_space=pltpu.SMEM)]
+        + [pl.BlockSpec(memory_space=pltpu.VMEM)] * (1 + len(pieces)),
         out_specs=[pl.BlockSpec(memory_space=pltpu.VMEM)] * 2,
         out_shape=[result, result],
+        scratch_shapes=[pltpu.VMEM((rows, features), held)],
         compiler_params=params(),
-    )(weights, *pieces)
-
-
-def project_kernel(near, far, proj_weight, proj_bias, out):
-    joined = jnp.concatenate([near[...], far[...]], axis=1)
-    total = jnp.dot(joined, proj_weight[...], preferred_element_type=jnp.float32)
-    out[...] = (total + proj_bias[...]).astype(jnp.bfloat16)
-
-
-def project(near, far, proj_weight, proj_bias):
+    )(place.reshape(1), weights, *pieces)
+
+
+def project_kernel(core, near, far, proj_weight, proj_bias, out):
+    half = near.shape[1]
+    total = proj_bias[...]
+    for held, place in ((near, core[0]), (far, 1 - core[0])):
+        rows = pl.ds(pl.multiple_of(place * half, half), half)
+        total = total + jnp.dot(held[...], proj_weight[rows, :], preferred_element_type=jnp.float32)
+    out[...] = total.astype(jnp.bfloat16)
+
+
+def project(near, far, proj_weight, proj_bias, core):
     return pl.pallas_call(
         project_kernel,
-        in_specs=[pl.BlockSpec(memory_space=pltpu.VMEM)] * 4,
+        in_specs=[pl.BlockSpec(memory_space=pltpu.SMEM)]
+        + [pl.BlockSpec(memory_space=pltpu.VMEM)] * 4,
         out_specs=pl.BlockSpec(memory_space=pltpu.VMEM),
-        out_shape=jax.ShapeDtypeStruct((near.shape[0], proj_weight.shape[1]), jnp.bfloat16),
+        out_shape=pltpu.HBM((near.shape[0], proj_weight.shape[1]), jnp.bfloat16),
         compiler_params=params(),
-    )(near, far, proj_weight, proj_bias.reshape(1, -1))
+    )(core.reshape(1), near, far, proj_weight, proj_bias.reshape(1, -1))
 
 
 def line_of(line, rows):
@@ -205,13 +291,22 @@
     taken[0:EDGE, 0:depth] = jnp.zeros((EDGE, depth), jnp.bfloat16)
     for i in range(rows + 2):
         if i == 0:
-            body = above[...]
+            source, at = above, 0
         elif i == rows + 1:
-            body = below[...]
+            source, at = below, 0
         else:
             part, at = line_of(i - 1, rows)
-            body = (outer, middle)[part][pl.ds(at * cols, cols), :]
-        body = body.astype(jnp.float32)
+            source = (outer, middle)[part]
+        _, windows, piece, _ = source.shape
+        per = TILE_COLS // piece
+        body = jnp.concatenate(
+            [
+                source[at * per + across, window].astype(jnp.float32)
+                for window in range(windows)
+                for across in range(per)
+            ],
+            axis=0,
+        )
         for p in range(2):
             lanes = slice(p * half, (p + 1) * half)
             y = 2 * i + p
@@ -273,7 +368,8 @@
 
 
 def convolve_twice(outer, middle, above, below, left, right, keep, first_kernel, first_bias, second_kernel, second_bias):
-    rows, cols, width = (2 * outer.shape[0],) + outer.shape[1:]
+    pieces, windows, piece, _ = outer.shape
+    rows, cols = 2 * pieces * piece // TILE_COLS, windows * TILE_COLS
     pitch = cols + EDGE
     total = (2 * rows + 2) * pitch + EDGE
     depth = CHANNELS
@@ -291,7 +387,7 @@
         ],
         compiler_params=params(),
     )(
-        outer.reshape(-1, width), middle.reshape(-1, width), above, below, left, right, keep,
+        outer, middle, above, below, left, right, keep,
         first_kernel.reshape(3, 3 * depth, depth), first_bias.reshape(1, depth),
         second_kernel.reshape(3, 3 * depth, depth), second_bias.reshape(1, depth),
     )
@@ -323,17 +419,29 @@
     return lax.ppermute(value, axis, pairs)
 
 
-def across(value, axis, by, unit=1):
-    size = lax.axis_size(axis)
-    return lax.ppermute(value, axis, [(i, (i + by * unit) % size) for i in range(size)])
-
-
-def paired(value, axis):
-    return lax.ppermute(value, axis, [(i, i ^ 1) for i in range(lax.axis_size(axis))])
+def swapped(value, axis, by):
+    return lax.ppermute(value, axis, [(i, i ^ by) for i in range(lax.axis_size(axis))])
+
+
+def exchanged(value, axes):
+    return lax.all_to_all(value, axes, split_axis=0, concat_axis=0, tiled=True)
+
+
+def in_pieces(value):
+    places, windows, owned, width = value.shape
+    if owned < PIECE:
+        joined = value.reshape(-1, PIECE // owned, windows, owned, width)
+        return jnp.swapaxes(joined, 1, 2).reshape(-1, windows, PIECE, width)
+    cut = value.reshape(places, windows, owned // PIECE, PIECE, width)
+    return jnp.swapaxes(cut, 1, 2).reshape(-1, windows, PIECE, width)
 
 
 def picked(value, index, axis=0):
     return lax.dynamic_index_in_dim(value, index, axis, keepdims=False)
+
+
+def after(value, *earlier):
+    return lax.optimization_barrier((value,) + earlier)[0]
 
 
 def shards(
@@ -343,95 +451,91 @@
     rows_dev, cols_dev, tokens_win, features = query_window.shape
     windows = rows_dev * cols_dev
     flat = (windows, tokens_win, features)
-    inner, cores = 2, lax.axis_size("col")
-    outer = lax.axis_size("row") // inner
+    inner, cores, places = 2, lax.axis_size("col"), lax.axis_size("row")
+    outer = places // inner
     row, core = lax.axis_index("row"), lax.axis_index("col")
     z, y = row // inner, row % inner
     chunk = tokens_win // 2
-    owned = chunk // (outer * inner)
-    slab = inner * owned
+    owned = chunk // places
     half = features // cores
 
-    def slab_of(value, part, place):
-        at = place * slab
+    def slab_of(value, part, place, count):
+        at = place * owned
         if part == 0:
             at = jnp.where(at < chunk // 2, at, at + chunk)
         else:
             at = at + chunk // 2
-        cut = lax.dynamic_slice_in_dim(value, at, slab, axis=value.ndim - 2)
-        return cut.reshape(cut.shape[:-2] + (inner, owned, cut.shape[-1]))
+        cut = lax.dynamic_slice_in_dim(value, at, count * owned, axis=value.ndim - 2)
+        return cut.reshape(cut.shape[:-2] + (count, owned, cut.shape[-1]))
 
     query, key_rows = query_index.reshape(flat), key_index.reshape(flat)
-    sent = []
-    for k in range(outer):
-        place = (z + k) % outer
-        block = jnp.stack(
-            [slab_of(value, part, place) for part in range(2) for value in (query, key_rows)]
-        )
-        sent.append(across(block, "row", k, inner) if k else block)
-    near = [picked(block, y, 2) for block in sent]
-    far = [paired(picked(block, 1 - y, 2), "row") for block in sent]
-    pair = jnp.stack([jnp.stack([a, b], axis=1) for a, b in zip(near, far)], axis=1)
-    pair = pair.reshape(2, 2, -1, features)
-    own_half = lax.dynamic_slice_in_dim(pair, core * half, half, axis=3)
-    other_half = lax.dynamic_slice_in_dim(pair, (1 - core) * half, half, axis=3)
-    weights = []
+    pair = exchanged(
+        dealt(query, key_rows, places, cores).reshape(places * cores, 2, 2, windows * owned, half),
+        ("row", "col"),
+    ).reshape(places, cores, 2, 2, windows * owned, half)
+
+    window_out = window_attend(
+        query_window.reshape(flat), key_window.reshape(flat),
+        value_window.reshape(flat), cores,
+    )
+    window_out = jnp.stack([picked(window_out, core), swapped(picked(window_out, 1 - core), "col", 1)])
+    blocks = jnp.stack(
+        [
+            jnp.stack([slab_of(window_out, part, (z ^ k) * inner, inner) for part in range(2)])
+            for k in range(outer)
+        ]
+    )
+    values_near, values_far = picked(blocks, y, 4), swapped(picked(blocks, 1 - y, 4), "row", 1)
+    weights = [index_weights(core, pair, part, owned) for part in range(2)]
+    keep = kept_rows(rows_dev * TILE_ROWS, cols_dev * TILE_COLS)
+
+    images = []
+    earlier = []
+    pieces = []
     for part in range(2):
-        here, there = own_half[part], paired(other_half[part], "col")
-        weights.append(index_weights(here[0], there[0], here[1], there[1], owned))
-
-    window_out = window_attend(
-        query_window.reshape(flat), key_window.reshape(flat), value_window.reshape(flat), cores
-    )
-    window_out = jnp.stack([picked(window_out, core), paired(picked(window_out, 1 - core), "col")])
-    ordered = jnp.concatenate([proj_weight, proj_weight], axis=0)
-    ordered = lax.dynamic_slice_in_dim(ordered, core * half, features, axis=0)
-    keep = kept_rows(rows_dev * TILE_ROWS, cols_dev * TILE_COLS)
-
-    images = []
+        pieces.append([])
+        for k in range(outer):
+            piece = jnp.stack([values_near[k, part], values_far[k, part]])
+            piece = piece.reshape(inner, cores, windows * owned, half)
+            pieces[part].append(swapped(piece, "row", k * inner) if k else piece)
     for part in range(2):
-        blocks = jnp.stack([slab_of(window_out, part, (z + k) % outer) for k in range(outer)])
-        here, there = picked(blocks, y, 3), paired(picked(blocks, 1 - y, 3), "row")
-        pieces = []
-        for k in range(outer):
-            piece = jnp.stack([here[k], there[k]]).reshape(inner, cores, windows * owned, half)
-            pieces.append(across(piece, "row", k, inner) if k else piece)
-        mixed_near, mixed_far = index_mix(weights[part], pieces)
-        projected = project(mixed_near, paired(mixed_far, "col"), ordered, proj_bias)
+        mixed_near, mixed_far = index_mix(row, after(weights[part], *earlier), pieces[part])
+        projected = project(mixed_near, swapped(mixed_far, "col", 1), proj_weight, proj_bias, core)
         width = projected.shape[-1]
-        projected = projected.reshape(outer, inner, windows, owned, width)
-        here, there = projected[:, 0], paired(projected[:, 1], "row")
-        returned = []
-        for k in range(outer):
-            piece = jnp.stack([here[k], there[k]])
-            returned.append(across(piece, "row", -k, inner) if k else piece)
-        returned = jnp.stack(returned)
-        placed = jnp.stack([picked(returned, (place - z) % outer) for place in range(outer)])
-        placed = jnp.where(y == 0, placed, placed[:, ::-1])
-        tokens = jnp.transpose(placed, (2, 0, 1, 3, 4)).reshape(
-            rows_dev, cols_dev, TILE_ROWS // 2, TILE_COLS, width
-        )
-        images.append(
-            jnp.transpose(tokens, (0, 2, 1, 3, 4)).reshape(-1, cols_dev * TILE_COLS, width)
-        )
-    image_outer, image_middle = images
-    above = shifted(image_outer[-1:], "row", 1)
-    below = shifted(image_outer[:1], "row", -1)
-    quarter = image_outer.shape[0] // 2
-
-    def column(at):
+        earlier = [projected]
+        if not part:
+            projected = after(projected, *pieces[1])
+        returned = in_pieces(exchanged(projected.reshape(places, windows, owned, width), "row"))
+        line = TILE_COLS // PIECE
+        if part:
+            above = shifted(after(images[0][-line:], projected), "row", 1)
+            below = shifted(after(images[0][:line], projected), "row", -1)
+            returned = after(returned, above, below)
+        images.append(returned)
+    outer_rows, middle_rows = images
+    half_way = outer_rows.shape[0] // 2
+
+    def column(first):
+        window, token = (0, 0) if first else (-1, -1)
+        start = 0 if first else line - 1
         return jnp.concatenate(
             [
-                above[:, at], image_outer[:quarter, at], image_middle[:, at],
-                image_outer[quarter:, at], below[:, at],
+                lines[start::line, window, token]
+                for lines in (
+                    above, outer_rows[:half_way], middle_rows, outer_rows[half_way:], below
+                )
             ],
             axis=0,
         )
 
-    left = shifted(column(-1), "col", 1)
-    right = shifted(column(0), "col", -1)
+    if cores == 2:
+        other = swapped(jnp.where(core == 0, column(False), column(True)), "col", 1)
+        left = jnp.where(core == 1, other, 0)
+        right = jnp.where(core == 0, other, 0)
+    else:
+        left, right = shifted(column(False), "col", 1), shifted(column(True), "col", -1)
     return convolve_twice(
-        image_outer, image_middle, above[0], below[0], left, right, keep,
+        outer_rows, middle_rows, above, below, left, right, keep,
         first_kernel, first_bias, second_kernel, second_bias,
     )
 

time: 187 us -> 153 us (0.82)
  starting transfers between devices: 80 us -> 34.1 us
  waiting for transfers between devices: 59.7 us -> 73.2 us
  Pallas kernels: 23.4 us -> 27.2 us
  local copies, waits for them, and re-layouts: 15 us -> 11.9 us
    ppermute x28 -> x11, starting transfers between devices: 69.5 us -> 12.4 us  [swapped(): lax.ppermute(value, axis, [(i, i ^ by) for i in range(lax.axis_size(axis))])]
    all_to_all x0 -> x3, starting transfers between devices: none -> 15.7 us  [exchanged(): return lax.all_to_all(value, axes, split_axis=0, concat_axis=0, tiled=True)]
    all_to_all x0 -> x3, waiting for transfers between devices: none -> 12.7 us  [exchanged(): return lax.all_to_all(value, axes, split_axis=0, concat_axis=0, tiled=True)]
    ppermute x4 -> x2, starting transfers between devices: 10.5 us -> 6.03 us  [shifted(): return lax.ppermute(value, axis, pairs)]
    another operation x8 -> x2, local copies, waits for them, and re-layouts: 5.88 us -> 1.44 us  [shards(): piece = jnp.stack([values_near[k, part], values_far[k, part]])]
    unnamed x26 -> x48, local copies, waits for them, and re-layouts: 4.81 us -> 8.34 us
    ppermute x4 -> x2, waiting for transfers between devices: 2.46 us -> 5.95 us  [shifted(): return lax.ppermute(value, axis, pairs)]
    concatenate x1 -> x0, other arithmetic: 3.48 us -> none  [shards(): ordered = jnp.concatenate([proj_weight, proj_weight], axis=0)]
  transfers between devices with their start and end apart: 32 -> 16, of which waited for: 12 -> 11; matrix products, arithmetic and copies ran while one was open for 8% -> 5% of each run, Pallas kernels for 6% -> 10%
where the time goes in v3:
time: 153 us; the launch traced here: 152 us
  waiting for transfers between devices  73.2 us (48%)
  starting transfers between devices  34.1 us (22%)
  Pallas kernels  27.2 us (18%)
  local copies, waits for them, and re-layouts  11.9 us (8%)
  other arithmetic  5.38 us (4%)
    ppermute x11, waiting for transfers between devices, swapped(): lax.ppermute(value, axis, [(i, i ^ by) for i in range(lax.axis_size(axis))])  54.6 us
    all_to_all x3, starting transfers between devices, exchanged(): return lax.all_to_all(value, axes, split_axis=0, concat_axis=0, tiled=True)  15.7 us
    all_to_all x3, waiting for transfers between devices, exchanged(): return lax.all_to_all(value, axes, split_axis=0, concat_axis=0, tiled=True)  12.7 us
    ppermute x11, starting transfers between devices, swapped(): lax.ppermute(value, axis, [(i, i ^ by) for i in range(lax.axis_size(axis))])  12.4 us
    pallas_call x1, Pallas kernels, convolve_twice(): pl.pallas_call(functools.partial(conv_kernel, rows, cols), out_shape=jax....  8.56 us
    unnamed x48, local copies, waits for them, and re-layouts  8.34 us
    ppermute x2, starting transfers between devices, shifted(): return lax.ppermute(value, axis, pairs)  6.03 us
    ppermute x2, waiting for transfers between devices, shifted(): return lax.ppermute(value, axis, pairs)  5.95 us
  transfers between devices with their start and end apart: 16, of which 11 were waited for; matrix products, arithmetic and copies ran while one was open for 5% of the time, Pallas kernels for 10%

profile of v3, /device:TPU:0, one launch (start us, length us, event | category | flops | bytes accessed | tf_op | source)
XLA Modules:
  0.0 152.3 jit_solution(7172367794870549162)
XLA Ops:
  0.0 3.3 %shard_map.109 = bf16[8,2,2,2,32,640]{5,4,3,2,1,0:T(8,128)(2,1)} custom-call(bf16[4,128,1280]{2,1,0:T(8,128)(2,1)} %bitcast.116, bf16[4,128,1280]{2,1,0:T(8,128)(2,1)} %bitcast.117), custom_call_target="tpu_custom_call" | custom-call | tf_op jit(solution)/shard_map/pallas_call | solution.py:132
  3.3 7.4 %all-to-all-start = ((bf16[16,2,2,32,640]{4,3,2,1,0:T(8,128)(2,1)}), bf16[16,2,2,32,640]{4,3,2,1,0:T(8,128)(2,1)S(1)}, u32[]{:S(2)}, u32[]{:S(2)}) async-start(bf16[16,2,2,32,640]{4,3,2,1,0:T(8,128)(2,1)} %bitcast.113), calls=%async_computation | async-start | bytes 5242880 | tf_op jit(solution)/shard_map/all_to_all | solution.py:427
  10.7 1.3 copy-done.2
  12.0 1.3 copy-done.3
  13.4 1.3 copy-done.4
  14.7 4.5 %shard_map.111 = bf16[2,4,128,640]{3,2,1,0:T(8,128)(2,1)S(1)} custom-call(bf16[4,128,1280]{2,1,0:T(8,128)(2,1)S(1)} %bitcast.104, bf16[4,128,1280]{2,1,0:T(8,128)(2,1)S(1)} %bitcast.105, bf16[4,128,1280]{2,1,0:T(8,128)(2,1)S(1)} %bitcast.106), custom_call_target="tpu_custom_call" | custom-call | tf_op jit(solution)/shard_map/pallas_call | solution.py:83
  19.2 1.0 constant_dynamic-slice_fusion
  20.2 0.4 collective-permute-start
  20.6 2.1 %collective-permute-done = bf16[4,128,640]{2,1,0:T(8,128)(2,1)} collective-permute-done((bf16[4,128,640]{2,1,0:T(8,128)(2,1)}, bf16[4,128,640]{2,1,0:T(8,128)(2,1)}, u32[]{:S(2)}, u32[]{:S(2)}) %collective-permute-start) | collective-permute-done | bytes 655392 | tf_op jit(solution)/shard_map/ppermute | solution.py:423
  22.7 1.0 fusion.8
  23.6 1.2 fusion.14
  24.9 0.1 maximum_bitcast_fusion
  24.9 0.1 maximum_bitcast_fusion.2
  25.0 0.2 pad_maximum_fusion
  25.2 0.1 dynamic-slice_bitcast_fusion.1
  25.4 2.0 %collective-permute-start.1 = (bf16[4,2,2,4,8,640]{5,4,3,2,1,0:T(8,128)(2,1)S(1)}, bf16[4,2,2,4,8,640]{5,4,3,2,1,0:T(8,128)(2,1)S(1)}, u32[]{:S(2)}, u32[]{:S(2)}) collective-permute-start(bf16[4,2,2,4,8,640]{5,4,3,2,1,0:T(8,128)(2,1)S(1)} %get-tuple-element.24), channel_id=1, source_target_pairs={{0,2},{2,0},{4,6},{6,4},{8,10},{10,8},{12,14},{14,12},{1,3},{3,1},... | collective-permute-start | bytes 1966088 | tf_op jit(solution)/shard_map/ppermute | solution.py:423
  27.3 0.7 slice_bitcast_fusion.1
  28.0 24.5 %collective-permute-done.1 = bf16[4,2,2,4,8,640]{5,4,3,2,1,0:T(8,128)(2,1)S(1)} collective-permute-done((bf16[4,2,2,4,8,640]{5,4,3,2,1,0:T(8,128)(2,1)S(1)}, bf16[4,2,2,4,8,640]{5,4,3,2,1,0:T(8,128)(2,1)S(1)}, u32[]{:S(2)}, u32[]{:S(2)}) %collective-permute-start.1) | collective-permute-done | bytes 655392 | tf_op jit(solution)/shard_map/ppermute | solution.py:423
  52.5 0.7 slice_bitcast_fusion
  53.3 0.7 pad_maximum_fusion.4
  53.9 3.4 %collective-permute-start.4 = (bf16[2,2,32,640]{3,2,1,0:T(8,128)(2,1)}, bf16[2,2,32,640]{3,2,1,0:T(8,128)(2,1)S(1)}, u32[]{:S(2)}, u32[]{:S(2)}) collective-permute-start(bf16[2,2,32,640]{3,2,1,0:T(8,128)(2,1)} %pad_maximum_fusion.4), channel_id=1, source_target_pairs={{0,12},{2,14},{4,8},{6,10},{8,4},{10,6},{12,0},{14,2},{1,13},{3,15... | collective-permute-start | bytes 491528 | tf_op jit(solution)/shard_map/ppermute | solution.py:423
  57.4 0.7 pad_maximum_fusion.3
  58.1 0.1 collective-permute-start.3
  58.2 0.7 pad_maximum_fusion.2
  58.9 0.8 collective-permute-start.2
  59.7 0.7 pad_maximum_fusion.8
  60.4 3.4 %collective-permute-start.8 = (bf16[2,2,32,640]{3,2,1,0:T(8,128)(2,1)}, bf16[2,2,32,640]{3,2,1,0:T(8,128)(2,1)S(1)}, u32[]{:S(2)}, u32[]{:S(2)}) collective-permute-start(bf16[2,2,32,640]{3,2,1,0:T(8,128)(2,1)} %pad_maximum_fusion.8), channel_id=1, source_target_pairs={{0,12},{2,14},{4,8},{6,10},{8,4},{10,6},{12,0},{14,2},{1,13},{3,15... | collective-permute-start | bytes 491528 | tf_op jit(solution)/shard_map/ppermute | solution.py:423
  63.8 3.8 %all-to-all-done = bf16[16,2,2,32,640]{4,3,2,1,0:T(8,128)(2,1)S(1)} async-done(((bf16[16,2,2,32,640]{4,3,2,1,0:T(8,128)(2,1)}), bf16[16,2,2,32,640]{4,3,2,1,0:T(8,128)(2,1)S(1)}, u32[]{:S(2)}, u32[]{:S(2)}) %all-to-all-start) | async-done | bytes 2621472 | tf_op jit(solution)/shard_map/all_to_all | solution.py:427
  67.6 2.5 %shard_map.110.weights = bf16[4,512,512]{2,1,0:T(8,128)(2,1)S(1)} custom-call(s32[1]{0:T(128)} %bitcast.core, bf16[8,2,2,2,32,640]{5,4,3,2,1,0:T(8,128)(2,1)S(1)} %bitcast.102), custom_call_target="tpu_custom_call" | custom-call | tf_op jit(solution)/shard_map/pallas_call | solution.py:183
  70.1 19.0 %collective-permute-done.3.refs_2_ = bf16[2,2,32,640]{3,2,1,0:T(8,128)(2,1)S(1)} collective-permute-done((bf16[2,2,32,640]{3,2,1,0:T(8,128)(2,1)}, bf16[2,2,32,640]{3,2,1,0:T(8,128)(2,1)S(1)}, u32[]{:S(2)}, u32[]{:S(2)}) %collective-permute-start.3) | collective-permute-done | bytes 163872 | tf_op jit(solution)/shard_map/ppermute | solution.py:423
  89.2 0.0 copy-start
  89.2 0.0 copy-start.13
  89.2 0.8 shard_map.112
  90.0 0.1 collective-permute-start.5
  90.1 0.1 collective-permute-start.7
  90.2 2.0 %collective-permute-start.6 = (bf16[2,2,32,640]{3,2,1,0:T(8,128)(2,1)S(1)}, bf16[2,2,32,640]{3,2,1,0:T(8,128)(2,1)S(1)}, u32[]{:S(2)}, u32[]{:S(2)}) collective-permute-start(bf16[2,2,32,640]{3,2,1,0:T(8,128)(2,1)S(1)} %pad_maximum_fusion.6), channel_id=1, source_target_pairs={{0,4},{2,6},{4,0},{6,2},{8,12},{10,14},{12,8},{14,10},{1,5},{3,7},... | collective-permute-start | bytes 491528 | tf_op jit(solution)/shard_map/ppermute | solution.py:423
  92.3 1.8 %shard_map.113 = bf16[256,1024]{1,0:T(8,128)(2,1)} custom-call(s32[1]{0:T(128)} %bitcast.core, bf16[256,640]{1,0:T(8,128)(2,1)S(1)} %get-tuple-element.14.near, bf16[256,640]{1,0:T(8,128)(2,1)S(1)} %collective-permute-done.5.far, bf16[1280,1024]{1,0:T(8,128)(2,1)S(1)} %copy-done, f32[1,1024]{1,0:T(1,128)S(1)} %bitcast.109), custom_call_target="tpu_custom_call" | custom-call | tf_op jit(solution)/shard_map/pallas_call | solution.py:244
  94.1 5.9 %collective-permute-done.7.refs_2_ = bf16[2,2,32,640]{3,2,1,0:T(8,128)(2,1)S(1)} collective-permute-done((bf16[2,2,32,640]{3,2,1,0:T(8,128)(2,1)S(1)}, bf16[2,2,32,640]{3,2,1,0:T(8,128)(2,1)S(1)}, u32[]{:S(2)}, u32[]{:S(2)}) %collective-permute-start.7) | collective-permute-done | bytes 163872 | tf_op jit(solution)/shard_map/ppermute | solution.py:423
  100.0 0.7 copy-done.9
  100.7 0.7 copy-done.11
  101.4 4.6 %all-to-all-start.1 = ((bf16[8,4,8,1024]{3,2,1,0:T(8,128)(2,1)}), bf16[8,4,8,1024]{3,2,1,0:T(8,128)(2,1)S(1)}, u32[]{:S(2)}, u32[]{:S(2)}) async-start(bf16[8,4,8,1024]{3,2,1,0:T(8,128)(2,1)} %bitcast.115), calls=%async_computation.1 | async-start | bytes 1048576 | tf_op jit(solution)/shard_map/all_to_all | solution.py:427
  106.0 2.5 %shard_map.114.weights = bf16[4,512,512]{2,1,0:T(8,128)(2,1)S(1)} custom-call(s32[1]{0:T(128)} %bitcast.core, bf16[8,2,2,2,32,640]{5,4,3,2,1,0:T(8,128)(2,1)S(1)} %bitcast.103), custom_call_target="tpu_custom_call" | custom-call | tf_op jit(solution)/shard_map/pallas_call | solution.py:183
  108.5 1.5 shard_map.115
  110.0 0.7 copy-done.7
  110.8 1.8 %collective-permute-done.9.far = bf16[256,640]{1,0:T(8,128)(2,1)S(1)} collective-permute-done((bf16[256,640]{1,0:T(8,128)(2,1)}, bf16[256,640]{1,0:T(8,128)(2,1)S(1)}, u32[]{:S(2)}, u32[]{:S(2)}) %collective-permute-start.9) | collective-permute-done | bytes 327712 | tf_op jit(solution)/shard_map/ppermute | solution.py:423
  112.6 1.0 copy-done.8
  113.6 1.8 %shard_map.116 = bf16[256,1024]{1,0:T(8,128)(2,1)} custom-call(s32[1]{0:T(128)} %bitcast.core, bf16[256,640]{1,0:T(8,128)(2,1)S(1)} %copy-done.8, bf16[256,640]{1,0:T(8,128)(2,1)S(1)} %collective-permute-done.9.far, bf16[1280,1024]{1,0:T(8,128)(2,1)S(1)} %copy-done.1, f32[1,1024]{1,0:T(1,128)S(1)} %bitcast.110), custom_call_target="tpu_custom_call" | custom-call | tf_op jit(solution)/shard_map/pallas_call | solution.py:244
  115.4 5.2 %all-to-all-done.1.outer = bf16[8,4,8,1024]{3,2,1,0:T(8,128)(2,1)S(1)} async-done(((bf16[8,4,8,1024]{3,2,1,0:T(8,128)(2,1)}), bf16[8,4,8,1024]{3,2,1,0:T(8,128)(2,1)S(1)}, u32[]{:S(2)}, u32[]{:S(2)}) %all-to-all-start.1) | async-done | bytes 524320 | tf_op jit(solution)/shard_map/all_to_all | solution.py:427
  120.6 3.6 %all-to-all-start.2 = ((bf16[8,4,8,1024]{3,2,1,0:T(8,128)(2,1)}), bf16[8,4,8,1024]{3,2,1,0:T(8,128)(2,1)S(1)}, u32[]{:S(2)}, u32[]{:S(2)}) async-start(bf16[8,4,8,1024]{3,2,1,0:T(8,128)(2,1)} %bitcast.114), calls=%async_computation.2 | async-start | bytes 1048576 | tf_op jit(solution)/shard_map/all_to_all | solution.py:427
  124.3 1.3 collective-permute-start.11
  125.6 4.7 %collective-permute-start.10 = (bf16[2,4,8,1024]{3,2,1,0:T(8,128)(2,1)S(1)}, bf16[2,4,8,1024]{3,2,1,0:T(8,128)(2,1)S(1)}, u32[]{:S(2)}, u32[]{:S(2)}) collective-permute-start(bf16[2,4,8,1024]{3,2,1,0:T(8,128)(2,1)S(1)} %get-tuple-element.20), channel_id=1, source_target_pairs={{0,2},{2,4},{4,6},{6,8},{8,10},{10,12},{12,14},{1,3},{3,5},{5,7},{... | collective-permute-start | bytes 393224 | tf_op jit(solution)/shard_map/ppermute | solution.py:419
  130.4 0.0 copy-start.5
  130.4 0.0 copy-start.14
  130.5 4.2 %collective-permute-done.11.below = bf16[2,4,8,1024]{3,2,1,0:T(8,128)(2,1)S(1)} collective-permute-done((bf16[2,4,8,1024]{3,2,1,0:T(8,128)(2,1)S(1)}, bf16[2,4,8,1024]{3,2,1,0:T(8,128)(2,1)S(1)}, u32[]{:S(2)}, u32[]{:S(2)}) %collective-permute-start.11) | collective-permute-done | bytes 131104 | tf_op jit(solution)/shard_map/ppermute | solution.py:419
  134.7 1.8 %collective-permute-done.10.above = bf16[2,4,8,1024]{3,2,1,0:T(8,128)(2,1)S(1)} collective-permute-done((bf16[2,4,8,1024]{3,2,1,0:T(8,128)(2,1)S(1)}, bf16[2,4,8,1024]{3,2,1,0:T(8,128)(2,1)S(1)}, u32[]{:S(2)}, u32[]{:S(2)}) %collective-permute-start.10) | collective-permute-done | bytes 131104 | tf_op jit(solution)/shard_map/ppermute | solution.py:419
  136.5 3.7 %all-to-all-done.2.middle = bf16[8,4,8,1024]{3,2,1,0:T(8,128)(2,1)S(1)} async-done(((bf16[8,4,8,1024]{3,2,1,0:T(8,128)(2,1)}), bf16[8,4,8,1024]{3,2,1,0:T(8,128)(2,1)S(1)}, u32[]{:S(2)}, u32[]{:S(2)}) %all-to-all-start.2) | async-done | bytes 524320 | tf_op jit(solution)/shard_map/all_to_all | solution.py:427
  140.2 0.3 copy.23
  140.6 0.2 concatenate.15
  140.7 0.2 concatenate.14
  140.9 0.1 collective-permute-start.12
  141.0 1.2 collective-permute-done.12
  142.2 0.2 broadcast_in_dim.27.keep
  142.5 1.3 copy-done.6
  143.8 8.6 %shard_map.117 = bf16[2048,256]{1,0:T(8,128)(2,1)} custom-call(bf16[8,4,8,1024]{3,2,1,0:T(8,128)(2,1)S(1)} %all-to-all-done.1.outer, bf16[8,4,8,1024]{3,2,1,0:T(8,128)(2,1)S(1)} %all-to-all-done.2.middle, bf16[2,4,8,1024]{3,2,1,0:T(8,128)(2,1)S(1)} %collective-permute-done.10.above, bf16[2,4,8,1024]{3,2,1,0:T(8,128)(2,1)S(1)} %collective-permute-done.11.below, ...), custom_call_target="tpu_custom_call" | custom-call | tf_op jit(solution)/shard_map/pallas_call | solution.py:376
  (57 shorter events, 0.4 us)
Async XLA Ops:
  3.3 64.3 %all-to-all-start = ((bf16[16,2,2,32,640]{4,3,2,1,0:T(8,128)(2,1)}), bf16[16,2,2,32,640]{4,3,2,1,0:T(8,128)(2,1)S(1)}, u32[]{:S(2)}, u32[]{:S(2)}) async-start(bf16[16,2,2,32,640]{4,3,2,1,0:T(8,128)(2,1)} %bitcast.113), calls=%async_computation | async-start | bytes 5242880 | tf_op jit(solution)/shard_map/all_to_all | solution.py:427
  10.7 1.3 copy-start.2
  12.0 1.3 copy-start.3
  13.4 1.3 copy-start.4
  20.2 2.5 %collective-permute-start = (bf16[4,128,640]{2,1,0:T(8,128)(2,1)}, bf16[4,128,640]{2,1,0:T(8,128)(2,1)}, u32[]{:S(2)}, u32[]{:S(2)}) collective-permute-start(bf16[4,128,640]{2,1,0:T(8,128)(2,1)} %get-tuple-element.34), channel_id=1, source_target_pairs={{0,1},{1,0},{2,3},{3,2},{4,5},{5,4},{6,7},{7,6},{8,9},{9,8},{10,11... | collective-permute-start | bytes 1966088 | tf_op jit(solution)/shard_map/ppermute | solution.py:423
  25.4 27.2 %collective-permute-start.1 = (bf16[4,2,2,4,8,640]{5,4,3,2,1,0:T(8,128)(2,1)S(1)}, bf16[4,2,2,4,8,640]{5,4,3,2,1,0:T(8,128)(2,1)S(1)}, u32[]{:S(2)}, u32[]{:S(2)}) collective-permute-start(bf16[4,2,2,4,8,640]{5,4,3,2,1,0:T(8,128)(2,1)S(1)} %get-tuple-element.24), channel_id=1, source_target_pairs={{0,2},{2,0},{4,6},{6,4},{8,10},{10,8},{12,14},{14,12},{1,3},{3,1},... | collective-permute-start | bytes 1966088 | tf_op jit(solution)/shard_map/ppermute | solution.py:423
  53.9 16.2 %collective-permute-start.4 = (bf16[2,2,32,640]{3,2,1,0:T(8,128)(2,1)}, bf16[2,2,32,640]{3,2,1,0:T(8,128)(2,1)S(1)}, u32[]{:S(2)}, u32[]{:S(2)}) collective-permute-start(bf16[2,2,32,640]{3,2,1,0:T(8,128)(2,1)} %pad_maximum_fusion.4), channel_id=1, source_target_pairs={{0,12},{2,14},{4,8},{6,10},{8,4},{10,6},{12,0},{14,2},{1,13},{3,15... | collective-permute-start | bytes 491528 | tf_op jit(solution)/shard_map/ppermute | solution.py:423
  58.1 31.1 %collective-permute-start.3 = (bf16[2,2,32,640]{3,2,1,0:T(8,128)(2,1)}, bf16[2,2,32,640]{3,2,1,0:T(8,128)(2,1)S(1)}, u32[]{:S(2)}, u32[]{:S(2)}) collective-permute-start(bf16[2,2,32,640]{3,2,1,0:T(8,128)(2,1)} %pad_maximum_fusion.3), channel_id=1, source_target_pairs={{0,8},{2,10},{4,12},{6,14},{8,0},{10,2},{12,4},{14,6},{1,9},{3,11}... | collective-permute-start | bytes 491528 | tf_op jit(solution)/shard_map/ppermute | solution.py:423
  58.9 30.3 %collective-permute-start.2 = (bf16[2,2,32,640]{3,2,1,0:T(8,128)(2,1)}, bf16[2,2,32,640]{3,2,1,0:T(8,128)(2,1)S(1)}, u32[]{:S(2)}, u32[]{:S(2)}) collective-permute-start(bf16[2,2,32,640]{3,2,1,0:T(8,128)(2,1)} %pad_maximum_fusion.2), channel_id=1, source_target_pairs={{0,4},{2,6},{4,0},{6,2},{8,12},{10,14},{12,8},{14,10},{1,5},{3,7},... | collective-permute-start | bytes 491528 | tf_op jit(solution)/shard_map/ppermute | solution.py:423
  60.4 33.7 %collective-permute-start.8 = (bf16[2,2,32,640]{3,2,1,0:T(8,128)(2,1)}, bf16[2,2,32,640]{3,2,1,0:T(8,128)(2,1)S(1)}, u32[]{:S(2)}, u32[]{:S(2)}) collective-permute-start(bf16[2,2,32,640]{3,2,1,0:T(8,128)(2,1)} %pad_maximum_fusion.8), channel_id=1, source_target_pairs={{0,12},{2,14},{4,8},{6,10},{8,4},{10,6},{12,0},{14,2},{1,13},{3,15... | collective-permute-start | bytes 491528 | tf_op jit(solution)/shard_map/ppermute | solution.py:423
  67.6 22.4 %copy-start.18 = (bf16[1,2,32,640]{3,2,1,0:T(8,128)(2,1)S(1)}, bf16[1,2,32,640]{3,2,1,0:T(8,128)(2,1)}, u32[]{:S(2)}) copy-start(bf16[1,2,32,640]{3,2,1,0:T(8,128)(2,1)} %get-tuple-element.36) | copy-start | bytes 245764
  67.6 22.4 %copy-start.21 = (bf16[1,2,32,640]{3,2,1,0:T(8,128)(2,1)S(1)}, bf16[1,2,32,640]{3,2,1,0:T(8,128)(2,1)}, u32[]{:S(2)}) copy-start(bf16[1,2,32,640]{3,2,1,0:T(8,128)(2,1)} %get-tuple-element.44) | copy-start | bytes 245764
  89.1 1.0 copy-start.17
  89.1 1.0 copy-start.20
  89.1 3.1 %copy-start.16 = (bf16[1,2,32,640]{3,2,1,0:T(8,128)(2,1)S(1)}, bf16[1,2,32,640]{3,2,1,0:T(8,128)(2,1)}, u32[]{:S(2)}) copy-start(bf16[1,2,32,640]{3,2,1,0:T(8,128)(2,1)} %get-tuple-element.38) | copy-start | bytes 245764
  89.1 3.1 %copy-start.19 = (bf16[1,2,32,640]{3,2,1,0:T(8,128)(2,1)S(1)}, bf16[1,2,32,640]{3,2,1,0:T(8,128)(2,1)}, u32[]{:S(2)}) copy-start(bf16[1,2,32,640]{3,2,1,0:T(8,128)(2,1)} %get-tuple-element.46) | copy-start | bytes 245764
  89.2 3.1 %copy-start = (bf16[1280,1024]{1,0:T(8,128)(2,1)S(1)}, bf16[1280,1024]{1,0:T(8,128)(2,1)}, u32[]{:S(2)}) copy-start(bf16[1280,1024]{1,0:T(8,128)(2,1)} %proj_weight.3) | copy-start | bytes 7864324
  89.2 3.1 %copy-start.13 = (f32[1024]{0:T(1024)S(1)}, f32[1024]{0:T(1024)}, u32[]{:S(2)}) copy-start(f32[1024]{0:T(1024)} %param.17) | copy-start | bytes 12292
  90.0 2.3 %collective-permute-start.5 = (bf16[256,640]{1,0:T(8,128)(2,1)S(1)}, bf16[256,640]{1,0:T(8,128)(2,1)S(1)}, u32[]{:S(2)}, u32[]{:S(2)}) collective-permute-start(bf16[256,640]{1,0:T(8,128)(2,1)S(1)} %get-tuple-element.15), channel_id=1, source_target_pairs={{0,1},{1,0},{2,3},{3,2},{4,5},{5,4},{6,7},{7,6},{8,9},{9,8},{10,11... | collective-permute-start | bytes 983048 | tf_op jit(solution)/shard_map/ppermute | solution.py:423
  90.1 9.9 %collective-permute-start.7 = (bf16[2,2,32,640]{3,2,1,0:T(8,128)(2,1)S(1)}, bf16[2,2,32,640]{3,2,1,0:T(8,128)(2,1)S(1)}, u32[]{:S(2)}, u32[]{:S(2)}) collective-permute-start(bf16[2,2,32,640]{3,2,1,0:T(8,128)(2,1)S(1)} %pad_maximum_fusion.7), channel_id=1, source_target_pairs={{0,8},{2,10},{4,12},{6,14},{8,0},{10,2},{12,4},{14,6},{1,9},{3,11}... | collective-permute-start | bytes 491528 | tf_op jit(solution)/shard_map/ppermute | solution.py:423
  90.2 10.5 %collective-permute-start.6 = (bf16[2,2,32,640]{3,2,1,0:T(8,128)(2,1)S(1)}, bf16[2,2,32,640]{3,2,1,0:T(8,128)(2,1)S(1)}, u32[]{:S(2)}, u32[]{:S(2)}) collective-permute-start(bf16[2,2,32,640]{3,2,1,0:T(8,128)(2,1)S(1)} %pad_maximum_fusion.6), channel_id=1, source_target_pairs={{0,4},{2,6},{4,0},{6,2},{8,12},{10,14},{12,8},{14,10},{1,5},{3,7},... | collective-permute-start | bytes 491528 | tf_op jit(solution)/shard_map/ppermute | solution.py:423
  100.0 0.7 copy-start.9
  100.7 0.7 copy-start.11
  101.4 19.3 %all-to-all-start.1 = ((bf16[8,4,8,1024]{3,2,1,0:T(8,128)(2,1)}), bf16[8,4,8,1024]{3,2,1,0:T(8,128)(2,1)S(1)}, u32[]{:S(2)}, u32[]{:S(2)}) async-start(bf16[8,4,8,1024]{3,2,1,0:T(8,128)(2,1)} %bitcast.115), calls=%async_computation.1 | async-start | bytes 1048576 | tf_op jit(solution)/shard_map/all_to_all | solution.py:427
  106.0 2.5 %copy-start.10 = (bf16[2,2,32,640]{3,2,1,0:T(8,128)(2,1)S(1)}, bf16[2,2,32,640]{3,2,1,0:T(8,128)(2,1)}, u32[]{:S(2)}) copy-start(bf16[2,2,32,640]{3,2,1,0:T(8,128)(2,1)} %copy-done.9) | copy-start | bytes 491524
  106.0 2.5 %copy-start.12 = (bf16[2,2,32,640]{3,2,1,0:T(8,128)(2,1)S(1)}, bf16[2,2,32,640]{3,2,1,0:T(8,128)(2,1)}, u32[]{:S(2)}) copy-start(bf16[2,2,32,640]{3,2,1,0:T(8,128)(2,1)} %copy-done.11) | copy-start | bytes 491524
  108.5 4.1 %copy-start.1 = (bf16[1280,1024]{1,0:T(8,128)(2,1)S(1)}, bf16[1280,1024]{1,0:T(8,128)(2,1)}, u32[]{:S(2)}) copy-start(bf16[1280,1024]{1,0:T(8,128)(2,1)} %proj_weight.3) | copy-start | bytes 7864324
  110.0 0.7 copy-start.7
  110.8 1.8 %collective-permute-start.9 = (bf16[256,640]{1,0:T(8,128)(2,1)}, bf16[256,640]{1,0:T(8,128)(2,1)S(1)}, u32[]{:S(2)}, u32[]{:S(2)}) collective-permute-start(bf16[256,640]{1,0:T(8,128)(2,1)} %get-tuple-element.19), channel_id=1, source_target_pairs={{0,1},{1,0},{2,3},{3,2},{4,5},{5,4},{6,7},{7,6},{8,9},{9,8},{10,11... | collective-permute-start | bytes 983048 | tf_op jit(solution)/shard_map/ppermute | solution.py:423
  112.6 1.0 copy-start.8
  120.6 19.6 %all-to-all-start.2 = ((bf16[8,4,8,1024]{3,2,1,0:T(8,128)(2,1)}), bf16[8,4,8,1024]{3,2,1,0:T(8,128)(2,1)S(1)}, u32[]{:S(2)}, u32[]{:S(2)}) async-start(bf16[8,4,8,1024]{3,2,1,0:T(8,128)(2,1)} %bitcast.114), calls=%async_computation.2 | async-start | bytes 1048576 | tf_op jit(solution)/shard_map/all_to_all | solution.py:427
  124.3 10.4 %collective-permute-start.11 = (bf16[2,4,8,1024]{3,2,1,0:T(8,128)(2,1)S(1)}, bf16[2,4,8,1024]{3,2,1,0:T(8,128)(2,1)S(1)}, u32[]{:S(2)}, u32[]{:S(2)}) collective-permute-start(bf16[2,4,8,1024]{3,2,1,0:T(8,128)(2,1)S(1)} %get-tuple-element.21), channel_id=1, source_target_pairs={{2,0},{4,2},{6,4},{8,6},{10,8},{12,10},{14,12},{3,1},{5,3},{7,5},{... | collective-permute-start | bytes 393224 | tf_op jit(solution)/shard_map/ppermute | solution.py:419
  125.6 10.9 %collective-permute-start.10 = (bf16[2,4,8,1024]{3,2,1,0:T(8,128)(2,1)S(1)}, bf16[2,4,8,1024]{3,2,1,0:T(8,128)(2,1)S(1)}, u32[]{:S(2)}, u32[]{:S(2)}) collective-permute-start(bf16[2,4,8,1024]{3,2,1,0:T(8,128)(2,1)S(1)} %get-tuple-element.20), channel_id=1, source_target_pairs={{0,2},{2,4},{4,6},{6,8},{8,10},{10,12},{12,14},{1,3},{3,5},{5,7},{... | collective-permute-start | bytes 393224 | tf_op jit(solution)/shard_map/ppermute | solution.py:419
  130.4 12.1 %copy-start.5 = (bf16[3,3,256,256]{3,2,1,0:T(8,128)(2,1)S(1)}, bf16[3,3,256,256]{3,2,1,0:T(8,128)(2,1)}, u32[]{:S(2)}) copy-start(bf16[3,3,256,256]{3,2,1,0:T(8,128)(2,1)} %param.18) | copy-start | bytes 3538948
  130.4 12.1 %copy-start.14 = (f32[256]{0:T(256)S(1)}, f32[256]{0:T(256)}, u32[]{:S(2)}) copy-start(f32[256]{0:T(256)} %param.19) | copy-start | bytes 3076
  130.4 12.1 %copy-start.15 = (f32[256]{0:T(256)S(1)}, f32[256]{0:T(256)}, u32[]{:S(2)}) copy-start(f32[256]{0:T(256)} %param.21) | copy-start | bytes 3076
  140.9 1.3 collective-permute-start.12
  142.5 1.3 copy-start.6

commit v4 on v3

--- a/solution.py
+++ b/solution.py
@@ -17,13 +17,13 @@
 EDGE = 16
 PIECE = 8
 SPAN = 2 * LANES
-VMEM_BYTES = 40 * 1024 * 1024
-
-
-def params(steps=0):
+VMEM_BYTES = 16 * 1024 * 1024
+
+
+def params(steps=0, size=VMEM_BYTES):
     return pltpu.CompilerParams(
         dimension_semantics=("arbitrary",) * steps if steps else None,
-        vmem_limit_bytes=VMEM_BYTES,
+        vmem_limit_bytes=size,
     )
 
 
@@ -101,28 +101,27 @@
     places, cores, parts, kinds, block, half = out.shape
     windows = query.shape[0]
     owned = block // windows
-    copies = [
+    arriving = [
         pltpu.make_async_copy(source, held.at[kind], arrived.at[kind])
         for kind, source in enumerate((query, key_rows))
     ]
-    for copy in copies:
+    for copy in arriving:
         copy.start()
-    for copy in copies:
-        copy.wait()
-    copies = []
-    for place in range(places):
-        for part in range(parts):
-            rows = pl.ds(token_of(place, part, owned, places), owned)
-            for kind in range(kinds):
+    leaving = []
+    for kind in range(kinds):
+        arriving[kind].wait()
+        for place in range(places):
+            for part in range(parts):
+                rows = pl.ds(token_of(place, part, owned, places), owned)
                 for window in range(windows):
                     for core in range(cores):
-                        packed[place, core, part, kind, pl.ds(window * owned, owned), :] = held[
+                        packed[kind, place, core, part, pl.ds(window * owned, owned), :] = held[
                             kind, window, rows, core * half : (core + 1) * half
                         ]
-        copy = pltpu.make_async_copy(packed.at[place], out.at[place], left.at[place])
+        copy = pltpu.make_async_copy(packed.at[kind], out.at[:, :, :, kind], left.at[kind])
         copy.start()
-        copies.append(copy)
-    for copy in copies:
+        leaving.append(copy)
+    for copy in leaving:
         copy.wait()
 
 
@@ -136,9 +135,9 @@
         out_shape=pltpu.HBM(result, query.dtype),
         scratch_shapes=[
             pltpu.VMEM((2,) + query.shape, query.dtype),
-            pltpu.VMEM(result, query.dtype),
+            pltpu.VMEM((2,) + result[:3] + result[4:], query.dtype),
             pltpu.SemaphoreType.DMA((2,)),
-            pltpu.SemaphoreType.DMA((places,)),
+            pltpu.SemaphoreType.DMA((2,)),
         ],
         compiler_params=params(),
     )(
@@ -147,9 +146,9 @@
     )
 
 
-def weights_kernel(tokens, core, pair, out):
+def weights_kernel(tokens, core, pair, *outs):
     places, cores, _, _, block, _ = pair.shape
-    head = pl.program_id(0)
+    head = pl.program_id(1)
     start = head * HEAD_DIM // LANES * LANES
     lanes = pl.ds(pl.multiple_of(start, LANES), SPAN)
     lane = lax.broadcasted_iota(jnp.int32, (1, SPAN), 1) + start
@@ -173,41 +172,64 @@
     rows = scores.shape[0]
     token_row = lax.broadcasted_iota(jnp.int32, (rows, 1), 0) % tokens
     token_col = lax.broadcasted_iota(jnp.int32, (1, rows), 1) % tokens
-    out[0] = softmax_rows(jnp.where(token_row == token_col, scores, -jnp.inf))
-
-
-def index_weights(core, pair, part, tokens):
-    places, cores, _, kinds, block, features = pair.shape
+    found = softmax_rows(jnp.where(token_row == token_col, scores, -jnp.inf))
+    for part, out in enumerate(outs):
+
+        @pl.when(pl.program_id(0) == part)
+        def _(out=out):
+            out[0] = found
+
+
+def index_weights(core, pair, tokens):
+    places, cores, parts, kinds, block, features = pair.shape
     heads = features // HEAD_DIM
     rows = places * cores * block
     return pl.pallas_call(
         functools.partial(weights_kernel, tokens),
-        grid=(heads,),
+        grid=(parts, heads),
         in_specs=[
             pl.BlockSpec(memory_space=pltpu.SMEM),
-            pl.BlockSpec((places, cores, 1, kinds, block, features), lambda h: (0, 0, part, 0, 0, 0)),
+            pl.BlockSpec((places, cores, 1, kinds, block, features), lambda p, h: (0, 0, p, 0, 0, 0)),
         ],
-        out_specs=pl.BlockSpec((1, rows, rows), lambda h: (h, 0, 0)),
-        out_shape=jax.ShapeDtypeStruct((heads, rows, rows), jnp.bfloat16),
-        compiler_params=params(1),
+        out_specs=[
+            pl.BlockSpec(
+                (1, rows, rows),
+                lambda p, h, part=part: (jnp.where(p < part, 0, jnp.where(p == part, h, heads - 1)), 0, 0),
+            )
+            for part in range(parts)
+        ],
+        out_shape=[pltpu.HBM((heads, rows, rows), jnp.bfloat16)] * parts,
+        compiler_params=params(2),
     )(core.reshape(1), pair)
 
 
 def mix_kernel(place, weights, *refs):
-    pieces, (near, far, value) = refs[:-3], refs[-3:]
-    inner, cores, rows, features = pieces[0].shape
+    pieces, (near, far, value, held, held_weights, arrived) = refs[:-6], refs[-6:]
+    each, cores, rows, features = pieces[0].shape
     half = value.shape[0] // cores
-    for k, piece in enumerate(pieces):
-        for j in range(inner):
-            at = pl.multiple_of((place[0] ^ (k * inner + j)) * rows, rows)
+    heads = features // HEAD_DIM
+    copies = [
+        pltpu.make_async_copy(piece, held.at[k], arrived.at[k]) for k, piece in enumerate(pieces)
+    ]
+    copies += [
+        pltpu.make_async_copy(weights.at[head], held_weights.at[head], arrived.at[len(pieces) + head])
+        for head in range(heads)
+    ]
+    for copy in copies:
+        copy.start()
+    for k in range(len(pieces)):
+        copies[k].wait()
+        for j in range(each):
+            at = pl.multiple_of((place[0] ^ (k * each + j)) * rows, rows)
             for core in range(cores):
-                value[pl.ds(core * half + at, rows), :] = piece[j, core].astype(value.dtype)
+                value[pl.ds(core * half + at, rows), :] = held[k, j, core].astype(value.dtype)
     mixed = []
-    for head in range(features // HEAD_DIM):
+    for head in range(heads):
+        copies[len(pieces) + head].wait()
         lanes = slice(head_start(head), head_start(head) + SPAN)
         mixed.append(
             jnp.dot(
-                weights[head], value[:, lanes].astype(jnp.bfloat16),
+                held_weights[head], value[:, lanes].astype(jnp.bfloat16),
                 preferred_element_type=jnp.float32,
             )
         )
@@ -217,38 +239,101 @@
 
 
 def index_mix(place, weights, pieces):
-    rows, features = weights.shape[1], pieces[0].shape[-1]
-    result = jax.ShapeDtypeStruct((rows // 2, features), jnp.bfloat16)
+    heads, rows, _ = weights.shape
+    features = pieces[0].shape[-1]
+    result = pltpu.VMEM((rows // 2, features), jnp.bfloat16)
     held = jnp.float32 if pieces[0].shape[2] % EDGE else jnp.bfloat16
+    far = pl.BlockSpec(memory_space=pltpu.HBM)
     return pl.pallas_call(
         mix_kernel,
-        in_specs=[pl.BlockSpec(memory_space=pltpu.SMEM)]
-        + [pl.BlockSpec(memory_space=pltpu.VMEM)] * (1 + len(pieces)),
+        in_specs=[pl.BlockSpec(memory_space=pltpu.SMEM)] + [far] * (1 + len(pieces)),
         out_specs=[pl.BlockSpec(memory_space=pltpu.VMEM)] * 2,
         out_shape=[result, result],
-        scratch_shapes=[pltpu.VMEM((rows, features), held)],
+        scratch_shapes=[
+            pltpu.VMEM((rows, features), held),
+            pltpu.VMEM((len(pieces),) + pieces[0].shape, jnp.bfloat16),
+            pltpu.VMEM(weights.shape, jnp.bfloat16),
+            pltpu.SemaphoreType.DMA((len(pieces) + heads,)),
+        ],
         compiler_params=params(),
-    )(place.reshape(1), weights, *pieces)
-
-
-def project_kernel(core, near, far, proj_weight, proj_bias, out):
+    )(
+        place.reshape(1),
+        *[pltpu.with_memory_space_constraint(value, pltpu.HBM) for value in [weights] + pieces],
+    )
+
+
+def project_kernel(places, inner, scalars, near, far, proj_weight, proj_bias, *refs):
+    core, twist = scalars[0], scalars[1]
     half = near.shape[1]
     total = proj_bias[...]
-    for held, place in ((near, core[0]), (far, 1 - core[0])):
+    for held, place in ((near, core), (far, 1 - core)):
         rows = pl.ds(pl.multiple_of(place * half, half), half)
         total = total + jnp.dot(held[...], proj_weight[rows, :], preferred_element_type=jnp.float32)
-    out[...] = total.astype(jnp.bfloat16)
-
-
-def project(near, far, proj_weight, proj_bias, core):
+    total = total.astype(jnp.bfloat16)
+    if len(refs) == 1:
+        refs[0][...] = total
+        return
+    *outs, turned = refs
+    block = total.shape[0] // places
+    for place in range(places):
+        turned[place] = total[place * block : (place + 1) * block]
+    for k in range(places):
+        outs[k % inner][k // inner] = turned[twist ^ k]
+
+
+def project(near, far, proj_weight, proj_bias, core, row, places, inner):
+    rows, width = near.shape[0], proj_weight.shape[1]
+    block = rows // places
+    shapes = [pltpu.HBM((rows, width), jnp.bfloat16)]
+    if inner:
+        shapes = [jax.ShapeDtypeStruct((places // inner, block, width), jnp.bfloat16)] * inner
     return pl.pallas_call(
-        project_kernel,
+        functools.partial(project_kernel, places, inner),
         in_specs=[pl.BlockSpec(memory_space=pltpu.SMEM)]
         + [pl.BlockSpec(memory_space=pltpu.VMEM)] * 4,
+        out_specs=[pl.BlockSpec(memory_space=pltpu.VMEM)] * len(shapes),
+        out_shape=shapes,
+        scratch_shapes=[pltpu.VMEM((places, block, width), jnp.bfloat16)] if inner else [],
+        compiler_params=params(),
+    )(jnp.stack([core, row]), near, far, proj_weight, proj_bias.reshape(1, -1))
+
+
+def gate_kernel(*refs):
+    del refs
+
+
+def gated(value, earlier):
+    anywhere = pl.BlockSpec(memory_space=pl.ANY)
+    return pl.pallas_call(
+        gate_kernel,
+        in_specs=[anywhere] * (1 + len(earlier)),
+        out_specs=anywhere,
+        out_shape=pltpu.HBM(value.shape, value.dtype),
+        input_output_aliases={0: 0},
+    )(value, *earlier)
+
+
+def column_kernel(core, *refs):
+    *lines, out = refs
+    at = 0
+    for ref in lines:
+        for place in range(ref.shape[0]):
+            first = ref[place, 0].astype(jnp.float32)[:1]
+            last = ref[place, ref.shape[1] - 1].astype(jnp.float32)[ref.shape[2] - 1 :]
+            out[at : at + 1, :] = jnp.where(core[0] == 0, last, first)
+            at += 1
+
+
+def next_column(core, lines):
+    total = sum(value.shape[0] for value in lines)
+    return pl.pallas_call(
+        column_kernel,
+        in_specs=[pl.BlockSpec(memory_space=pltpu.SMEM)]
+        + [pl.BlockSpec(memory_space=pltpu.VMEM)] * len(lines),
         out_specs=pl.BlockSpec(memory_space=pltpu.VMEM),
-        out_shape=pltpu.HBM((near.shape[0], proj_weight.shape[1]), jnp.bfloat16),
+        out_shape=jax.ShapeDtypeStruct((total, lines[0].shape[-1]), jnp.float32),
         compiler_params=params(),
-    )(core.reshape(1), near, far, proj_weight, proj_bias.reshape(1, -1))
+    )(core.reshape(1), *lines)
 
 
 def line_of(line, rows):
@@ -261,30 +346,57 @@
 
 
 def conv_kernel(
-    rows, cols, outer, middle, above, below, left, right, keep,
-    first_kernel, first_bias, second_kernel, second_bias, out,
-    taken, even, odd, acted, woven,
+    rows, cols, count, scalars, *refs,
 ):
+    core, twist = scalars[0], scalars[1]
+    middles, refs = refs[:count], refs[count:]
+    (
+        outer, above, below, side_outer, side_middle, keep,
+        first_kernel, first_bias, second_kernel, second_bias, out,
+        taken, even, odd, acted, woven, middle, second_held, fetched,
+    ) = refs
+    fetches = [
+        pltpu.make_async_copy(second_kernel, second_held, fetched.at[0]),
+    ]
+    for fetch in fetches:
+        fetch.start()
     pitch = cols + EDGE
     depth = CHANNELS
     place = lax.broadcasted_iota(jnp.int32, (EDGE, 1), 0)
     half = 2 * depth
+    _, windows, piece, _ = outer.shape
+    per = TILE_COLS // piece
+    if count > 1:
+        each = middle.shape[0] // count
+        for k in range(count):
+            for j in range(each):
+                middle[twist ^ (k * each + j)] = middles[k][j]
+    else:
+        middle[...] = middles[0][...]
+
+    def side(token, lanes, first):
+        within = 0 if first else per - 1
+        if token == 0 or token == rows + 1:
+            edge, at = side_outer, (0 if token == 0 else rows // 2 + 1)
+        else:
+            part, at = line_of(token - 1, rows)
+            edge, at = (side_middle, at) if part else (side_outer, at + 1)
+        at = at * per + within
+        if edge is side_middle:
+            found = edge[pl.ds(at ^ twist, 1), lanes]
+        else:
+            found = edge[at : at + 1, lanes]
+        return jnp.where(core == (0 if first else 1), found, 0.0)
 
     def gap_of(row):
         block = jnp.zeros((EDGE, half), jnp.float32)
         if row >= 1:
             token, sub = (row - 1) // 2, (row - 1) % 2
-            block = jnp.where(
-                place == 0,
-                right[token : token + 1, sub * half : (sub + 1) * half].astype(jnp.float32),
-                block,
-            )
+            block = jnp.where(place == 0, side(token, slice(sub * half, (sub + 1) * half), True), block)
         if row < 2 * (rows + 2):
             token, sub = row // 2, row % 2
             block = jnp.where(
-                place == EDGE - 1,
-                left[token : token + 1, sub * half : (sub + 1) * half].astype(jnp.float32),
-                block,
+                place == EDGE - 1, side(token, slice(sub * half, (sub + 1) * half), False), block
             )
         return block
 
@@ -297,8 +409,6 @@
         else:
             part, at = line_of(i - 1, rows)
             source = (outer, middle)[part]
-        _, windows, piece, _ = source.shape
-        per = TILE_COLS // piece
         body = jnp.concatenate(
             [
                 source[at * per + across, window].astype(jnp.float32)
@@ -328,24 +438,25 @@
     even[EDGE + total :] = jnp.zeros((EDGE, depth), jnp.float32)
     odd[EDGE + total :] = jnp.zeros((EDGE, depth), jnp.float32)
 
-    def taps(source, kernel, at, size, q):
+    def taps(source, kernel, starts, size, q):
         found = None
         for r in range(3):
-            part = jnp.dot(
-                source[pl.ds(at + r * pitch, size), q * depth : (q + 3) * depth], kernel[r],
-                preferred_element_type=jnp.float32,
-            )
+            cells = [
+                source[at + r * pitch : at + r * pitch + size, q * depth : (q + 3) * depth]
+                for at in starts
+            ]
+            cells = cells[0] if len(cells) == 1 else jnp.concatenate(cells, axis=0)
+            part = jnp.dot(cells, kernel[r], preferred_element_type=jnp.float32)
             found = part if found is None else found + part
         return found
 
-    pieces = 3
-    step = -(-total // pieces // EDGE) * EDGE
+    step = -(-total // 6 // EDGE) * EDGE
     for at in range(0, total, step):
         size = min(step, total - at)
         kept = keep[at : at + size, :] > 0.0
         kept = jnp.concatenate([kept] * (depth // LANES), axis=1)
         for q, held in ((0, even), (1, odd)):
-            value = taps(taken, first_kernel, at, size, q) + first_bias[...]
+            value = taps(taken, first_kernel, [at], size, q) + first_bias[...]
             value = jax.nn.gelu(value)
             held[EDGE + at : EDGE + at + size] = jnp.where(kept, value, 0.0)
     acted[:, depth : 2 * depth] = even[EDGE : EDGE + total].astype(jnp.bfloat16)
@@ -353,43 +464,55 @@
     acted[:, 0:depth] = odd[EDGE - 1 : EDGE - 1 + total].astype(jnp.bfloat16)
     acted[:, 3 * depth :] = even[EDGE + 1 : EDGE + 1 + total].astype(jnp.bfloat16)
 
-    group = max(lines // 4, 1)
+    fetches[0].wait()
+    group = max(lines // 8, 1)
     for at in range(0, lines, group):
-        size = group * pitch - EDGE
         for q in range(2):
-            value = taps(acted, second_kernel, EDGE + at * pitch, size, q) + second_bias[...]
+            starts = [EDGE + (at + y) * pitch for y in range(group)]
+            value = taps(acted, second_held, starts, cols, q) + second_bias[...]
             for y in range(group):
                 for lane in range(depth // LANES):
                     woven[lane, pl.ds((at + y) * 2 * cols + q, cols, stride=2), :] = value[
-                        y * pitch : y * pitch + cols, lane * LANES : (lane + 1) * LANES
+                        y * cols : (y + 1) * cols, lane * LANES : (lane + 1) * LANES
                     ]
     for lane in range(depth // LANES):
         out[:, lane * LANES : (lane + 1) * LANES] = woven[lane].astype(jnp.bfloat16)
 
 
-def convolve_twice(outer, middle, above, below, left, right, keep, first_kernel, first_bias, second_kernel, second_bias):
-    pieces, windows, piece, _ = outer.shape
-    rows, cols = 2 * pieces * piece // TILE_COLS, windows * TILE_COLS
+def convolve_twice(
+    scalars, middles, outer, above, below, side_outer, side_middle, keep,
+    first_kernel, first_bias, second_kernel, second_bias,
+):
+    places, windows, piece, width = outer.shape
+    rows, cols = 2 * places * piece // TILE_COLS, windows * TILE_COLS
     pitch = cols + EDGE
     total = (2 * rows + 2) * pitch + EDGE
     depth = CHANNELS
+    near = pl.BlockSpec(memory_space=pltpu.VMEM)
+    far = pl.BlockSpec(memory_space=pltpu.HBM)
+    kernels = [kernel.reshape(3, 3 * depth, depth) for kernel in (first_kernel, second_kernel)]
+    kernels[1] = pltpu.with_memory_space_constraint(kernels[1], pltpu.HBM)
     found = pl.pallas_call(
-        functools.partial(conv_kernel, rows, cols),
+        functools.partial(conv_kernel, rows, cols, len(middles)),
         out_shape=jax.ShapeDtypeStruct((4 * rows * cols, depth), jnp.bfloat16),
-        in_specs=[pl.BlockSpec(memory_space=pltpu.VMEM)] * 11,
-        out_specs=pl.BlockSpec(memory_space=pltpu.VMEM),
+        in_specs=[pl.BlockSpec(memory_space=pltpu.SMEM)]
+        + [near] * (len(middles) + 6)
+        + [near, near, far, near],
+        out_specs=near,
         scratch_shapes=[
             pltpu.VMEM(((2 * rows + 4) * pitch + EDGE, 4 * depth), jnp.bfloat16),
             pltpu.VMEM((total + 2 * EDGE, depth), jnp.float32),
             pltpu.VMEM((total + 2 * EDGE, depth), jnp.float32),
             pltpu.VMEM((total, 4 * depth), jnp.bfloat16),
             pltpu.VMEM((depth // LANES, 4 * rows * cols, LANES), jnp.float32),
+            pltpu.VMEM(outer.shape, jnp.bfloat16),
+            pltpu.VMEM((3, 3 * depth, depth), jnp.bfloat16),
+            pltpu.SemaphoreType.DMA((1,)),
         ],
-        compiler_params=params(),
+        compiler_params=params(size=2 * VMEM_BYTES),
     )(
-        outer, middle, above, below, left, right, keep,
-        first_kernel.reshape(3, 3 * depth, depth), first_bias.reshape(1, depth),
-        second_kernel.reshape(3, 3 * depth, depth), second_bias.reshape(1, depth),
+        scalars, *middles, outer, above, below, side_outer, side_middle, keep,
+        kernels[0], first_bias.reshape(1, depth), kernels[1], second_bias.reshape(1, depth),
     )
     return found.reshape(2 * rows, 2 * cols, depth)
 
@@ -441,7 +564,8 @@
 
 
 def after(value, *earlier):
-    return lax.optimization_barrier((value,) + earlier)[0]
+    corners = tuple(array[(0,) * (array.ndim - 2)][:PIECE, :LANES] for array in earlier)
+    return lax.optimization_barrier((value,) + corners)[0]
 
 
 def shards(
@@ -486,11 +610,6 @@
         ]
     )
     values_near, values_far = picked(blocks, y, 4), swapped(picked(blocks, 1 - y, 4), "row", 1)
-    weights = [index_weights(core, pair, part, owned) for part in range(2)]
-    keep = kept_rows(rows_dev * TILE_ROWS, cols_dev * TILE_COLS)
-
-    images = []
-    earlier = []
     pieces = []
     for part in range(2):
         pieces.append([])
@@ -498,44 +617,37 @@
             piece = jnp.stack([values_near[k, part], values_far[k, part]])
             piece = piece.reshape(inner, cores, windows * owned, half)
             pieces[part].append(swapped(piece, "row", k * inner) if k else piece)
-    for part in range(2):
-        mixed_near, mixed_far = index_mix(row, after(weights[part], *earlier), pieces[part])
-        projected = project(mixed_near, swapped(mixed_far, "col", 1), proj_weight, proj_bias, core)
-        width = projected.shape[-1]
-        earlier = [projected]
-        if not part:
-            projected = after(projected, *pieces[1])
-        returned = in_pieces(exchanged(projected.reshape(places, windows, owned, width), "row"))
-        line = TILE_COLS // PIECE
-        if part:
-            above = shifted(after(images[0][-line:], projected), "row", 1)
-            below = shifted(after(images[0][:line], projected), "row", -1)
-            returned = after(returned, above, below)
-        images.append(returned)
-    outer_rows, middle_rows = images
-    half_way = outer_rows.shape[0] // 2
-
-    def column(first):
-        window, token = (0, 0) if first else (-1, -1)
-        start = 0 if first else line - 1
-        return jnp.concatenate(
-            [
-                lines[start::line, window, token]
-                for lines in (
-                    above, outer_rows[:half_way], middle_rows, outer_rows[half_way:], below
-                )
-            ],
-            axis=0,
+    weights = index_weights(core, pair, owned)
+    keep = kept_rows(rows_dev * TILE_ROWS, cols_dev * TILE_COLS)
+
+    images = []
+    earlier = []
+    line = TILE_COLS // PIECE
+
+    def projected_of(part, apart):
+        near, far = index_mix(row, weights[part], pieces[part])
+        return project(
+            near, swapped(far, "col", 1), proj_weight, proj_bias, core, row, places, apart
         )
 
-    if cores == 2:
-        other = swapped(jnp.where(core == 0, column(False), column(True)), "col", 1)
-        left = jnp.where(core == 1, other, 0)
-        right = jnp.where(core == 0, other, 0)
+    projected = gated(projected_of(0, 0)[0], pieces[1])
+    outer_rows = in_pieces(exchanged(projected.reshape(places, windows, owned, -1), "row"))
+    above = shifted(outer_rows[-line:], "row", 1)
+    below = shifted(outer_rows[:line], "row", -1)
+    side_outer = swapped(next_column(core, [above, outer_rows, below]), "col", 1)
+    if owned == PIECE:
+        middles = [
+            (swapped(block, "row", k) if k else block).reshape(1, windows, owned, -1)
+            for k, block in enumerate(projected_of(1, places))
+        ]
+        twist = row
     else:
-        left, right = shifted(column(False), "col", 1), shifted(column(True), "col", -1)
+        projected = projected_of(1, 0)[0].reshape(places, windows, owned, -1)
+        middles = [in_pieces(exchanged(projected, "row"))]
+        twist = jnp.zeros_like(row)
+    side_middle = swapped(next_column(core, middles), "col", 1)
     return convolve_twice(
-        outer_rows, middle_rows, above, below, left, right, keep,
+        jnp.stack([core, twist]), middles, outer_rows, above, below, side_outer, side_middle, keep,
         first_kernel, first_bias, second_kernel, second_bias,
     )
 

time: 153 us -> 149 us (0.974)
  waiting for transfers between devices: 73.2 us -> 54.4 us
  starting transfers between devices: 34.1 us -> 44.9 us
  Pallas kernels: 27.2 us -> 34.2 us
  local copies, waits for them, and re-layouts: 11.9 us -> 6.76 us
  other arithmetic: 5.38 us -> 7.45 us
    ppermute x11 -> x19, starting transfers between devices: 12.4 us -> 25.1 us  [swapped(): lax.ppermute(value, axis, [(i, i ^ by) for i in range(lax.axis_size(axis))])]
    all_to_all x3 -> x2, waiting for transfers between devices: 12.7 us -> 1.55 us  [exchanged(): return lax.all_to_all(value, axes, split_axis=0, concat_axis=0, tiled=True)]
    ppermute x2, waiting for transfers between devices: 5.95 us -> 0.01 us  [shifted(): return lax.ppermute(value, axis, pairs)]
    pallas_call x2, Pallas kernels: 2.28 us -> 6.44 us  [index_mix(): pl.pallas_call(mix_kernel, in_specs=[pl.BlockSpec(memory_space=pltpu.SMEM...]
    unnamed x48 -> x24, local copies, waits for them, and re-layouts: 8.34 us -> 4.65 us
    pallas_call x5 -> x7, Pallas kernels: 17.1 us -> 20.3 us  [the longest x1 8.75 us: convolve_twice(): pl.pallas_call(functools.partial(conv_kernel, rows, cols, len(middles)),...]
    another operation x8, other arithmetic: 2.81 us -> 4.83 us  [shards(): piece = jnp.stack([values_near[k, part], values_far[k, part]])]
    ppermute x11 -> x19, waiting for transfers between devices: 54.6 us -> 52.9 us  [swapped(): lax.ppermute(value, axis, [(i, i ^ by) for i in range(lax.axis_size(axis))])]
  transfers between devices with their start and end apart: 16 -> 23, of which waited for: 11 -> 12; matrix products, arithmetic and copies ran while one was open for 5% -> 6% of each run, Pallas kernels for 10% -> 15%
where the time goes in v4:
time: 149 us; the launch traced here: 148 us
  waiting for transfers between devices  54.4 us (37%)
  starting transfers between devices  44.9 us (30%)
  Pallas kernels  34.2 us (23%)
  other arithmetic  7.45 us (5%)
  local copies, waits for them, and re-layouts  6.76 us (5%)
    ppermute x19, waiting for transfers between devices, swapped(): lax.ppermute(value, axis, [(i, i ^ by) for i in range(lax.axis_size(axis))])  52.9 us
    ppermute x19, starting transfers between devices, swapped(): lax.ppermute(value, axis, [(i, i ^ by) for i in range(lax.axis_size(axis))])  25.1 us
    all_to_all x2, starting transfers between devices, exchanged(): return lax.all_to_all(value, axes, split_axis=0, concat_axis=0, tiled=True)  15.1 us
    pallas_call x1, Pallas kernels, convolve_twice(): pl.pallas_call(functools.partial(conv_kernel, rows, cols, len(middles)),...  8.75 us
    pallas_call x1, Pallas kernels, index_weights(): pl.pallas_call(functools.partial(weights_kernel, tokens), grid=(parts, he...  6.81 us
    pallas_call x2, Pallas kernels, index_mix(): pl.pallas_call(mix_kernel, in_specs=[pl.BlockSpec(memory_space=pltpu.SMEM...  6.44 us
    another operation x8, other arithmetic, shards(): piece = jnp.stack([values_near[k, part], values_far[k, part]])  4.83 us
    unnamed x24, local copies, waits for them, and re-layouts  4.65 us
  transfers between devices with their start and end apart: 23, of which 12 were waited for; matrix products, arithmetic and copies ran while one was open for 6% of the time, Pallas kernels for 15%

profile of v4, /device:TPU:0, one launch (start us, length us, event | category | flops | bytes accessed | tf_op | source)
XLA Modules:
  0.0 148.2 jit_solution(6286054020762944688)
XLA Ops:
  0.0 3.0 %shard_map.109 = bf16[8,2,2,2,32,640]{5,4,3,2,1,0:T(8,128)(2,1)} custom-call(bf16[4,128,1280]{2,1,0:T(8,128)(2,1)} %bitcast.114, bf16[4,128,1280]{2,1,0:T(8,128)(2,1)} %bitcast.115), custom_call_target="tpu_custom_call" | custom-call | tf_op jit(solution)/shard_map/pallas_call | solution.py:131
  3.0 7.4 %all-to-all-start = ((bf16[16,2,2,32,640]{4,3,2,1,0:T(8,128)(2,1)}), bf16[16,2,2,32,640]{4,3,2,1,0:T(8,128)(2,1)S(1)}, u32[]{:S(2)}, u32[]{:S(2)}) async-start(bf16[16,2,2,32,640]{4,3,2,1,0:T(8,128)(2,1)} %bitcast.112), calls=%async_computation | async-start | bytes 5242880 | tf_op jit(solution)/shard_map/all_to_all | solution.py:550
  10.4 1.3 copy-done.1
  11.7 1.3 copy-done.2
  13.0 1.3 copy-done.3
  14.3 4.5 %shard_map.111 = bf16[2,4,128,640]{3,2,1,0:T(8,128)(2,1)S(1)} custom-call(bf16[4,128,1280]{2,1,0:T(8,128)(2,1)S(1)} %bitcast.88, bf16[4,128,1280]{2,1,0:T(8,128)(2,1)S(1)} %bitcast.89, bf16[4,128,1280]{2,1,0:T(8,128)(2,1)S(1)} %bitcast.90), custom_call_target="tpu_custom_call" | custom-call | tf_op jit(solution)/shard_map/pallas_call | solution.py:83
  18.9 1.0 constant_dynamic-slice_fusion
  19.9 0.4 collective-permute-start
  20.3 2.1 %collective-permute-done = bf16[4,128,640]{2,1,0:T(8,128)(2,1)} collective-permute-done((bf16[4,128,640]{2,1,0:T(8,128)(2,1)}, bf16[4,128,640]{2,1,0:T(8,128)(2,1)}, u32[]{:S(2)}, u32[]{:S(2)}) %collective-permute-start) | collective-permute-done | bytes 655392 | tf_op jit(solution)/shard_map/ppermute | solution.py:546
  22.3 1.0 fusion.8
  23.3 1.2 fusion.14
  24.5 0.1 maximum_bitcast_fusion.2
  24.6 0.1 maximum_bitcast_fusion
  24.7 0.2 pad_maximum_fusion
  24.9 0.1 dynamic-slice_bitcast_fusion.1
  25.0 2.0 %collective-permute-start.1 = (bf16[4,2,2,4,8,640]{5,4,3,2,1,0:T(8,128)(2,1)S(1)}, bf16[4,2,2,4,8,640]{5,4,3,2,1,0:T(8,128)(2,1)S(1)}, u32[]{:S(2)}, u32[]{:S(2)}) collective-permute-start(bf16[4,2,2,4,8,640]{5,4,3,2,1,0:T(8,128)(2,1)S(1)} %get-tuple-element.34), channel_id=1, source_target_pairs={{0,2},{2,0},{4,6},{6,4},{8,10},{10,8},{12,14},{14,12},{1,3},{3,1},... | collective-permute-start | bytes 1966088 | tf_op jit(solution)/shard_map/ppermute | solution.py:546
  27.0 0.1 slice_bitcast_fusion.1
  27.0 25.2 %collective-permute-done.1 = bf16[4,2,2,4,8,640]{5,4,3,2,1,0:T(8,128)(2,1)S(1)} collective-permute-done((bf16[4,2,2,4,8,640]{5,4,3,2,1,0:T(8,128)(2,1)S(1)}, bf16[4,2,2,4,8,640]{5,4,3,2,1,0:T(8,128)(2,1)S(1)}, u32[]{:S(2)}, u32[]{:S(2)}) %collective-permute-start.1) | collective-permute-done | bytes 655392 | tf_op jit(solution)/shard_map/ppermute | solution.py:546
  52.2 0.7 slice_bitcast_fusion
  52.9 0.7 pad_maximum_fusion.2
  53.6 2.1 %collective-permute-start.2 = (bf16[2,2,32,640]{3,2,1,0:T(8,128)(2,1)}, bf16[2,2,32,640]{3,2,1,0:T(8,128)(2,1)S(1)}, u32[]{:S(2)}, u32[]{:S(2)}) collective-permute-start(bf16[2,2,32,640]{3,2,1,0:T(8,128)(2,1)} %pad_maximum_fusion.2), channel_id=1, source_target_pairs={{0,4},{2,6},{4,0},{6,2},{8,12},{10,14},{12,8},{14,10},{1,5},{3,7},... | collective-permute-start | bytes 491528 | tf_op jit(solution)/shard_map/ppermute | solution.py:546
  55.7 0.7 pad_maximum_fusion.6
  56.4 0.7 pad_maximum_fusion.7
  57.1 1.9 %collective-permute-start.14 = (bf16[2,2,32,640]{3,2,1,0:T(8,128)(2,1)}, bf16[2,2,32,640]{3,2,1,0:T(8,128)(2,1)}, u32[]{:S(2)}, u32[]{:S(2)}) collective-permute-start(bf16[2,2,32,640]{3,2,1,0:T(8,128)(2,1)} %pad_maximum_fusion.7), channel_id=1, source_target_pairs={{0,8},{2,10},{4,12},{6,14},{8,0},{10,2},{12,4},{14,6},{1,9},{3,11}... | collective-permute-start | bytes 491528 | tf_op jit(solution)/shard_map/ppermute | solution.py:546
  58.9 0.7 pad_maximum_fusion.8
  59.6 2.5 %collective-permute-start.15 = (bf16[2,2,32,640]{3,2,1,0:T(8,128)(2,1)}, bf16[2,2,32,640]{3,2,1,0:T(8,128)(2,1)}, u32[]{:S(2)}, u32[]{:S(2)}) collective-permute-start(bf16[2,2,32,640]{3,2,1,0:T(8,128)(2,1)} %pad_maximum_fusion.8), channel_id=1, source_target_pairs={{0,12},{2,14},{4,8},{6,10},{8,4},{10,6},{12,0},{14,2},{1,13},{3,15... | collective-permute-start | bytes 491528 | tf_op jit(solution)/shard_map/ppermute | solution.py:546
  62.1 0.7 pad_maximum_fusion.3
  62.8 1.0 collective-permute-start.3
  63.8 0.7 pad_maximum_fusion.5.refs_0_
  64.5 6.8 %shard_map.110 = (bf16[4,512,512]{2,1,0:T(8,128)(2,1)}, bf16[4,512,512]{2,1,0:T(8,128)(2,1)}) custom-call(s32[1]{0:T(128)} %bitcast.core, bf16[8,2,2,2,32,640]{5,4,3,2,1,0:T(8,128)(2,1)S(1)} %bitcast.87), custom_call_target="tpu_custom_call" | custom-call | tf_op jit(solution)/shard_map/pallas_call | solution.py:187
  71.3 2.4 %collective-permute-done.13.refs_1_ = bf16[2,2,32,640]{3,2,1,0:T(8,128)(2,1)} collective-permute-done((bf16[2,2,32,640]{3,2,1,0:T(8,128)(2,1)}, bf16[2,2,32,640]{3,2,1,0:T(8,128)(2,1)}, u32[]{:S(2)}, u32[]{:S(2)}) %collective-permute-start.13) | collective-permute-done | bytes 163872 | tf_op jit(solution)/shard_map/ppermute | solution.py:546
  73.7 11.7 %collective-permute-done.14.refs_2_ = bf16[2,2,32,640]{3,2,1,0:T(8,128)(2,1)} collective-permute-done((bf16[2,2,32,640]{3,2,1,0:T(8,128)(2,1)}, bf16[2,2,32,640]{3,2,1,0:T(8,128)(2,1)}, u32[]{:S(2)}, u32[]{:S(2)}) %collective-permute-start.14) | collective-permute-done | bytes 163872 | tf_op jit(solution)/shard_map/ppermute | solution.py:546
  85.4 3.3 %shard_map.114 = (bf16[256,640]{1,0:T(8,128)(2,1)S(1)}, bf16[256,640]{1,0:T(8,128)(2,1)S(1)}) custom-call(s32[1]{0:T(128)} %bitcast.1.place, bf16[4,512,512]{2,1,0:T(8,128)(2,1)} %get-tuple-element.30.weights, bf16[2,2,32,640]{3,2,1,0:T(8,128)(2,1)} %pad_maximum_fusion.5.refs_0_, bf16[2,2,32,640]{3,2,1,0:T(8,128)(2,1)} %collective-permute-done.13.refs_1_, ...), custom_call_target="tpu_custom_call" | custom-call | tf_op jit(solution)/shard_map/pallas_call | solution.py:247
  88.7 0.1 collective-permute-start.16
  88.9 1.4 collective-permute-start.4
  90.3 0.1 pad_add_fusion.scalars
  90.4 0.7 pad_maximum_fusion.1.refs_0_.refs_1_
  91.1 2.3 %shard_map.115.refs_0_ = bf16[256,1024]{1,0:T(8,128)(2,1)} custom-call(s32[2]{0:T(128)S(1)} %pad_add_fusion.scalars, bf16[256,640]{1,0:T(8,128)(2,1)S(1)} %get-tuple-element.31.near, bf16[256,640]{1,0:T(8,128)(2,1)S(1)} %collective-permute-done.16.far, bf16[1280,1024]{1,0:T(8,128)(2,1)S(1)} %copy-done, f32[1,1024]{1,0:T(1,128)S(1)} %bitcast.108), custom_call_target="tpu_custom_call" | custom-call | tf_op jit(solution)/shard_map/pallas_call | solution.py:290
  93.4 4.0 %collective-permute-done.4.refs_3_.refs_4_ = bf16[2,2,32,640]{3,2,1,0:T(8,128)(2,1)S(1)} collective-permute-done((bf16[2,2,32,640]{3,2,1,0:T(8,128)(2,1)S(1)}, bf16[2,2,32,640]{3,2,1,0:T(8,128)(2,1)S(1)}, u32[]{:S(2)}, u32[]{:S(2)}) %collective-permute-start.4) | collective-permute-done | bytes 163872 | tf_op jit(solution)/shard_map/ppermute | solution.py:546
  97.4 0.7 copy-done.10
  98.1 7.7 %all-to-all-start.1 = ((bf16[8,4,8,1024]{3,2,1,0:T(8,128)(2,1)}), bf16[8,4,8,1024]{3,2,1,0:T(8,128)(2,1)S(1)}, u32[]{:S(2)}, u32[]{:S(2)}) async-start(bf16[8,4,8,1024]{3,2,1,0:T(8,128)(2,1)} %bitcast.113), calls=%async_computation.1 | async-start | bytes 1048576 | tf_op jit(solution)/shard_map/all_to_all | solution.py:550
  105.8 3.1 %shard_map.112 = (bf16[256,640]{1,0:T(8,128)(2,1)S(1)}, bf16[256,640]{1,0:T(8,128)(2,1)S(1)}) custom-call(s32[1]{0:T(128)} %bitcast.1.place, bf16[4,512,512]{2,1,0:T(8,128)(2,1)} %get-tuple-element.19.weights, bf16[2,2,32,640]{3,2,1,0:T(8,128)(2,1)} %pad_maximum_fusion.1.refs_0_.refs_1_, bf16[2,2,32,640]{3,2,1,0:T(8,128)(2,1)} %copy-done.8, ...), custom_call_target="tpu_custom_call" | custom-call | tf_op jit(solution)/shard_map/pallas_call | solution.py:247
  109.0 0.1 collective-permute-start.5
  109.1 1.6 %collective-permute-done.5.far = bf16[256,640]{1,0:T(8,128)(2,1)S(1)} collective-permute-done((bf16[256,640]{1,0:T(8,128)(2,1)S(1)}, bf16[256,640]{1,0:T(8,128)(2,1)S(1)}, u32[]{:S(2)}, u32[]{:S(2)}) %collective-permute-start.5) | collective-permute-done | bytes 327712 | tf_op jit(solution)/shard_map/ppermute | solution.py:546
  110.7 2.2 %shard_map.113 = (bf16[1,32,1024]{2,1,0:T(8,128)(2,1)S(1)}, bf16[1,32,1024]{2,1,0:T(8,128)(2,1)}, bf16[1,32,1024]{2,1,0:T(8,128)(2,1)}, bf16[1,32,1024]{2,1,0:T(...) custom-call(s32[2]{0:T(128)S(1)} %pad_add_fusion.scalars, ...), custom_call_target="tpu_custom_call" | custom-call | tf_op jit(solution)/shard_map/pallas_call | solution.py:290
  112.9 2.0 %collective-permute-start.6 = (bf16[1,32,1024]{2,1,0:T(8,128)(2,1)}, bf16[1,32,1024]{2,1,0:T(8,128)(2,1)S(1)}, u32[]{:S(2)}, u32[]{:S(2)}) collective-permute-start(bf16[1,32,1024]{2,1,0:T(8,128)(2,1)} %get-tuple-element.23), channel_id=1, source_target_pairs={{0,2},{2,0},{4,6},{6,4},{8,10},{10,8},{12,14},{14,12},{1,3},{3,1},... | collective-permute-start | bytes 196616 | tf_op jit(solution)/shard_map/ppermute | solution.py:546
  114.9 1.5 collective-permute-start.7
  116.4 2.9 %collective-permute-start.9 = (bf16[1,32,1024]{2,1,0:T(8,128)(2,1)S(1)}, bf16[1,32,1024]{2,1,0:T(8,128)(2,1)S(1)}, u32[]{:S(2)}, u32[]{:S(2)}) collective-permute-start(bf16[1,32,1024]{2,1,0:T(8,128)(2,1)S(1)} %get-tuple-element.26), channel_id=1, source_target_pairs={{0,8},{2,10},{4,12},{6,14},{8,0},{10,2},{12,4},{14,6},{1,9},{3,11}... | collective-permute-start | bytes 196616 | tf_op jit(solution)/shard_map/ppermute | solution.py:546
  119.3 1.5 %all-to-all-done.1.refs_1_.refs_8_ = bf16[8,4,8,1024]{3,2,1,0:T(8,128)(2,1)S(1)} async-done(((bf16[8,4,8,1024]{3,2,1,0:T(8,128)(2,1)}), bf16[8,4,8,1024]{3,2,1,0:T(8,128)(2,1)S(1)}, u32[]{:S(2)}, u32[]{:S(2)}) %all-to-all-start.1) | async-done | bytes 524320 | tf_op jit(solution)/shard_map/all_to_all | solution.py:550
  120.9 3.2 %collective-permute-start.17 = (bf16[2,4,8,1024]{3,2,1,0:T(8,128)(2,1)S(1)}, bf16[2,4,8,1024]{3,2,1,0:T(8,128)(2,1)S(1)}, u32[]{:S(2)}, u32[]{:S(2)}) collective-permute-start(bf16[2,4,8,1024]{3,2,1,0:T(8,128)(2,1)S(1)} %get-tuple-element.62), channel_id=1, source_target_pairs={{0,2},{2,4},{4,6},{6,8},{8,10},{10,12},{12,14},{1,3},{3,5},{5,7},{... | collective-permute-start | bytes 393224 | tf_op jit(solution)/shard_map/ppermute | solution.py:542
  124.1 1.5 collective-permute-start.18
  125.6 1.7 %collective-permute-start.10 = (bf16[1,32,1024]{2,1,0:T(8,128)(2,1)S(1)}, bf16[1,32,1024]{2,1,0:T(8,128)(2,1)S(1)}, u32[]{:S(2)}, u32[]{:S(2)}) collective-permute-start(bf16[1,32,1024]{2,1,0:T(8,128)(2,1)S(1)} %get-tuple-element.27), channel_id=1, source_target_pairs={{0,10},{2,8},{4,14},{6,12},{8,2},{10,0},{12,6},{14,4},{1,11},{3,9}... | collective-permute-start | bytes 196616 | tf_op jit(solution)/shard_map/ppermute | solution.py:546
  127.3 2.9 %collective-permute-start.11 = (bf16[1,32,1024]{2,1,0:T(8,128)(2,1)S(1)}, bf16[1,32,1024]{2,1,0:T(8,128)(2,1)S(1)}, u32[]{:S(2)}, u32[]{:S(2)}) collective-permute-start(bf16[1,32,1024]{2,1,0:T(8,128)(2,1)S(1)} %get-tuple-element.28), channel_id=1, source_target_pairs={{0,12},{2,14},{4,8},{6,10},{8,4},{10,6},{12,0},{14,2},{1,13},{3,15... | collective-permute-start | bytes 196616 | tf_op jit(solution)/shard_map/ppermute | solution.py:546
  130.2 2.0 %collective-permute-start.12 = (bf16[1,32,1024]{2,1,0:T(8,128)(2,1)S(1)}, bf16[1,32,1024]{2,1,0:T(8,128)(2,1)S(1)}, u32[]{:S(2)}, u32[]{:S(2)}) collective-permute-start(bf16[1,32,1024]{2,1,0:T(8,128)(2,1)S(1)} %get-tuple-element.29), channel_id=1, source_target_pairs={{0,14},{2,12},{4,10},{6,8},{8,6},{10,4},{12,2},{14,0},{1,15},{3,13... | collective-permute-start | bytes 196616 | tf_op jit(solution)/shard_map/ppermute | solution.py:546
  132.3 0.9 collective-permute-done.10
  133.1 0.3 collective-permute-done.11
  133.5 3.8 %collective-permute-done.12 = bf16[1,32,1024]{2,1,0:T(8,128)(2,1)S(1)} collective-permute-done((bf16[1,32,1024]{2,1,0:T(8,128)(2,1)S(1)}, bf16[1,32,1024]{2,1,0:T(8,128)(2,1)S(1)}, u32[]{:S(2)}, u32[]{:S(2)}) %collective-permute-start.12) | collective-permute-done | bytes 65568 | tf_op jit(solution)/shard_map/ppermute | solution.py:546
  137.3 0.1 collective-permute-start.20
  137.4 0.1 shard_map.117
  137.5 0.5 collective-permute-start.19
  138.1 0.5 collective-permute-done.20.refs_12_
  138.6 0.4 collective-permute-done.19.refs_11_
  139.0 0.2 broadcast_in_dim.21.refs_13_
  139.3 8.8 %shard_map.119 = bf16[2048,256]{1,0:T(8,128)(2,1)} custom-call(s32[2]{0:T(128)S(1)} %pad_add_fusion.scalars, bf16[1,4,8,1024]{3,2,1,0:T(8,128)(2,1)S(1)} %bitcast.93, bf16[1,4,8,1024]{3,2,1,0:T(8,128)(2,1)S(1)} %bitcast.95, bf16[1,4,8,1024]{3,2,1,0:T(8,128)(2,1)S(1)} %bitcast.97, bf16[1,4,8,1024]{3,2,1,0:T(8,128)(2,1)S(1)} %bitcast.99, ...), custom_call_target="tpu_custom_call" | custom-call | tf_op jit(solution)/shard_map/pallas_call | solution.py:495
  (38 shorter events, 0.2 us)
Async XLA Ops:
  3.0 61.5 %all-to-all-start = ((bf16[16,2,2,32,640]{4,3,2,1,0:T(8,128)(2,1)}), bf16[16,2,2,32,640]{4,3,2,1,0:T(8,128)(2,1)S(1)}, u32[]{:S(2)}, u32[]{:S(2)}) async-start(bf16[16,2,2,32,640]{4,3,2,1,0:T(8,128)(2,1)} %bitcast.112), calls=%async_computation | async-start | bytes 5242880 | tf_op jit(solution)/shard_map/all_to_all | solution.py:550
  10.4 1.3 copy-start.1
  11.7 1.3 copy-start.2
  13.0 1.3 copy-start.3
  19.9 2.5 %collective-permute-start = (bf16[4,128,640]{2,1,0:T(8,128)(2,1)}, bf16[4,128,640]{2,1,0:T(8,128)(2,1)}, u32[]{:S(2)}, u32[]{:S(2)}) collective-permute-start(bf16[4,128,640]{2,1,0:T(8,128)(2,1)} %get-tuple-element.44), channel_id=1, source_target_pairs={{0,1},{1,0},{2,3},{3,2},{4,5},{5,4},{6,7},{7,6},{8,9},{9,8},{10,11... | collective-permute-start | bytes 1966088 | tf_op jit(solution)/shard_map/ppermute | solution.py:546
  25.0 27.2 %collective-permute-start.1 = (bf16[4,2,2,4,8,640]{5,4,3,2,1,0:T(8,128)(2,1)S(1)}, bf16[4,2,2,4,8,640]{5,4,3,2,1,0:T(8,128)(2,1)S(1)}, u32[]{:S(2)}, u32[]{:S(2)}) collective-permute-start(bf16[4,2,2,4,8,640]{5,4,3,2,1,0:T(8,128)(2,1)S(1)} %get-tuple-element.34), channel_id=1, source_target_pairs={{0,2},{2,0},{4,6},{6,4},{8,10},{10,8},{12,14},{14,12},{1,3},{3,1},... | collective-permute-start | bytes 1966088 | tf_op jit(solution)/shard_map/ppermute | solution.py:546
  53.6 39.8 %collective-permute-start.2 = (bf16[2,2,32,640]{3,2,1,0:T(8,128)(2,1)}, bf16[2,2,32,640]{3,2,1,0:T(8,128)(2,1)S(1)}, u32[]{:S(2)}, u32[]{:S(2)}) collective-permute-start(bf16[2,2,32,640]{3,2,1,0:T(8,128)(2,1)} %pad_maximum_fusion.2), channel_id=1, source_target_pairs={{0,4},{2,6},{4,0},{6,2},{8,12},{10,14},{12,8},{14,10},{1,5},{3,7},... | collective-permute-start | bytes 491528 | tf_op jit(solution)/shard_map/ppermute | solution.py:546
  56.4 17.4 %collective-permute-start.13 = (bf16[2,2,32,640]{3,2,1,0:T(8,128)(2,1)}, bf16[2,2,32,640]{3,2,1,0:T(8,128)(2,1)}, u32[]{:S(2)}, u32[]{:S(2)}) collective-permute-start(bf16[2,2,32,640]{3,2,1,0:T(8,128)(2,1)} %pad_maximum_fusion.6), channel_id=1, source_target_pairs={{0,4},{2,6},{4,0},{6,2},{8,12},{10,14},{12,8},{14,10},{1,5},{3,7},... | collective-permute-start | bytes 491528 | tf_op jit(solution)/shard_map/ppermute | solution.py:546
  57.1 28.4 %collective-permute-start.14 = (bf16[2,2,32,640]{3,2,1,0:T(8,128)(2,1)}, bf16[2,2,32,640]{3,2,1,0:T(8,128)(2,1)}, u32[]{:S(2)}, u32[]{:S(2)}) collective-permute-start(bf16[2,2,32,640]{3,2,1,0:T(8,128)(2,1)} %pad_maximum_fusion.7), channel_id=1, source_target_pairs={{0,8},{2,10},{4,12},{6,14},{8,0},{10,2},{12,4},{14,6},{1,9},{3,11}... | collective-permute-start | bytes 491528 | tf_op jit(solution)/shard_map/ppermute | solution.py:546
  59.6 25.8 %collective-permute-start.15 = (bf16[2,2,32,640]{3,2,1,0:T(8,128)(2,1)}, bf16[2,2,32,640]{3,2,1,0:T(8,128)(2,1)}, u32[]{:S(2)}, u32[]{:S(2)}) collective-permute-start(bf16[2,2,32,640]{3,2,1,0:T(8,128)(2,1)} %pad_maximum_fusion.8), channel_id=1, source_target_pairs={{0,12},{2,14},{4,8},{6,10},{8,4},{10,6},{12,0},{14,2},{1,13},{3,15... | collective-permute-start | bytes 491528 | tf_op jit(solution)/shard_map/ppermute | solution.py:546
  62.8 30.6 %collective-permute-start.3 = (bf16[2,2,32,640]{3,2,1,0:T(8,128)(2,1)}, bf16[2,2,32,640]{3,2,1,0:T(8,128)(2,1)S(1)}, u32[]{:S(2)}, u32[]{:S(2)}) collective-permute-start(bf16[2,2,32,640]{3,2,1,0:T(8,128)(2,1)} %pad_maximum_fusion.3), channel_id=1, source_target_pairs={{0,8},{2,10},{4,12},{6,14},{8,0},{10,2},{12,4},{14,6},{1,9},{3,11}... | collective-permute-start | bytes 491528 | tf_op jit(solution)/shard_map/ppermute | solution.py:546
  85.4 4.9 %copy-start.11 = (bf16[1,2,32,640]{3,2,1,0:T(8,128)(2,1)S(1)}, bf16[1,2,32,640]{3,2,1,0:T(8,128)(2,1)}, u32[]{:S(2)}) copy-start(bf16[1,2,32,640]{3,2,1,0:T(8,128)(2,1)} %get-tuple-element.60) | copy-start | bytes 245764
  85.4 5.6 %copy-start = (bf16[1280,1024]{1,0:T(8,128)(2,1)S(1)}, bf16[1280,1024]{1,0:T(8,128)(2,1)}, u32[]{:S(2)}) copy-start(bf16[1280,1024]{1,0:T(8,128)(2,1)} %proj_weight.3) | copy-start | bytes 7864324
  85.4 5.6 %copy-start.5 = (f32[1024]{0:T(1024)S(1)}, f32[1024]{0:T(1024)}, u32[]{:S(2)}) copy-start(f32[1024]{0:T(1024)} %param.17) | copy-start | bytes 12292
  88.7 2.3 %collective-permute-start.16 = (bf16[256,640]{1,0:T(8,128)(2,1)S(1)}, bf16[256,640]{1,0:T(8,128)(2,1)S(1)}, u32[]{:S(2)}, u32[]{:S(2)}) collective-permute-start(bf16[256,640]{1,0:T(8,128)(2,1)S(1)} %get-tuple-element.32), channel_id=1, source_target_pairs={{0,1},{1,0},{2,3},{3,2},{4,5},{5,4},{6,7},{7,6},{8,9},{9,8},{10,11... | collective-permute-start | bytes 983048 | tf_op jit(solution)/shard_map/ppermute | solution.py:546
  88.9 8.6 %collective-permute-start.4 = (bf16[2,2,32,640]{3,2,1,0:T(8,128)(2,1)S(1)}, bf16[2,2,32,640]{3,2,1,0:T(8,128)(2,1)S(1)}, u32[]{:S(2)}, u32[]{:S(2)}) collective-permute-start(bf16[2,2,32,640]{3,2,1,0:T(8,128)(2,1)S(1)} %pad_maximum_fusion.4), channel_id=1, source_target_pairs={{0,12},{2,14},{4,8},{6,10},{8,4},{10,6},{12,0},{14,2},{1,13},{3,15... | collective-permute-start | bytes 491528 | tf_op jit(solution)/shard_map/ppermute | solution.py:546
  93.4 4.0 %copy-start.8 = (bf16[2,2,32,640]{3,2,1,0:T(8,128)(2,1)}, bf16[2,2,32,640]{3,2,1,0:T(8,128)(2,1)S(1)}, u32[]{:S(2)}) copy-start(bf16[2,2,32,640]{3,2,1,0:T(8,128)(2,1)S(1)} %collective-permute-done.2.refs_1_.refs_2_) | copy-start | bytes 491524
  93.4 4.0 %copy-start.9 = (bf16[2,2,32,640]{3,2,1,0:T(8,128)(2,1)}, bf16[2,2,32,640]{3,2,1,0:T(8,128)(2,1)S(1)}, u32[]{:S(2)}) copy-start(bf16[2,2,32,640]{3,2,1,0:T(8,128)(2,1)S(1)} %collective-permute-done.3.refs_2_.refs_3_) | copy-start | bytes 491524
  97.4 0.7 copy-start.10
  98.1 22.8 %all-to-all-start.1 = ((bf16[8,4,8,1024]{3,2,1,0:T(8,128)(2,1)}), bf16[8,4,8,1024]{3,2,1,0:T(8,128)(2,1)S(1)}, u32[]{:S(2)}, u32[]{:S(2)}) async-start(bf16[8,4,8,1024]{3,2,1,0:T(8,128)(2,1)} %bitcast.113), calls=%async_computation.1 | async-start | bytes 1048576 | tf_op jit(solution)/shard_map/all_to_all | solution.py:550
  109.0 1.7 %collective-permute-start.5 = (bf16[256,640]{1,0:T(8,128)(2,1)S(1)}, bf16[256,640]{1,0:T(8,128)(2,1)S(1)}, u32[]{:S(2)}, u32[]{:S(2)}) collective-permute-start(bf16[256,640]{1,0:T(8,128)(2,1)S(1)} %get-tuple-element.21), channel_id=1, source_target_pairs={{0,1},{1,0},{2,3},{3,2},{4,5},{5,4},{6,7},{7,6},{8,9},{9,8},{10,11... | collective-permute-start | bytes 983048 | tf_op jit(solution)/shard_map/ppermute | solution.py:546
  112.9 11.2 %collective-permute-start.6 = (bf16[1,32,1024]{2,1,0:T(8,128)(2,1)}, bf16[1,32,1024]{2,1,0:T(8,128)(2,1)S(1)}, u32[]{:S(2)}, u32[]{:S(2)}) collective-permute-start(bf16[1,32,1024]{2,1,0:T(8,128)(2,1)} %get-tuple-element.23), channel_id=1, source_target_pairs={{0,2},{2,0},{4,6},{6,4},{8,10},{10,8},{12,14},{14,12},{1,3},{3,1},... | collective-permute-start | bytes 196616 | tf_op jit(solution)/shard_map/ppermute | solution.py:546
  114.9 10.6 %collective-permute-start.7 = (bf16[1,32,1024]{2,1,0:T(8,128)(2,1)}, bf16[1,32,1024]{2,1,0:T(8,128)(2,1)S(1)}, u32[]{:S(2)}, u32[]{:S(2)}) collective-permute-start(bf16[1,32,1024]{2,1,0:T(8,128)(2,1)} %get-tuple-element.24), channel_id=1, source_target_pairs={{0,4},{2,6},{4,0},{6,2},{8,12},{10,14},{12,8},{14,10},{1,5},{3,7},... | collective-permute-start | bytes 196616 | tf_op jit(solution)/shard_map/ppermute | solution.py:546
  116.4 10.9 %collective-permute-start.8 = (bf16[1,32,1024]{2,1,0:T(8,128)(2,1)S(1)}, bf16[1,32,1024]{2,1,0:T(8,128)(2,1)S(1)}, u32[]{:S(2)}, u32[]{:S(2)}) collective-permute-start(bf16[1,32,1024]{2,1,0:T(8,128)(2,1)S(1)} %get-tuple-element.25), channel_id=1, source_target_pairs={{0,6},{2,4},{4,2},{6,0},{8,14},{10,12},{12,10},{14,8},{1,7},{3,5},... | collective-permute-start | bytes 196616 | tf_op jit(solution)/shard_map/ppermute | solution.py:546
  116.4 22.8 %copy-start.4 = (bf16[3,3,256,256]{3,2,1,0:T(8,128)(2,1)S(1)}, bf16[3,3,256,256]{3,2,1,0:T(8,128)(2,1)}, u32[]{:S(2)}) copy-start(bf16[3,3,256,256]{3,2,1,0:T(8,128)(2,1)} %param.18) | copy-start | bytes 3538948
  116.4 22.8 %copy-start.6 = (f32[256]{0:T(256)S(1)}, f32[256]{0:T(256)}, u32[]{:S(2)}) copy-start(f32[256]{0:T(256)} %param.19) | copy-start | bytes 3076
  116.4 22.8 %copy-start.7 = (f32[256]{0:T(256)S(1)}, f32[256]{0:T(256)}, u32[]{:S(2)}) copy-start(f32[256]{0:T(256)} %param.21) | copy-start | bytes 3076
  116.4 13.8 %collective-permute-start.9 = (bf16[1,32,1024]{2,1,0:T(8,128)(2,1)S(1)}, bf16[1,32,1024]{2,1,0:T(8,128)(2,1)S(1)}, u32[]{:S(2)}, u32[]{:S(2)}) collective-permute-start(bf16[1,32,1024]{2,1,0:T(8,128)(2,1)S(1)} %get-tuple-element.26), channel_id=1, source_target_pairs={{0,8},{2,10},{4,12},{6,14},{8,0},{10,2},{12,4},{14,6},{1,9},{3,11}... | collective-permute-start | bytes 196616 | tf_op jit(solution)/shard_map/ppermute | solution.py:546
  120.9 16.5 %collective-permute-start.17 = (bf16[2,4,8,1024]{3,2,1,0:T(8,128)(2,1)S(1)}, bf16[2,4,8,1024]{3,2,1,0:T(8,128)(2,1)S(1)}, u32[]{:S(2)}, u32[]{:S(2)}) collective-permute-start(bf16[2,4,8,1024]{3,2,1,0:T(8,128)(2,1)S(1)} %get-tuple-element.62), channel_id=1, source_target_pairs={{0,2},{2,4},{4,6},{6,8},{8,10},{10,12},{12,14},{1,3},{3,5},{5,7},{... | collective-permute-start | bytes 393224 | tf_op jit(solution)/shard_map/ppermute | solution.py:542
  124.1 13.3 %collective-permute-start.18 = (bf16[2,4,8,1024]{3,2,1,0:T(8,128)(2,1)S(1)}, bf16[2,4,8,1024]{3,2,1,0:T(8,128)(2,1)S(1)}, u32[]{:S(2)}, u32[]{:S(2)}) collective-permute-start(bf16[2,4,8,1024]{3,2,1,0:T(8,128)(2,1)S(1)} %get-tuple-element.61), channel_id=1, source_target_pairs={{2,0},{4,2},{6,4},{8,6},{10,8},{12,10},{14,12},{3,1},{5,3},{7,5},{... | collective-permute-start | bytes 393224 | tf_op jit(solution)/shard_map/ppermute | solution.py:542
  125.6 7.5 %collective-permute-start.10 = (bf16[1,32,1024]{2,1,0:T(8,128)(2,1)S(1)}, bf16[1,32,1024]{2,1,0:T(8,128)(2,1)S(1)}, u32[]{:S(2)}, u32[]{:S(2)}) collective-permute-start(bf16[1,32,1024]{2,1,0:T(8,128)(2,1)S(1)} %get-tuple-element.27), channel_id=1, source_target_pairs={{0,10},{2,8},{4,14},{6,12},{8,2},{10,0},{12,6},{14,4},{1,11},{3,9}... | collective-permute-start | bytes 196616 | tf_op jit(solution)/shard_map/ppermute | solution.py:546
  127.3 6.1 %collective-permute-start.11 = (bf16[1,32,1024]{2,1,0:T(8,128)(2,1)S(1)}, bf16[1,32,1024]{2,1,0:T(8,128)(2,1)S(1)}, u32[]{:S(2)}, u32[]{:S(2)}) collective-permute-start(bf16[1,32,1024]{2,1,0:T(8,128)(2,1)S(1)} %get-tuple-element.28), channel_id=1, source_target_pairs={{0,12},{2,14},{4,8},{6,10},{8,4},{10,6},{12,0},{14,2},{1,13},{3,15... | collective-permute-start | bytes 196616 | tf_op jit(solution)/shard_map/ppermute | solution.py:546
  130.2 7.1 %collective-permute-start.12 = (bf16[1,32,1024]{2,1,0:T(8,128)(2,1)S(1)}, bf16[1,32,1024]{2,1,0:T(8,128)(2,1)S(1)}, u32[]{:S(2)}, u32[]{:S(2)}) collective-permute-start(bf16[1,32,1024]{2,1,0:T(8,128)(2,1)S(1)} %get-tuple-element.29), channel_id=1, source_target_pairs={{0,14},{2,12},{4,10},{6,8},{8,6},{10,4},{12,2},{14,0},{1,15},{3,13... | collective-permute-start | bytes 196616 | tf_op jit(solution)/shard_map/ppermute | solution.py:546
  137.3 1.3 collective-permute-start.20
  137.5 1.4 collective-permute-start.19

commit v5 on v4

--- a/solution.py
+++ b/solution.py
@@ -198,38 +198,45 @@
             )
             for part in range(parts)
         ],
-        out_shape=[pltpu.HBM((heads, rows, rows), jnp.bfloat16)] * parts,
+        out_shape=[
+            (pltpu.HBM if part else pltpu.VMEM)((heads, rows, rows), jnp.bfloat16) for part in range(parts)
+        ],
         compiler_params=params(2),
     )(core.reshape(1), pair)
 
 
-def mix_kernel(place, weights, *refs):
+def mix_kernel(fetched, place, weights, *refs):
     pieces, (near, far, value, held, held_weights, arrived) = refs[:-6], refs[-6:]
     each, cores, rows, features = pieces[0].shape
     half = value.shape[0] // cores
     heads = features // HEAD_DIM
-    copies = [
-        pltpu.make_async_copy(piece, held.at[k], arrived.at[k]) for k, piece in enumerate(pieces)
-    ]
-    copies += [
-        pltpu.make_async_copy(weights.at[head], held_weights.at[head], arrived.at[len(pieces) + head])
-        for head in range(heads)
-    ]
+    copies = []
+    if fetched:
+        copies = [
+            pltpu.make_async_copy(piece, held.at[k], arrived.at[k]) for k, piece in enumerate(pieces)
+        ]
+        copies += [
+            pltpu.make_async_copy(weights.at[head], held_weights.at[head], arrived.at[len(pieces) + head])
+            for head in range(heads)
+        ]
     for copy in copies:
         copy.start()
-    for k in range(len(pieces)):
-        copies[k].wait()
+    for k, piece in enumerate(pieces):
+        if fetched:
+            copies[k].wait()
+            piece = held.at[k]
         for j in range(each):
             at = pl.multiple_of((place[0] ^ (k * each + j)) * rows, rows)
             for core in range(cores):
-                value[pl.ds(core * half + at, rows), :] = held[k, j, core].astype(value.dtype)
+                value[pl.ds(core * half + at, rows), :] = piece[j, core].astype(value.dtype)
     mixed = []
     for head in range(heads):
-        copies[len(pieces) + head].wait()
+        if fetched:
+            copies[len(pieces) + head].wait()
         lanes = slice(head_start(head), head_start(head) + SPAN)
         mixed.append(
             jnp.dot(
-                held_weights[head], value[:, lanes].astype(jnp.bfloat16),
+                (held_weights if fetched else weights)[head], value[:, lanes].astype(jnp.bfloat16),
                 preferred_element_type=jnp.float32,
             )
         )
@@ -238,27 +245,30 @@
     far[...] = joined[half:]
 
 
-def index_mix(place, weights, pieces):
+def index_mix(place, weights, pieces, fetched):
     heads, rows, _ = weights.shape
     features = pieces[0].shape[-1]
     result = pltpu.VMEM((rows // 2, features), jnp.bfloat16)
     held = jnp.float32 if pieces[0].shape[2] % EDGE else jnp.bfloat16
-    far = pl.BlockSpec(memory_space=pltpu.HBM)
+    source = pl.BlockSpec(memory_space=pltpu.HBM if fetched else pltpu.VMEM)
+    if fetched:
+        weights, *pieces = [
+            pltpu.with_memory_space_constraint(value, pltpu.HBM) for value in [weights] + pieces
+        ]
     return pl.pallas_call(
-        mix_kernel,
-        in_specs=[pl.BlockSpec(memory_space=pltpu.SMEM)] + [far] * (1 + len(pieces)),
+        functools.partial(mix_kernel, fetched),
+        in_specs=[pl.BlockSpec(memory_space=pltpu.SMEM)] + [source] * (1 + len(pieces)),
         out_specs=[pl.BlockSpec(memory_space=pltpu.VMEM)] * 2,
         out_shape=[result, result],
         scratch_shapes=[
             pltpu.VMEM((rows, features), held),
             pltpu.VMEM((len(pieces),) + pieces[0].shape, jnp.bfloat16),
-            pltpu.VMEM(weights.shape, jnp.bfloat16),
+            pltpu.VMEM(weights.shape if fetched else (1, EDGE, LANES), jnp.bfloat16),
             pltpu.SemaphoreType.DMA((len(pieces) + heads,)),
         ],
         compiler_params=params(),
     )(
-        place.reshape(1),
-        *[pltpu.with_memory_space_constraint(value, pltpu.HBM) for value in [weights] + pieces],
+        place.reshape(1), weights, *pieces,
     )
 
 
@@ -353,7 +363,7 @@
     (
         outer, above, below, side_outer, side_middle, keep,
         first_kernel, first_bias, second_kernel, second_bias, out,
-        taken, even, odd, acted, woven, middle, second_held, fetched,
+        taken, even, odd, acted, woven, middle, second_held, fetched, ready, left,
     ) = refs
     fetches = [
         pltpu.make_async_copy(second_kernel, second_held, fetched.at[0]),
@@ -466,6 +476,7 @@
 
     fetches[0].wait()
     group = max(lines // 8, 1)
+    leaving = []
     for at in range(0, lines, group):
         for q in range(2):
             starts = [EDGE + (at + y) * pitch for y in range(group)]
@@ -475,8 +486,16 @@
                     woven[lane, pl.ds((at + y) * 2 * cols + q, cols, stride=2), :] = value[
                         y * cols : (y + 1) * cols, lane * LANES : (lane + 1) * LANES
                     ]
-    for lane in range(depth // LANES):
-        out[:, lane * LANES : (lane + 1) * LANES] = woven[lane].astype(jnp.bfloat16)
+        rows_here = pl.ds(at * 2 * cols, group * 2 * cols)
+        for lane in range(depth // LANES):
+            ready[rows_here, lane * LANES : (lane + 1) * LANES] = woven[lane, rows_here, :].astype(
+                jnp.bfloat16
+            )
+        copy = pltpu.make_async_copy(ready.at[rows_here], out.at[rows_here], left.at[at // group])
+        copy.start()
+        leaving.append(copy)
+    for copy in leaving:
+        copy.wait()
 
 
 def convolve_twice(
@@ -494,11 +513,11 @@
     kernels[1] = pltpu.with_memory_space_constraint(kernels[1], pltpu.HBM)
     found = pl.pallas_call(
         functools.partial(conv_kernel, rows, cols, len(middles)),
-        out_shape=jax.ShapeDtypeStruct((4 * rows * cols, depth), jnp.bfloat16),
+        out_shape=pltpu.HBM((4 * rows * cols, depth), jnp.bfloat16),
         in_specs=[pl.BlockSpec(memory_space=pltpu.SMEM)]
         + [near] * (len(middles) + 6)
         + [near, near, far, near],
-        out_specs=near,
+        out_specs=far,
         scratch_shapes=[
             pltpu.VMEM(((2 * rows + 4) * pitch + EDGE, 4 * depth), jnp.bfloat16),
             pltpu.VMEM((total + 2 * EDGE, depth), jnp.float32),
@@ -508,6 +527,8 @@
             pltpu.VMEM(outer.shape, jnp.bfloat16),
             pltpu.VMEM((3, 3 * depth, depth), jnp.bfloat16),
             pltpu.SemaphoreType.DMA((1,)),
+            pltpu.VMEM((4 * rows * cols, depth), jnp.bfloat16),
+            pltpu.SemaphoreType.DMA((2 * rows,)),
         ],
         compiler_params=params(size=2 * VMEM_BYTES),
     )(
@@ -625,7 +646,7 @@
     line = TILE_COLS // PIECE
 
     def projected_of(part, apart):
-        near, far = index_mix(row, weights[part], pieces[part])
+        near, far = index_mix(row, weights[part], pieces[part], part > 0)
         return project(
             near, swapped(far, "col", 1), proj_weight, proj_bias, core, row, places, apart
         )

time: 149 us -> 146 us (0.980)
  Pallas kernels: 34.2 us -> 31.3 us
    pallas_call x2, Pallas kernels: 6.44 us -> 4 us  [index_mix(): pl.pallas_call(functools.partial(mix_kernel, fetched), in_specs=[pl.Block...]
    unnamed x24 -> x26, local copies, waits for them, and re-layouts: 4.65 us -> 4.64 us
  transfers between devices with their start and end apart: 23 -> 23, of which waited for: 12 -> 11; matrix products, arithmetic and copies ran while one was open for 6% -> 6% of each run, Pallas kernels for 15% -> 14%
where the time goes in v5:
time: 146 us; the launch traced here: 145 us
  waiting for transfers between devices  55.7 us (38%)
  starting transfers between devices  43.8 us (30%)
  Pallas kernels  31.3 us (21%)
  local copies, waits for them, and re-layouts  7.42 us (5%)
  other arithmetic  6.79 us (5%)
    ppermute x19, waiting for transfers between devices, swapped(): lax.ppermute(value, axis, [(i, i ^ by) for i in range(lax.axis_size(axis))])  54.2 us
    ppermute x19, starting transfers between devices, swapped(): lax.ppermute(value, axis, [(i, i ^ by) for i in range(lax.axis_size(axis))])  25.1 us
    all_to_all x2, starting transfers between devices, exchanged(): return lax.all_to_all(value, axes, split_axis=0, concat_axis=0, tiled=True)  14.1 us
    pallas_call x1, Pallas kernels, convolve_twice(): pl.pallas_call(functools.partial(conv_kernel, rows, cols, len(middles)),...  8.59 us
    pallas_call x1, Pallas kernels, index_weights(): pl.pallas_call(functools.partial(weights_kernel, tokens), grid=(parts, he...  6.5 us
    unnamed x26, local copies, waits for them, and re-layouts  4.64 us
    ppermute x2, starting transfers between devices, shifted(): return lax.ppermute(value, axis, pairs)  4.63 us
    pallas_call x2, Pallas kernels, project(): pl.pallas_call(functools.partial(project_kernel, places, inner), in_specs...  4.61 us
  transfers between devices with their start and end apart: 23, of which 11 were waited for; matrix products, arithmetic and copies ran while one was open for 6% of the time, Pallas kernels for 14%

profile of v5, /device:TPU:0, one launch (start us, length us, event | category | flops | bytes accessed | tf_op | source)
XLA Modules:
  0.0 145.5 jit_solution(12566410954833188653)
XLA Ops:
  0.0 2.9 %shard_map.109 = bf16[8,2,2,2,32,640]{5,4,3,2,1,0:T(8,128)(2,1)} custom-call(bf16[4,128,1280]{2,1,0:T(8,128)(2,1)} %bitcast.114, bf16[4,128,1280]{2,1,0:T(8,128)(2,1)} %bitcast.115), custom_call_target="tpu_custom_call" | custom-call | tf_op jit(solution)/shard_map/pallas_call | solution.py:131
  2.9 7.4 %all-to-all-start = ((bf16[16,2,2,32,640]{4,3,2,1,0:T(8,128)(2,1)}), bf16[16,2,2,32,640]{4,3,2,1,0:T(8,128)(2,1)S(1)}, u32[]{:S(2)}, u32[]{:S(2)}) async-start(bf16[16,2,2,32,640]{4,3,2,1,0:T(8,128)(2,1)} %bitcast.112), calls=%async_computation | async-start | bytes 5242880 | tf_op jit(solution)/shard_map/all_to_all | solution.py:571
  10.3 0.0 copy-start.1
  10.4 1.3 copy-done.1
  11.7 1.3 copy-done.2
  13.0 1.3 copy-done.3
  14.3 4.5 %shard_map.111 = bf16[2,4,128,640]{3,2,1,0:T(8,128)(2,1)S(1)} custom-call(bf16[4,128,1280]{2,1,0:T(8,128)(2,1)S(1)} %bitcast.88, bf16[4,128,1280]{2,1,0:T(8,128)(2,1)S(1)} %bitcast.89, bf16[4,128,1280]{2,1,0:T(8,128)(2,1)S(1)} %bitcast.90), custom_call_target="tpu_custom_call" | custom-call | tf_op jit(solution)/shard_map/pallas_call | solution.py:83
  18.8 1.0 constant_dynamic-slice_fusion
  19.8 0.4 collective-permute-start
  20.2 2.1 %collective-permute-done = bf16[4,128,640]{2,1,0:T(8,128)(2,1)} collective-permute-done((bf16[4,128,640]{2,1,0:T(8,128)(2,1)}, bf16[4,128,640]{2,1,0:T(8,128)(2,1)}, u32[]{:S(2)}, u32[]{:S(2)}) %collective-permute-start) | collective-permute-done | bytes 655392 | tf_op jit(solution)/shard_map/ppermute | solution.py:567
  22.3 1.0 fusion.8
  23.3 1.2 fusion.14
  24.5 0.1 maximum_bitcast_fusion.2
  24.6 0.1 maximum_bitcast_fusion
  24.6 0.2 pad_maximum_fusion
  24.9 0.1 dynamic-slice_bitcast_fusion.1
  25.0 2.0 %collective-permute-start.1 = (bf16[4,2,2,4,8,640]{5,4,3,2,1,0:T(8,128)(2,1)S(1)}, bf16[4,2,2,4,8,640]{5,4,3,2,1,0:T(8,128)(2,1)S(1)}, u32[]{:S(2)}, u32[]{:S(2)}) collective-permute-start(bf16[4,2,2,4,8,640]{5,4,3,2,1,0:T(8,128)(2,1)S(1)} %get-tuple-element.34), channel_id=1, source_target_pairs={{0,2},{2,0},{4,6},{6,4},{8,10},{10,8},{12,14},{14,12},{1,3},{3,1},... | collective-permute-start | bytes 1966088 | tf_op jit(solution)/shard_map/ppermute | solution.py:567
  27.0 0.7 slice_bitcast_fusion.1
  27.6 24.5 %collective-permute-done.1 = bf16[4,2,2,4,8,640]{5,4,3,2,1,0:T(8,128)(2,1)S(1)} collective-permute-done((bf16[4,2,2,4,8,640]{5,4,3,2,1,0:T(8,128)(2,1)S(1)}, bf16[4,2,2,4,8,640]{5,4,3,2,1,0:T(8,128)(2,1)S(1)}, u32[]{:S(2)}, u32[]{:S(2)}) %collective-permute-start.1) | collective-permute-done | bytes 655392 | tf_op jit(solution)/shard_map/ppermute | solution.py:567
  52.2 0.7 slice_bitcast_fusion
  52.9 0.7 pad_maximum_fusion.2
  53.6 2.1 %collective-permute-start.2 = (bf16[2,2,32,640]{3,2,1,0:T(8,128)(2,1)}, bf16[2,2,32,640]{3,2,1,0:T(8,128)(2,1)S(1)}, u32[]{:S(2)}, u32[]{:S(2)}) collective-permute-start(bf16[2,2,32,640]{3,2,1,0:T(8,128)(2,1)} %pad_maximum_fusion.2), channel_id=1, source_target_pairs={{0,4},{2,6},{4,0},{6,2},{8,12},{10,14},{12,8},{14,10},{1,5},{3,7},... | collective-permute-start | bytes 491528 | tf_op jit(solution)/shard_map/ppermute | solution.py:567
  55.7 0.7 pad_maximum_fusion.6
  56.4 0.7 pad_maximum_fusion.7
  57.1 1.9 %collective-permute-start.14 = (bf16[2,2,32,640]{3,2,1,0:T(8,128)(2,1)}, bf16[2,2,32,640]{3,2,1,0:T(8,128)(2,1)S(1)}, u32[]{:S(2)}, u32[]{:S(2)}) collective-permute-start(bf16[2,2,32,640]{3,2,1,0:T(8,128)(2,1)} %pad_maximum_fusion.7), channel_id=1, source_target_pairs={{0,8},{2,10},{4,12},{6,14},{8,0},{10,2},{12,4},{14,6},{1,9},{3,11}... | collective-permute-start | bytes 491528 | tf_op jit(solution)/shard_map/ppermute | solution.py:567
  59.0 0.7 pad_maximum_fusion.8
  59.6 2.5 %collective-permute-start.15 = (bf16[2,2,32,640]{3,2,1,0:T(8,128)(2,1)}, bf16[2,2,32,640]{3,2,1,0:T(8,128)(2,1)S(1)}, u32[]{:S(2)}, u32[]{:S(2)}) collective-permute-start(bf16[2,2,32,640]{3,2,1,0:T(8,128)(2,1)} %pad_maximum_fusion.8), channel_id=1, source_target_pairs={{0,12},{2,14},{4,8},{6,10},{8,4},{10,6},{12,0},{14,2},{1,13},{3,15... | collective-permute-start | bytes 491528 | tf_op jit(solution)/shard_map/ppermute | solution.py:567
  62.2 0.7 pad_maximum_fusion.3
  62.8 1.0 collective-permute-start.3
  63.9 6.5 %shard_map.110 = (bf16[4,512,512]{2,1,0:T(8,128)(2,1)S(1)}, bf16[4,512,512]{2,1,0:T(8,128)(2,1)}) custom-call(s32[1]{0:T(128)} %bitcast.core, bf16[8,2,2,2,32,640]{5,4,3,2,1,0:T(8,128)(2,1)S(1)} %bitcast.87), custom_call_target="tpu_custom_call" | custom-call | tf_op jit(solution)/shard_map/pallas_call | solution.py:187
  70.4 3.3 %collective-permute-done.13.refs_1_ = bf16[2,2,32,640]{3,2,1,0:T(8,128)(2,1)S(1)} collective-permute-done((bf16[2,2,32,640]{3,2,1,0:T(8,128)(2,1)}, bf16[2,2,32,640]{3,2,1,0:T(8,128)(2,1)S(1)}, u32[]{:S(2)}, u32[]{:S(2)}) %collective-permute-start.13) | collective-permute-done | bytes 163872 | tf_op jit(solution)/shard_map/ppermute | solution.py:567
  73.6 11.7 %collective-permute-done.14.refs_2_ = bf16[2,2,32,640]{3,2,1,0:T(8,128)(2,1)S(1)} collective-permute-done((bf16[2,2,32,640]{3,2,1,0:T(8,128)(2,1)}, bf16[2,2,32,640]{3,2,1,0:T(8,128)(2,1)S(1)}, u32[]{:S(2)}, u32[]{:S(2)}) %collective-permute-start.14) | collective-permute-done | bytes 163872 | tf_op jit(solution)/shard_map/ppermute | solution.py:567
  85.3 0.9 shard_map.114
  86.2 0.1 collective-permute-start.16
  86.3 1.4 collective-permute-start.4
  87.7 0.1 pad_add_fusion.scalars
  87.8 0.7 pad_maximum_fusion.1.refs_0_.refs_1_
  88.5 2.3 %shard_map.115.refs_0_ = bf16[256,1024]{1,0:T(8,128)(2,1)} custom-call(s32[2]{0:T(128)S(1)} %pad_add_fusion.scalars, bf16[256,640]{1,0:T(8,128)(2,1)S(1)} %get-tuple-element.31.near, bf16[256,640]{1,0:T(8,128)(2,1)S(1)} %collective-permute-done.16.far, bf16[1280,1024]{1,0:T(8,128)(2,1)S(1)} %copy-done, f32[1,1024]{1,0:T(1,128)S(1)} %bitcast.108), custom_call_target="tpu_custom_call" | custom-call | tf_op jit(solution)/shard_map/pallas_call | solution.py:300
  90.9 5.1 %collective-permute-done.3.refs_2_.refs_3_ = bf16[2,2,32,640]{3,2,1,0:T(8,128)(2,1)} collective-permute-done((bf16[2,2,32,640]{3,2,1,0:T(8,128)(2,1)}, bf16[2,2,32,640]{3,2,1,0:T(8,128)(2,1)}, u32[]{:S(2)}, u32[]{:S(2)}) %collective-permute-start.3) | collective-permute-done | bytes 163872 | tf_op jit(solution)/shard_map/ppermute | solution.py:567
  96.0 0.7 copy-done.9
  96.6 6.7 %all-to-all-start.1 = ((bf16[8,4,8,1024]{3,2,1,0:T(8,128)(2,1)}), bf16[8,4,8,1024]{3,2,1,0:T(8,128)(2,1)S(1)}, u32[]{:S(2)}, u32[]{:S(2)}) async-start(bf16[8,4,8,1024]{3,2,1,0:T(8,128)(2,1)} %bitcast.113), calls=%async_computation.1 | async-start | bytes 1048576 | tf_op jit(solution)/shard_map/all_to_all | solution.py:571
  103.3 3.1 %shard_map.112 = (bf16[256,640]{1,0:T(8,128)(2,1)S(1)}, bf16[256,640]{1,0:T(8,128)(2,1)S(1)}) custom-call(s32[1]{0:T(128)} %bitcast.1.place, bf16[4,512,512]{2,1,0:T(8,128)(2,1)} %get-tuple-element.19.weights, bf16[2,2,32,640]{3,2,1,0:T(8,128)(2,1)} %pad_maximum_fusion.1.refs_0_.refs_1_, bf16[2,2,32,640]{3,2,1,0:T(8,128)(2,1)} %copy-done.8, ...), custom_call_target="tpu_custom_call" | custom-call | tf_op jit(solution)/shard_map/pallas_call | solution.py:258
  106.4 0.1 collective-permute-start.5
  106.5 1.6 %collective-permute-done.5.far = bf16[256,640]{1,0:T(8,128)(2,1)S(1)} collective-permute-done((bf16[256,640]{1,0:T(8,128)(2,1)S(1)}, bf16[256,640]{1,0:T(8,128)(2,1)S(1)}, u32[]{:S(2)}, u32[]{:S(2)}) %collective-permute-start.5) | collective-permute-done | bytes 327712 | tf_op jit(solution)/shard_map/ppermute | solution.py:567
  108.1 2.3 %shard_map.113 = (bf16[1,32,1024]{2,1,0:T(8,128)(2,1)S(1)}, bf16[1,32,1024]{2,1,0:T(8,128)(2,1)}, bf16[1,32,1024]{2,1,0:T(8,128)(2,1)}, bf16[1,32,1024]{2,1,0:T(...) custom-call(s32[2]{0:T(128)S(1)} %pad_add_fusion.scalars, ...), custom_call_target="tpu_custom_call" | custom-call | tf_op jit(solution)/shard_map/pallas_call | solution.py:300
  110.4 2.0 %collective-permute-start.6 = (bf16[1,32,1024]{2,1,0:T(8,128)(2,1)}, bf16[1,32,1024]{2,1,0:T(8,128)(2,1)S(1)}, u32[]{:S(2)}, u32[]{:S(2)}) collective-permute-start(bf16[1,32,1024]{2,1,0:T(8,128)(2,1)} %get-tuple-element.23), channel_id=1, source_target_pairs={{0,2},{2,0},{4,6},{6,4},{8,10},{10,8},{12,14},{14,12},{1,3},{3,1},... | collective-permute-start | bytes 196616 | tf_op jit(solution)/shard_map/ppermute | solution.py:567
  112.4 1.5 %collective-permute-start.7 = (bf16[1,32,1024]{2,1,0:T(8,128)(2,1)}, bf16[1,32,1024]{2,1,0:T(8,128)(2,1)S(1)}, u32[]{:S(2)}, u32[]{:S(2)}) collective-permute-start(bf16[1,32,1024]{2,1,0:T(8,128)(2,1)} %get-tuple-element.24), channel_id=1, source_target_pairs={{0,4},{2,6},{4,0},{6,2},{8,12},{10,14},{12,8},{14,10},{1,5},{3,7},... | collective-permute-start | bytes 196616 | tf_op jit(solution)/shard_map/ppermute | solution.py:567
  113.9 2.9 %collective-permute-start.9 = (bf16[1,32,1024]{2,1,0:T(8,128)(2,1)S(1)}, bf16[1,32,1024]{2,1,0:T(8,128)(2,1)S(1)}, u32[]{:S(2)}, u32[]{:S(2)}) collective-permute-start(bf16[1,32,1024]{2,1,0:T(8,128)(2,1)S(1)} %get-tuple-element.26), channel_id=1, source_target_pairs={{0,8},{2,10},{4,12},{6,14},{8,0},{10,2},{12,4},{14,6},{1,9},{3,11}... | collective-permute-start | bytes 196616 | tf_op jit(solution)/shard_map/ppermute | solution.py:567
  116.8 1.4 all-to-all-done.1.refs_1_.refs_8_
  118.3 3.2 %collective-permute-start.17 = (bf16[2,4,8,1024]{3,2,1,0:T(8,128)(2,1)S(1)}, bf16[2,4,8,1024]{3,2,1,0:T(8,128)(2,1)S(1)}, u32[]{:S(2)}, u32[]{:S(2)}) collective-permute-start(bf16[2,4,8,1024]{3,2,1,0:T(8,128)(2,1)S(1)} %get-tuple-element.62), channel_id=1, source_target_pairs={{0,2},{2,4},{4,6},{6,8},{8,10},{10,12},{12,14},{1,3},{3,5},{5,7},{... | collective-permute-start | bytes 393224 | tf_op jit(solution)/shard_map/ppermute | solution.py:563
  121.4 1.5 %collective-permute-start.18 = (bf16[2,4,8,1024]{3,2,1,0:T(8,128)(2,1)S(1)}, bf16[2,4,8,1024]{3,2,1,0:T(8,128)(2,1)S(1)}, u32[]{:S(2)}, u32[]{:S(2)}) collective-permute-start(bf16[2,4,8,1024]{3,2,1,0:T(8,128)(2,1)S(1)} %get-tuple-element.61), channel_id=1, source_target_pairs={{2,0},{4,2},{6,4},{8,6},{10,8},{12,10},{14,12},{3,1},{5,3},{7,5},{... | collective-permute-start | bytes 393224 | tf_op jit(solution)/shard_map/ppermute | solution.py:563
  122.9 1.7 %collective-permute-start.10 = (bf16[1,32,1024]{2,1,0:T(8,128)(2,1)S(1)}, bf16[1,32,1024]{2,1,0:T(8,128)(2,1)S(1)}, u32[]{:S(2)}, u32[]{:S(2)}) collective-permute-start(bf16[1,32,1024]{2,1,0:T(8,128)(2,1)S(1)} %get-tuple-element.27), channel_id=1, source_target_pairs={{0,10},{2,8},{4,14},{6,12},{8,2},{10,0},{12,6},{14,4},{1,11},{3,9}... | collective-permute-start | bytes 196616 | tf_op jit(solution)/shard_map/ppermute | solution.py:567
  124.7 3.0 %collective-permute-start.11 = (bf16[1,32,1024]{2,1,0:T(8,128)(2,1)S(1)}, bf16[1,32,1024]{2,1,0:T(8,128)(2,1)S(1)}, u32[]{:S(2)}, u32[]{:S(2)}) collective-permute-start(bf16[1,32,1024]{2,1,0:T(8,128)(2,1)S(1)} %get-tuple-element.28), channel_id=1, source_target_pairs={{0,12},{2,14},{4,8},{6,10},{8,4},{10,6},{12,0},{14,2},{1,13},{3,15... | collective-permute-start | bytes 196616 | tf_op jit(solution)/shard_map/ppermute | solution.py:567
  127.7 1.9 %collective-permute-start.12 = (bf16[1,32,1024]{2,1,0:T(8,128)(2,1)S(1)}, bf16[1,32,1024]{2,1,0:T(8,128)(2,1)S(1)}, u32[]{:S(2)}, u32[]{:S(2)}) collective-permute-start(bf16[1,32,1024]{2,1,0:T(8,128)(2,1)S(1)} %get-tuple-element.29), channel_id=1, source_target_pairs={{0,14},{2,12},{4,10},{6,8},{8,6},{10,4},{12,2},{14,0},{1,15},{3,13... | collective-permute-start | bytes 196616 | tf_op jit(solution)/shard_map/ppermute | solution.py:567
  129.7 2.9 %collective-permute-done.10 = bf16[1,32,1024]{2,1,0:T(8,128)(2,1)S(1)} collective-permute-done((bf16[1,32,1024]{2,1,0:T(8,128)(2,1)S(1)}, bf16[1,32,1024]{2,1,0:T(8,128)(2,1)S(1)}, u32[]{:S(2)}, u32[]{:S(2)}) %collective-permute-start.10) | collective-permute-done | bytes 65568 | tf_op jit(solution)/shard_map/ppermute | solution.py:567
  132.6 2.2 %collective-permute-done.12 = bf16[1,32,1024]{2,1,0:T(8,128)(2,1)S(1)} collective-permute-done((bf16[1,32,1024]{2,1,0:T(8,128)(2,1)S(1)}, bf16[1,32,1024]{2,1,0:T(8,128)(2,1)S(1)}, u32[]{:S(2)}, u32[]{:S(2)}) %collective-permute-start.12) | collective-permute-done | bytes 65568 | tf_op jit(solution)/shard_map/ppermute | solution.py:567
  134.8 0.1 shard_map.118
  134.8 0.1 collective-permute-start.20
  134.9 0.1 shard_map.117
  135.0 0.5 collective-permute-start.19
  135.6 0.5 collective-permute-done.20.refs_12_
  136.1 0.4 collective-permute-done.19.refs_11_
  136.5 0.2 broadcast_in_dim.21.refs_13_
  136.7 8.6 %shard_map.119 = bf16[2048,256]{1,0:T(8,128)(2,1)} custom-call(s32[2]{0:T(128)S(1)} %pad_add_fusion.scalars, bf16[1,4,8,1024]{3,2,1,0:T(8,128)(2,1)S(1)} %bitcast.93, bf16[1,4,8,1024]{3,2,1,0:T(8,128)(2,1)S(1)} %bitcast.95, bf16[1,4,8,1024]{3,2,1,0:T(8,128)(2,1)S(1)} %bitcast.97, bf16[1,4,8,1024]{3,2,1,0:T(8,128)(2,1)S(1)} %bitcast.99, ...), custom_call_target="tpu_custom_call" | custom-call | tf_op jit(solution)/shard_map/pallas_call | solution.py:514
  (40 shorter events, 0.2 us)
Async XLA Ops:
  2.9 60.9 %all-to-all-start = ((bf16[16,2,2,32,640]{4,3,2,1,0:T(8,128)(2,1)}), bf16[16,2,2,32,640]{4,3,2,1,0:T(8,128)(2,1)S(1)}, u32[]{:S(2)}, u32[]{:S(2)}) async-start(bf16[16,2,2,32,640]{4,3,2,1,0:T(8,128)(2,1)} %bitcast.112), calls=%async_computation | async-start | bytes 5242880 | tf_op jit(solution)/shard_map/all_to_all | solution.py:571
  10.3 1.3 copy-start.1
  11.7 1.3 copy-start.2
  13.0 1.3 copy-start.3
  19.8 2.5 %collective-permute-start = (bf16[4,128,640]{2,1,0:T(8,128)(2,1)}, bf16[4,128,640]{2,1,0:T(8,128)(2,1)}, u32[]{:S(2)}, u32[]{:S(2)}) collective-permute-start(bf16[4,128,640]{2,1,0:T(8,128)(2,1)} %get-tuple-element.44), channel_id=1, source_target_pairs={{0,1},{1,0},{2,3},{3,2},{4,5},{5,4},{6,7},{7,6},{8,9},{9,8},{10,11... | collective-permute-start | bytes 1966088 | tf_op jit(solution)/shard_map/ppermute | solution.py:567
  25.0 27.2 %collective-permute-start.1 = (bf16[4,2,2,4,8,640]{5,4,3,2,1,0:T(8,128)(2,1)S(1)}, bf16[4,2,2,4,8,640]{5,4,3,2,1,0:T(8,128)(2,1)S(1)}, u32[]{:S(2)}, u32[]{:S(2)}) collective-permute-start(bf16[4,2,2,4,8,640]{5,4,3,2,1,0:T(8,128)(2,1)S(1)} %get-tuple-element.34), channel_id=1, source_target_pairs={{0,2},{2,0},{4,6},{6,4},{8,10},{10,8},{12,14},{14,12},{1,3},{3,1},... | collective-permute-start | bytes 1966088 | tf_op jit(solution)/shard_map/ppermute | solution.py:567
  53.6 37.3 %collective-permute-start.2 = (bf16[2,2,32,640]{3,2,1,0:T(8,128)(2,1)}, bf16[2,2,32,640]{3,2,1,0:T(8,128)(2,1)S(1)}, u32[]{:S(2)}, u32[]{:S(2)}) collective-permute-start(bf16[2,2,32,640]{3,2,1,0:T(8,128)(2,1)} %pad_maximum_fusion.2), channel_id=1, source_target_pairs={{0,4},{2,6},{4,0},{6,2},{8,12},{10,14},{12,8},{14,10},{1,5},{3,7},... | collective-permute-start | bytes 491528 | tf_op jit(solution)/shard_map/ppermute | solution.py:567
  56.4 17.3 %collective-permute-start.13 = (bf16[2,2,32,640]{3,2,1,0:T(8,128)(2,1)}, bf16[2,2,32,640]{3,2,1,0:T(8,128)(2,1)S(1)}, u32[]{:S(2)}, u32[]{:S(2)}) collective-permute-start(bf16[2,2,32,640]{3,2,1,0:T(8,128)(2,1)} %pad_maximum_fusion.6), channel_id=1, source_target_pairs={{0,4},{2,6},{4,0},{6,2},{8,12},{10,14},{12,8},{14,10},{1,5},{3,7},... | collective-permute-start | bytes 491528 | tf_op jit(solution)/shard_map/ppermute | solution.py:567
  57.1 28.2 %collective-permute-start.14 = (bf16[2,2,32,640]{3,2,1,0:T(8,128)(2,1)}, bf16[2,2,32,640]{3,2,1,0:T(8,128)(2,1)S(1)}, u32[]{:S(2)}, u32[]{:S(2)}) collective-permute-start(bf16[2,2,32,640]{3,2,1,0:T(8,128)(2,1)} %pad_maximum_fusion.7), channel_id=1, source_target_pairs={{0,8},{2,10},{4,12},{6,14},{8,0},{10,2},{12,4},{14,6},{1,9},{3,11}... | collective-permute-start | bytes 491528 | tf_op jit(solution)/shard_map/ppermute | solution.py:567
  59.6 25.7 %collective-permute-start.15 = (bf16[2,2,32,640]{3,2,1,0:T(8,128)(2,1)}, bf16[2,2,32,640]{3,2,1,0:T(8,128)(2,1)S(1)}, u32[]{:S(2)}, u32[]{:S(2)}) collective-permute-start(bf16[2,2,32,640]{3,2,1,0:T(8,128)(2,1)} %pad_maximum_fusion.8), channel_id=1, source_target_pairs={{0,12},{2,14},{4,8},{6,10},{8,4},{10,6},{12,0},{14,2},{1,13},{3,15... | collective-permute-start | bytes 491528 | tf_op jit(solution)/shard_map/ppermute | solution.py:567
  62.8 33.1 %collective-permute-start.3 = (bf16[2,2,32,640]{3,2,1,0:T(8,128)(2,1)}, bf16[2,2,32,640]{3,2,1,0:T(8,128)(2,1)}, u32[]{:S(2)}, u32[]{:S(2)}) collective-permute-start(bf16[2,2,32,640]{3,2,1,0:T(8,128)(2,1)} %pad_maximum_fusion.3), channel_id=1, source_target_pairs={{0,8},{2,10},{4,12},{6,14},{8,0},{10,2},{12,4},{14,6},{1,9},{3,11}... | collective-permute-start | bytes 491528 | tf_op jit(solution)/shard_map/ppermute | solution.py:567
  63.8 22.4 %copy-start.12 = (bf16[1,2,32,640]{3,2,1,0:T(8,128)(2,1)S(1)}, bf16[1,2,32,640]{3,2,1,0:T(8,128)(2,1)}, u32[]{:S(2)}) copy-start(bf16[1,2,32,640]{3,2,1,0:T(8,128)(2,1)} %get-tuple-element.57) | copy-start | bytes 245764
  85.3 1.0 copy-start.10
  85.3 2.5 %copy-start.11 = (bf16[1,2,32,640]{3,2,1,0:T(8,128)(2,1)S(1)}, bf16[1,2,32,640]{3,2,1,0:T(8,128)(2,1)}, u32[]{:S(2)}) copy-start(bf16[1,2,32,640]{3,2,1,0:T(8,128)(2,1)} %get-tuple-element.60) | copy-start | bytes 245764
  85.3 3.2 %copy-start = (bf16[1280,1024]{1,0:T(8,128)(2,1)S(1)}, bf16[1280,1024]{1,0:T(8,128)(2,1)}, u32[]{:S(2)}) copy-start(bf16[1280,1024]{1,0:T(8,128)(2,1)} %proj_weight.3) | copy-start | bytes 7864324
  85.3 3.2 %copy-start.5 = (f32[1024]{0:T(1024)S(1)}, f32[1024]{0:T(1024)}, u32[]{:S(2)}) copy-start(f32[1024]{0:T(1024)} %param.17) | copy-start | bytes 12292
  86.2 2.3 %collective-permute-start.16 = (bf16[256,640]{1,0:T(8,128)(2,1)S(1)}, bf16[256,640]{1,0:T(8,128)(2,1)S(1)}, u32[]{:S(2)}, u32[]{:S(2)}) collective-permute-start(bf16[256,640]{1,0:T(8,128)(2,1)S(1)} %get-tuple-element.32), channel_id=1, source_target_pairs={{0,1},{1,0},{2,3},{3,2},{4,5},{5,4},{6,7},{7,6},{8,9},{9,8},{10,11... | collective-permute-start | bytes 983048 | tf_op jit(solution)/shard_map/ppermute | solution.py:567
  86.3 9.6 %collective-permute-start.4 = (bf16[2,2,32,640]{3,2,1,0:T(8,128)(2,1)S(1)}, bf16[2,2,32,640]{3,2,1,0:T(8,128)(2,1)S(1)}, u32[]{:S(2)}, u32[]{:S(2)}) collective-permute-start(bf16[2,2,32,640]{3,2,1,0:T(8,128)(2,1)S(1)} %pad_maximum_fusion.4), channel_id=1, source_target_pairs={{0,12},{2,14},{4,8},{6,10},{8,4},{10,6},{12,0},{14,2},{1,13},{3,15... | collective-permute-start | bytes 491528 | tf_op jit(solution)/shard_map/ppermute | solution.py:567
  90.9 5.1 %copy-start.8 = (bf16[2,2,32,640]{3,2,1,0:T(8,128)(2,1)}, bf16[2,2,32,640]{3,2,1,0:T(8,128)(2,1)S(1)}, u32[]{:S(2)}) copy-start(bf16[2,2,32,640]{3,2,1,0:T(8,128)(2,1)S(1)} %collective-permute-done.2.refs_1_.refs_2_) | copy-start | bytes 491524
  95.9 0.7 copy-start.9
  96.6 21.6 %all-to-all-start.1 = ((bf16[8,4,8,1024]{3,2,1,0:T(8,128)(2,1)}), bf16[8,4,8,1024]{3,2,1,0:T(8,128)(2,1)S(1)}, u32[]{:S(2)}, u32[]{:S(2)}) async-start(bf16[8,4,8,1024]{3,2,1,0:T(8,128)(2,1)} %bitcast.113), calls=%async_computation.1 | async-start | bytes 1048576 | tf_op jit(solution)/shard_map/all_to_all | solution.py:571
  106.4 1.7 %collective-permute-start.5 = (bf16[256,640]{1,0:T(8,128)(2,1)S(1)}, bf16[256,640]{1,0:T(8,128)(2,1)S(1)}, u32[]{:S(2)}, u32[]{:S(2)}) collective-permute-start(bf16[256,640]{1,0:T(8,128)(2,1)S(1)} %get-tuple-element.21), channel_id=1, source_target_pairs={{0,1},{1,0},{2,3},{3,2},{4,5},{5,4},{6,7},{7,6},{8,9},{9,8},{10,11... | collective-permute-start | bytes 983048 | tf_op jit(solution)/shard_map/ppermute | solution.py:567
  110.4 11.0 %collective-permute-start.6 = (bf16[1,32,1024]{2,1,0:T(8,128)(2,1)}, bf16[1,32,1024]{2,1,0:T(8,128)(2,1)S(1)}, u32[]{:S(2)}, u32[]{:S(2)}) collective-permute-start(bf16[1,32,1024]{2,1,0:T(8,128)(2,1)} %get-tuple-element.23), channel_id=1, source_target_pairs={{0,2},{2,0},{4,6},{6,4},{8,10},{10,8},{12,14},{14,12},{1,3},{3,1},... | collective-permute-start | bytes 196616 | tf_op jit(solution)/shard_map/ppermute | solution.py:567
  112.4 10.5 %collective-permute-start.7 = (bf16[1,32,1024]{2,1,0:T(8,128)(2,1)}, bf16[1,32,1024]{2,1,0:T(8,128)(2,1)S(1)}, u32[]{:S(2)}, u32[]{:S(2)}) collective-permute-start(bf16[1,32,1024]{2,1,0:T(8,128)(2,1)} %get-tuple-element.24), channel_id=1, source_target_pairs={{0,4},{2,6},{4,0},{6,2},{8,12},{10,14},{12,8},{14,10},{1,5},{3,7},... | collective-permute-start | bytes 196616 | tf_op jit(solution)/shard_map/ppermute | solution.py:567
  113.9 10.8 %collective-permute-start.8 = (bf16[1,32,1024]{2,1,0:T(8,128)(2,1)}, bf16[1,32,1024]{2,1,0:T(8,128)(2,1)S(1)}, u32[]{:S(2)}, u32[]{:S(2)}) collective-permute-start(bf16[1,32,1024]{2,1,0:T(8,128)(2,1)} %get-tuple-element.25), channel_id=1, source_target_pairs={{0,6},{2,4},{4,2},{6,0},{8,14},{10,12},{12,10},{14,8},{1,7},{3,5},... | collective-permute-start | bytes 196616 | tf_op jit(solution)/shard_map/ppermute | solution.py:567
  113.9 22.8 %copy-start.4 = (bf16[3,3,256,256]{3,2,1,0:T(8,128)(2,1)S(1)}, bf16[3,3,256,256]{3,2,1,0:T(8,128)(2,1)}, u32[]{:S(2)}) copy-start(bf16[3,3,256,256]{3,2,1,0:T(8,128)(2,1)} %param.18) | copy-start | bytes 3538948
  113.9 22.8 %copy-start.6 = (f32[256]{0:T(256)S(1)}, f32[256]{0:T(256)}, u32[]{:S(2)}) copy-start(f32[256]{0:T(256)} %param.19) | copy-start | bytes 3076
  113.9 22.8 %copy-start.7 = (f32[256]{0:T(256)S(1)}, f32[256]{0:T(256)}, u32[]{:S(2)}) copy-start(f32[256]{0:T(256)} %param.21) | copy-start | bytes 3076
  113.9 13.8 %collective-permute-start.9 = (bf16[1,32,1024]{2,1,0:T(8,128)(2,1)S(1)}, bf16[1,32,1024]{2,1,0:T(8,128)(2,1)S(1)}, u32[]{:S(2)}, u32[]{:S(2)}) collective-permute-start(bf16[1,32,1024]{2,1,0:T(8,128)(2,1)S(1)} %get-tuple-element.26), channel_id=1, source_target_pairs={{0,8},{2,10},{4,12},{6,14},{8,0},{10,2},{12,4},{14,6},{1,9},{3,11}... | collective-permute-start | bytes 196616 | tf_op jit(solution)/shard_map/ppermute | solution.py:567
  118.3 16.6 %collective-permute-start.17 = (bf16[2,4,8,1024]{3,2,1,0:T(8,128)(2,1)S(1)}, bf16[2,4,8,1024]{3,2,1,0:T(8,128)(2,1)S(1)}, u32[]{:S(2)}, u32[]{:S(2)}) collective-permute-start(bf16[2,4,8,1024]{3,2,1,0:T(8,128)(2,1)S(1)} %get-tuple-element.62), channel_id=1, source_target_pairs={{0,2},{2,4},{4,6},{6,8},{8,10},{10,12},{12,14},{1,3},{3,5},{5,7},{... | collective-permute-start | bytes 393224 | tf_op jit(solution)/shard_map/ppermute | solution.py:563
  121.4 13.5 %collective-permute-start.18 = (bf16[2,4,8,1024]{3,2,1,0:T(8,128)(2,1)S(1)}, bf16[2,4,8,1024]{3,2,1,0:T(8,128)(2,1)S(1)}, u32[]{:S(2)}, u32[]{:S(2)}) collective-permute-start(bf16[2,4,8,1024]{3,2,1,0:T(8,128)(2,1)S(1)} %get-tuple-element.61), channel_id=1, source_target_pairs={{2,0},{4,2},{6,4},{8,6},{10,8},{12,10},{14,12},{3,1},{5,3},{7,5},{... | collective-permute-start | bytes 393224 | tf_op jit(solution)/shard_map/ppermute | solution.py:563
  122.9 9.7 %collective-permute-start.10 = (bf16[1,32,1024]{2,1,0:T(8,128)(2,1)S(1)}, bf16[1,32,1024]{2,1,0:T(8,128)(2,1)S(1)}, u32[]{:S(2)}, u32[]{:S(2)}) collective-permute-start(bf16[1,32,1024]{2,1,0:T(8,128)(2,1)S(1)} %get-tuple-element.27), channel_id=1, source_target_pairs={{0,10},{2,8},{4,14},{6,12},{8,2},{10,0},{12,6},{14,4},{1,11},{3,9}... | collective-permute-start | bytes 196616 | tf_op jit(solution)/shard_map/ppermute | solution.py:567
  124.7 7.9 %collective-permute-start.11 = (bf16[1,32,1024]{2,1,0:T(8,128)(2,1)S(1)}, bf16[1,32,1024]{2,1,0:T(8,128)(2,1)S(1)}, u32[]{:S(2)}, u32[]{:S(2)}) collective-permute-start(bf16[1,32,1024]{2,1,0:T(8,128)(2,1)S(1)} %get-tuple-element.28), channel_id=1, source_target_pairs={{0,12},{2,14},{4,8},{6,10},{8,4},{10,6},{12,0},{14,2},{1,13},{3,15... | collective-permute-start | bytes 196616 | tf_op jit(solution)/shard_map/ppermute | solution.py:567
  127.7 7.1 %collective-permute-start.12 = (bf16[1,32,1024]{2,1,0:T(8,128)(2,1)S(1)}, bf16[1,32,1024]{2,1,0:T(8,128)(2,1)S(1)}, u32[]{:S(2)}, u32[]{:S(2)}) collective-permute-start(bf16[1,32,1024]{2,1,0:T(8,128)(2,1)S(1)} %get-tuple-element.29), channel_id=1, source_target_pairs={{0,14},{2,12},{4,10},{6,8},{8,6},{10,4},{12,2},{14,0},{1,15},{3,13... | collective-permute-start | bytes 196616 | tf_op jit(solution)/shard_map/ppermute | solution.py:567
  134.8 1.3 collective-permute-start.20
  135.0 1.4 collective-permute-start.19

commit v6 on v5

--- a/solution.py
+++ b/solution.py
@@ -199,14 +199,14 @@
             for part in range(parts)
         ],
         out_shape=[
-            (pltpu.HBM if part else pltpu.VMEM)((heads, rows, rows), jnp.bfloat16) for part in range(parts)
+            pltpu.VMEM((heads, rows, rows), jnp.bfloat16) for part in range(parts)
         ],
         compiler_params=params(2),
     )(core.reshape(1), pair)
 
 
 def mix_kernel(fetched, place, weights, *refs):
-    pieces, (near, far, value, held, held_weights, arrived) = refs[:-6], refs[-6:]
+    pieces, (near, far, value, held, arrived) = refs[:-5], refs[-5:]
     each, cores, rows, features = pieces[0].shape
     half = value.shape[0] // cores
     heads = features // HEAD_DIM
@@ -214,10 +214,6 @@
     if fetched:
         copies = [
             pltpu.make_async_copy(piece, held.at[k], arrived.at[k]) for k, piece in enumerate(pieces)
-        ]
-        copies += [
-            pltpu.make_async_copy(weights.at[head], held_weights.at[head], arrived.at[len(pieces) + head])
-            for head in range(heads)
         ]
     for copy in copies:
         copy.start()
@@ -231,12 +227,10 @@
                 value[pl.ds(core * half + at, rows), :] = piece[j, core].astype(value.dtype)
     mixed = []
     for head in range(heads):
-        if fetched:
-            copies[len(pieces) + head].wait()
         lanes = slice(head_start(head), head_start(head) + SPAN)
         mixed.append(
             jnp.dot(
-                (held_weights if fetched else weights)[head], value[:, lanes].astype(jnp.bfloat16),
+                weights[head], value[:, lanes].astype(jnp.bfloat16),
                 preferred_element_type=jnp.float32,
             )
         )
@@ -252,19 +246,17 @@
     held = jnp.float32 if pieces[0].shape[2] % EDGE else jnp.bfloat16
     source = pl.BlockSpec(memory_space=pltpu.HBM if fetched else pltpu.VMEM)
     if fetched:
-        weights, *pieces = [
-            pltpu.with_memory_space_constraint(value, pltpu.HBM) for value in [weights] + pieces
-        ]
+        pieces = [pltpu.with_memory_space_constraint(piece, pltpu.HBM) for piece in pieces]
     return pl.pallas_call(
         functools.partial(mix_kernel, fetched),
-        in_specs=[pl.BlockSpec(memory_space=pltpu.SMEM)] + [source] * (1 + len(pieces)),
+        in_specs=[pl.BlockSpec(memory_space=pltpu.SMEM), pl.BlockSpec(memory_space=pltpu.VMEM)]
+        + [source] * len(pieces),
         out_specs=[pl.BlockSpec(memory_space=pltpu.VMEM)] * 2,
         out_shape=[result, result],
         scratch_shapes=[
             pltpu.VMEM((rows, features), held),
             pltpu.VMEM((len(pieces),) + pieces[0].shape, jnp.bfloat16),
-            pltpu.VMEM(weights.shape if fetched else (1, EDGE, LANES), jnp.bfloat16),
-            pltpu.SemaphoreType.DMA((len(pieces) + heads,)),
+            pltpu.SemaphoreType.DMA((len(pieces),)),
         ],
         compiler_params=params(),
     )(

time: 146 us -> 146 us (level)
  local copies, waits for them, and re-layouts: 7.42 us -> 10.3 us
  Pallas kernels: 31.3 us -> 29.1 us
    unnamed x26 -> x30, local copies, waits for them, and re-layouts: 4.64 us -> 7.56 us
  transfers between devices with their start and end apart: 23 -> 23, of which waited for: 11 -> 11; matrix products, arithmetic and copies ran while one was open for 6% -> 6% of each run, Pallas kernels for 14% -> 12%
where the time goes in v6:
time: 146 us
  waiting for transfers between devices  54.9 us (38%)
  starting transfers between devices  44.3 us (30%)
  Pallas kernels  29.1 us (20%)
  local copies, waits for them, and re-layouts  10.3 us (7%)
  other arithmetic  6.78 us (5%)
    ppermute x19, waiting for transfers between devices, swapped(): lax.ppermute(value, axis, [(i, i ^ by) for i in range(lax.axis_size(axis))])  54.1 us
    ppermute x19, starting transfers between devices, swapped(): lax.ppermute(value, axis, [(i, i ^ by) for i in range(lax.axis_size(axis))])  25.6 us
    all_to_all x2, starting transfers between devices, exchanged(): return lax.all_to_all(value, axes, split_axis=0, concat_axis=0, tiled=True)  14 us
    pallas_call x1, Pallas kernels, convolve_twice(): pl.pallas_call(functools.partial(conv_kernel, rows, cols, len(middles)),...  8.58 us
    unnamed x30, local copies, waits for them, and re-layouts  7.56 us
    pallas_call x1, Pallas kernels, index_weights(): pl.pallas_call(functools.partial(weights_kernel, tokens), grid=(parts, he...  5.49 us
    ppermute x2, starting transfers between devices, shifted(): return lax.ppermute(value, axis, pairs)  4.65 us
    pallas_call x2, Pallas kernels, project(): pl.pallas_call(functools.partial(project_kernel, places, inner), in_specs...  4.6 us
  transfers between devices with their start and end apart: 23, of which 11 were waited for; matrix products, arithmetic and copies ran while one was open for 6% of the time, Pallas kernels for 12%

profile of v6, /device:TPU:0, one launch (start us, length us, event | category | flops | bytes accessed | tf_op | source)
XLA Modules:
  0.0 145.9 jit_solution(3194773539365938124)
XLA Ops:
  0.0 3.0 %shard_map.109 = bf16[8,2,2,2,32,640]{5,4,3,2,1,0:T(8,128)(2,1)} custom-call(bf16[4,128,1280]{2,1,0:T(8,128)(2,1)} %bitcast.114, bf16[4,128,1280]{2,1,0:T(8,128)(2,1)} %bitcast.115), custom_call_target="tpu_custom_call" | custom-call | tf_op jit(solution)/shard_map/pallas_call | solution.py:131
  3.0 7.4 %all-to-all-start = ((bf16[16,2,2,32,640]{4,3,2,1,0:T(8,128)(2,1)}), bf16[16,2,2,32,640]{4,3,2,1,0:T(8,128)(2,1)S(1)}, u32[]{:S(2)}, u32[]{:S(2)}) async-start(bf16[16,2,2,32,640]{4,3,2,1,0:T(8,128)(2,1)} %bitcast.112), calls=%async_computation | async-start | bytes 5242880 | tf_op jit(solution)/shard_map/all_to_all | solution.py:563
  10.4 1.3 copy-done.3
  11.7 1.3 copy-done.4
  13.1 1.3 copy-done.5
  14.4 4.5 %shard_map.111 = bf16[2,4,128,640]{3,2,1,0:T(8,128)(2,1)S(1)} custom-call(bf16[4,128,1280]{2,1,0:T(8,128)(2,1)S(1)} %bitcast.88, bf16[4,128,1280]{2,1,0:T(8,128)(2,1)S(1)} %bitcast.89, bf16[4,128,1280]{2,1,0:T(8,128)(2,1)S(1)} %bitcast.90), custom_call_target="tpu_custom_call" | custom-call | tf_op jit(solution)/shard_map/pallas_call | solution.py:83
  18.9 1.0 constant_dynamic-slice_fusion
  19.9 0.4 collective-permute-start
  20.3 2.1 %collective-permute-done = bf16[4,128,640]{2,1,0:T(8,128)(2,1)} collective-permute-done((bf16[4,128,640]{2,1,0:T(8,128)(2,1)}, bf16[4,128,640]{2,1,0:T(8,128)(2,1)}, u32[]{:S(2)}, u32[]{:S(2)}) %collective-permute-start) | collective-permute-done | bytes 655392 | tf_op jit(solution)/shard_map/ppermute | solution.py:559
  22.4 1.0 fusion.8
  23.3 1.2 fusion.14
  24.6 0.1 maximum_bitcast_fusion.2
  24.6 0.1 maximum_bitcast_fusion
  24.7 0.2 pad_maximum_fusion
  24.9 0.1 dynamic-slice_bitcast_fusion.1
  25.1 2.0 %collective-permute-start.1 = (bf16[4,2,2,4,8,640]{5,4,3,2,1,0:T(8,128)(2,1)S(1)}, bf16[4,2,2,4,8,640]{5,4,3,2,1,0:T(8,128)(2,1)S(1)}, u32[]{:S(2)}, u32[]{:S(2)}) collective-permute-start(bf16[4,2,2,4,8,640]{5,4,3,2,1,0:T(8,128)(2,1)S(1)} %get-tuple-element.34), channel_id=1, source_target_pairs={{0,2},{2,0},{4,6},{6,4},{8,10},{10,8},{12,14},{14,12},{1,3},{3,1},... | collective-permute-start | bytes 1966088 | tf_op jit(solution)/shard_map/ppermute | solution.py:559
  27.0 0.7 slice_bitcast_fusion.1
  27.7 24.5 %collective-permute-done.1 = bf16[4,2,2,4,8,640]{5,4,3,2,1,0:T(8,128)(2,1)S(1)} collective-permute-done((bf16[4,2,2,4,8,640]{5,4,3,2,1,0:T(8,128)(2,1)S(1)}, bf16[4,2,2,4,8,640]{5,4,3,2,1,0:T(8,128)(2,1)S(1)}, u32[]{:S(2)}, u32[]{:S(2)}) %collective-permute-start.1) | collective-permute-done | bytes 655392 | tf_op jit(solution)/shard_map/ppermute | solution.py:559
  52.3 0.7 slice_bitcast_fusion
  53.0 0.7 pad_maximum_fusion.2
  53.7 2.1 %collective-permute-start.2 = (bf16[2,2,32,640]{3,2,1,0:T(8,128)(2,1)}, bf16[2,2,32,640]{3,2,1,0:T(8,128)(2,1)S(1)}, u32[]{:S(2)}, u32[]{:S(2)}) collective-permute-start(bf16[2,2,32,640]{3,2,1,0:T(8,128)(2,1)} %pad_maximum_fusion.2), channel_id=1, source_target_pairs={{0,4},{2,6},{4,0},{6,2},{8,12},{10,14},{12,8},{14,10},{1,5},{3,7},... | collective-permute-start | bytes 491528 | tf_op jit(solution)/shard_map/ppermute | solution.py:559
  55.8 0.7 pad_maximum_fusion.6
  56.5 0.7 pad_maximum_fusion.7
  57.2 1.9 %collective-permute-start.14 = (bf16[2,2,32,640]{3,2,1,0:T(8,128)(2,1)}, bf16[2,2,32,640]{3,2,1,0:T(8,128)(2,1)S(1)}, u32[]{:S(2)}, u32[]{:S(2)}) collective-permute-start(bf16[2,2,32,640]{3,2,1,0:T(8,128)(2,1)} %pad_maximum_fusion.7), channel_id=1, source_target_pairs={{0,8},{2,10},{4,12},{6,14},{8,0},{10,2},{12,4},{14,6},{1,9},{3,11}... | collective-permute-start | bytes 491528 | tf_op jit(solution)/shard_map/ppermute | solution.py:559
  59.0 0.7 pad_maximum_fusion.8
  59.7 2.5 %collective-permute-start.15 = (bf16[2,2,32,640]{3,2,1,0:T(8,128)(2,1)}, bf16[2,2,32,640]{3,2,1,0:T(8,128)(2,1)S(1)}, u32[]{:S(2)}, u32[]{:S(2)}) collective-permute-start(bf16[2,2,32,640]{3,2,1,0:T(8,128)(2,1)} %pad_maximum_fusion.8), channel_id=1, source_target_pairs={{0,12},{2,14},{4,8},{6,10},{8,4},{10,6},{12,0},{14,2},{1,13},{3,15... | collective-permute-start | bytes 491528 | tf_op jit(solution)/shard_map/ppermute | solution.py:559
  62.2 0.7 pad_maximum_fusion.3
  62.9 1.0 collective-permute-start.3
  63.9 5.5 %shard_map.110 = (bf16[4,512,512]{2,1,0:T(8,128)(2,1)S(1)}, bf16[4,512,512]{2,1,0:T(8,128)(2,1)S(1)}) custom-call(s32[1]{0:T(128)} %bitcast.core, bf16[8,2,2,2,32,640]{5,4,3,2,1,0:T(8,128)(2,1)S(1)} %bitcast.87), custom_call_target="tpu_custom_call" | custom-call | tf_op jit(solution)/shard_map/pallas_call | solution.py:187
  69.4 1.3 copy-done.1
  70.8 2.9 %collective-permute-done.13.refs_1_ = bf16[2,2,32,640]{3,2,1,0:T(8,128)(2,1)S(1)} collective-permute-done((bf16[2,2,32,640]{3,2,1,0:T(8,128)(2,1)}, bf16[2,2,32,640]{3,2,1,0:T(8,128)(2,1)S(1)}, u32[]{:S(2)}, u32[]{:S(2)}) %collective-permute-start.13) | collective-permute-done | bytes 163872 | tf_op jit(solution)/shard_map/ppermute | solution.py:559
  73.7 11.7 %collective-permute-done.14.refs_2_ = bf16[2,2,32,640]{3,2,1,0:T(8,128)(2,1)S(1)} collective-permute-done((bf16[2,2,32,640]{3,2,1,0:T(8,128)(2,1)}, bf16[2,2,32,640]{3,2,1,0:T(8,128)(2,1)S(1)}, u32[]{:S(2)}, u32[]{:S(2)}) %collective-permute-start.14) | collective-permute-done | bytes 163872 | tf_op jit(solution)/shard_map/ppermute | solution.py:559
  85.4 0.8 shard_map.114
  86.2 0.1 collective-permute-start.16
  86.4 1.4 collective-permute-start.4
  87.8 0.1 pad_add_fusion.scalars
  87.9 0.7 pad_maximum_fusion.1.refs_0_.refs_1_
  88.6 2.3 %shard_map.115.refs_0_ = bf16[256,1024]{1,0:T(8,128)(2,1)} custom-call(s32[2]{0:T(128)S(1)} %pad_add_fusion.scalars, bf16[256,640]{1,0:T(8,128)(2,1)S(1)} %get-tuple-element.31.near, bf16[256,640]{1,0:T(8,128)(2,1)S(1)} %collective-permute-done.16.far, bf16[1280,1024]{1,0:T(8,128)(2,1)S(1)} %copy-done, f32[1,1024]{1,0:T(1,128)S(1)} %bitcast.108), custom_call_target="tpu_custom_call" | custom-call | tf_op jit(solution)/shard_map/pallas_call | solution.py:292
  90.9 5.1 %collective-permute-done.3.refs_2_.refs_3_ = bf16[2,2,32,640]{3,2,1,0:T(8,128)(2,1)} collective-permute-done((bf16[2,2,32,640]{3,2,1,0:T(8,128)(2,1)}, bf16[2,2,32,640]{3,2,1,0:T(8,128)(2,1)}, u32[]{:S(2)}, u32[]{:S(2)}) %collective-permute-start.3) | collective-permute-done | bytes 163872 | tf_op jit(solution)/shard_map/ppermute | solution.py:559
  96.0 0.7 copy-done.11
  96.7 6.6 %all-to-all-start.1 = ((bf16[8,4,8,1024]{3,2,1,0:T(8,128)(2,1)}), bf16[8,4,8,1024]{3,2,1,0:T(8,128)(2,1)S(1)}, u32[]{:S(2)}, u32[]{:S(2)}) async-start(bf16[8,4,8,1024]{3,2,1,0:T(8,128)(2,1)} %bitcast.113), calls=%async_computation.1 | async-start | bytes 1048576 | tf_op jit(solution)/shard_map/all_to_all | solution.py:563
  103.3 1.6 %copy-done.2 = bf16[4,512,512]{2,1,0:T(8,128)(2,1)S(1)} copy-done((bf16[4,512,512]{2,1,0:T(8,128)(2,1)S(1)}, bf16[4,512,512]{2,1,0:T(8,128)(2,1)}, u32[]{:S(2)}) %copy-start.2) | copy-done | bytes 2097176
  104.9 1.9 %shard_map.112 = (bf16[256,640]{1,0:T(8,128)(2,1)S(1)}, bf16[256,640]{1,0:T(8,128)(2,1)S(1)}) custom-call(s32[1]{0:T(128)} %bitcast.1.place, bf16[4,512,512]{2,1,0:T(8,128)(2,1)S(1)} %copy-done.2, bf16[2,2,32,640]{3,2,1,0:T(8,128)(2,1)} %pad_maximum_fusion.1.refs_0_.refs_1_, bf16[2,2,32,640]{3,2,1,0:T(8,128)(2,1)} %copy-done.10, ...), custom_call_target="tpu_custom_call" | custom-call | tf_op jit(solution)/shard_map/pallas_call | solution.py:250
  106.8 0.1 collective-permute-start.5
  106.9 1.6 %collective-permute-done.5.far = bf16[256,640]{1,0:T(8,128)(2,1)S(1)} collective-permute-done((bf16[256,640]{1,0:T(8,128)(2,1)S(1)}, bf16[256,640]{1,0:T(8,128)(2,1)S(1)}, u32[]{:S(2)}, u32[]{:S(2)}) %collective-permute-start.5) | collective-permute-done | bytes 327712 | tf_op jit(solution)/shard_map/ppermute | solution.py:559
  108.5 2.3 %shard_map.113 = (bf16[1,32,1024]{2,1,0:T(8,128)(2,1)S(1)}, bf16[1,32,1024]{2,1,0:T(8,128)(2,1)}, bf16[1,32,1024]{2,1,0:T(8,128)(2,1)}, bf16[1,32,1024]{2,1,0:T(...) custom-call(s32[2]{0:T(128)S(1)} %pad_add_fusion.scalars, ...), custom_call_target="tpu_custom_call" | custom-call | tf_op jit(solution)/shard_map/pallas_call | solution.py:292
  110.8 2.0 %collective-permute-start.6 = (bf16[1,32,1024]{2,1,0:T(8,128)(2,1)}, bf16[1,32,1024]{2,1,0:T(8,128)(2,1)S(1)}, u32[]{:S(2)}, u32[]{:S(2)}) collective-permute-start(bf16[1,32,1024]{2,1,0:T(8,128)(2,1)} %get-tuple-element.23), channel_id=1, source_target_pairs={{0,2},{2,0},{4,6},{6,4},{8,10},{10,8},{12,14},{14,12},{1,3},{3,1},... | collective-permute-start | bytes 196616 | tf_op jit(solution)/shard_map/ppermute | solution.py:559
  112.8 1.5 %collective-permute-start.7 = (bf16[1,32,1024]{2,1,0:T(8,128)(2,1)}, bf16[1,32,1024]{2,1,0:T(8,128)(2,1)S(1)}, u32[]{:S(2)}, u32[]{:S(2)}) collective-permute-start(bf16[1,32,1024]{2,1,0:T(8,128)(2,1)} %get-tuple-element.24), channel_id=1, source_target_pairs={{0,4},{2,6},{4,0},{6,2},{8,12},{10,14},{12,8},{14,10},{1,5},{3,7},... | collective-permute-start | bytes 196616 | tf_op jit(solution)/shard_map/ppermute | solution.py:559
  114.3 2.9 %collective-permute-start.9 = (bf16[1,32,1024]{2,1,0:T(8,128)(2,1)S(1)}, bf16[1,32,1024]{2,1,0:T(8,128)(2,1)S(1)}, u32[]{:S(2)}, u32[]{:S(2)}) collective-permute-start(bf16[1,32,1024]{2,1,0:T(8,128)(2,1)S(1)} %get-tuple-element.26), channel_id=1, source_target_pairs={{0,8},{2,10},{4,12},{6,14},{8,0},{10,2},{12,4},{14,6},{1,9},{3,11}... | collective-permute-start | bytes 196616 | tf_op jit(solution)/shard_map/ppermute | solution.py:559
  117.2 0.8 all-to-all-done.1.refs_1_.refs_8_
  118.0 3.2 %collective-permute-start.17 = (bf16[2,4,8,1024]{3,2,1,0:T(8,128)(2,1)S(1)}, bf16[2,4,8,1024]{3,2,1,0:T(8,128)(2,1)S(1)}, u32[]{:S(2)}, u32[]{:S(2)}) collective-permute-start(bf16[2,4,8,1024]{3,2,1,0:T(8,128)(2,1)S(1)} %get-tuple-element.62), channel_id=1, source_target_pairs={{0,2},{2,4},{4,6},{6,8},{8,10},{10,12},{12,14},{1,3},{3,5},{5,7},{... | collective-permute-start | bytes 393224 | tf_op jit(solution)/shard_map/ppermute | solution.py:555
  121.2 1.5 %collective-permute-start.18 = (bf16[2,4,8,1024]{3,2,1,0:T(8,128)(2,1)S(1)}, bf16[2,4,8,1024]{3,2,1,0:T(8,128)(2,1)S(1)}, u32[]{:S(2)}, u32[]{:S(2)}) collective-permute-start(bf16[2,4,8,1024]{3,2,1,0:T(8,128)(2,1)S(1)} %get-tuple-element.61), channel_id=1, source_target_pairs={{2,0},{4,2},{6,4},{8,6},{10,8},{12,10},{14,12},{3,1},{5,3},{7,5},{... | collective-permute-start | bytes 393224 | tf_op jit(solution)/shard_map/ppermute | solution.py:555
  122.7 2.1 %collective-permute-start.10 = (bf16[1,32,1024]{2,1,0:T(8,128)(2,1)S(1)}, bf16[1,32,1024]{2,1,0:T(8,128)(2,1)S(1)}, u32[]{:S(2)}, u32[]{:S(2)}) collective-permute-start(bf16[1,32,1024]{2,1,0:T(8,128)(2,1)S(1)} %get-tuple-element.27), channel_id=1, source_target_pairs={{0,10},{2,8},{4,14},{6,12},{8,2},{10,0},{12,6},{14,4},{1,11},{3,9}... | collective-permute-start | bytes 196616 | tf_op jit(solution)/shard_map/ppermute | solution.py:559
  124.8 3.3 %collective-permute-start.11 = (bf16[1,32,1024]{2,1,0:T(8,128)(2,1)S(1)}, bf16[1,32,1024]{2,1,0:T(8,128)(2,1)S(1)}, u32[]{:S(2)}, u32[]{:S(2)}) collective-permute-start(bf16[1,32,1024]{2,1,0:T(8,128)(2,1)S(1)} %get-tuple-element.28), channel_id=1, source_target_pairs={{0,12},{2,14},{4,8},{6,10},{8,4},{10,6},{12,0},{14,2},{1,13},{3,15... | collective-permute-start | bytes 196616 | tf_op jit(solution)/shard_map/ppermute | solution.py:559
  128.1 1.8 %collective-permute-start.12 = (bf16[1,32,1024]{2,1,0:T(8,128)(2,1)S(1)}, bf16[1,32,1024]{2,1,0:T(8,128)(2,1)S(1)}, u32[]{:S(2)}, u32[]{:S(2)}) collective-permute-start(bf16[1,32,1024]{2,1,0:T(8,128)(2,1)S(1)} %get-tuple-element.29), channel_id=1, source_target_pairs={{0,14},{2,12},{4,10},{6,8},{8,6},{10,4},{12,2},{14,0},{1,15},{3,13... | collective-permute-start | bytes 196616 | tf_op jit(solution)/shard_map/ppermute | solution.py:559
  129.9 3.0 %collective-permute-done.10 = bf16[1,32,1024]{2,1,0:T(8,128)(2,1)S(1)} collective-permute-done((bf16[1,32,1024]{2,1,0:T(8,128)(2,1)S(1)}, bf16[1,32,1024]{2,1,0:T(8,128)(2,1)S(1)}, u32[]{:S(2)}, u32[]{:S(2)}) %collective-permute-start.10) | collective-permute-done | bytes 65568 | tf_op jit(solution)/shard_map/ppermute | solution.py:559
  132.9 2.2 %collective-permute-done.12 = bf16[1,32,1024]{2,1,0:T(8,128)(2,1)S(1)} collective-permute-done((bf16[1,32,1024]{2,1,0:T(8,128)(2,1)S(1)}, bf16[1,32,1024]{2,1,0:T(8,128)(2,1)S(1)}, u32[]{:S(2)}, u32[]{:S(2)}) %collective-permute-start.12) | collective-permute-done | bytes 65568 | tf_op jit(solution)/shard_map/ppermute | solution.py:559
  135.2 0.1 collective-permute-start.20
  135.3 0.1 shard_map.117
  135.4 0.5 collective-permute-start.19
  136.0 0.5 collective-permute-done.20.refs_12_
  136.5 0.4 collective-permute-done.19.refs_11_
  136.8 0.2 broadcast_in_dim.21.refs_13_
  137.1 8.6 %shard_map.119 = bf16[2048,256]{1,0:T(8,128)(2,1)} custom-call(s32[2]{0:T(128)S(1)} %pad_add_fusion.scalars, bf16[1,4,8,1024]{3,2,1,0:T(8,128)(2,1)S(1)} %bitcast.93, bf16[1,4,8,1024]{3,2,1,0:T(8,128)(2,1)S(1)} %bitcast.95, bf16[1,4,8,1024]{3,2,1,0:T(8,128)(2,1)S(1)} %bitcast.97, bf16[1,4,8,1024]{3,2,1,0:T(8,128)(2,1)S(1)} %bitcast.99, ...), custom_call_target="tpu_custom_call" | custom-call | tf_op jit(solution)/shard_map/pallas_call | solution.py:506
  (44 shorter events, 0.2 us)
Async XLA Ops:
  3.0 60.9 %all-to-all-start = ((bf16[16,2,2,32,640]{4,3,2,1,0:T(8,128)(2,1)}), bf16[16,2,2,32,640]{4,3,2,1,0:T(8,128)(2,1)S(1)}, u32[]{:S(2)}, u32[]{:S(2)}) async-start(bf16[16,2,2,32,640]{4,3,2,1,0:T(8,128)(2,1)} %bitcast.112), calls=%async_computation | async-start | bytes 5242880 | tf_op jit(solution)/shard_map/all_to_all | solution.py:563
  10.4 1.3 copy-start.3
  11.7 1.3 copy-start.4
  13.1 1.3 copy-start.5
  19.9 2.5 %collective-permute-start = (bf16[4,128,640]{2,1,0:T(8,128)(2,1)}, bf16[4,128,640]{2,1,0:T(8,128)(2,1)}, u32[]{:S(2)}, u32[]{:S(2)}) collective-permute-start(bf16[4,128,640]{2,1,0:T(8,128)(2,1)} %get-tuple-element.44), channel_id=1, source_target_pairs={{0,1},{1,0},{2,3},{3,2},{4,5},{5,4},{6,7},{7,6},{8,9},{9,8},{10,11... | collective-permute-start | bytes 1966088 | tf_op jit(solution)/shard_map/ppermute | solution.py:559
  25.1 27.2 %collective-permute-start.1 = (bf16[4,2,2,4,8,640]{5,4,3,2,1,0:T(8,128)(2,1)S(1)}, bf16[4,2,2,4,8,640]{5,4,3,2,1,0:T(8,128)(2,1)S(1)}, u32[]{:S(2)}, u32[]{:S(2)}) collective-permute-start(bf16[4,2,2,4,8,640]{5,4,3,2,1,0:T(8,128)(2,1)S(1)} %get-tuple-element.34), channel_id=1, source_target_pairs={{0,2},{2,0},{4,6},{6,4},{8,10},{10,8},{12,14},{14,12},{1,3},{3,1},... | collective-permute-start | bytes 1966088 | tf_op jit(solution)/shard_map/ppermute | solution.py:559
  53.7 37.2 %collective-permute-start.2 = (bf16[2,2,32,640]{3,2,1,0:T(8,128)(2,1)}, bf16[2,2,32,640]{3,2,1,0:T(8,128)(2,1)S(1)}, u32[]{:S(2)}, u32[]{:S(2)}) collective-permute-start(bf16[2,2,32,640]{3,2,1,0:T(8,128)(2,1)} %pad_maximum_fusion.2), channel_id=1, source_target_pairs={{0,4},{2,6},{4,0},{6,2},{8,12},{10,14},{12,8},{14,10},{1,5},{3,7},... | collective-permute-start | bytes 491528 | tf_op jit(solution)/shard_map/ppermute | solution.py:559
  56.5 17.3 %collective-permute-start.13 = (bf16[2,2,32,640]{3,2,1,0:T(8,128)(2,1)}, bf16[2,2,32,640]{3,2,1,0:T(8,128)(2,1)S(1)}, u32[]{:S(2)}, u32[]{:S(2)}) collective-permute-start(bf16[2,2,32,640]{3,2,1,0:T(8,128)(2,1)} %pad_maximum_fusion.6), channel_id=1, source_target_pairs={{0,4},{2,6},{4,0},{6,2},{8,12},{10,14},{12,8},{14,10},{1,5},{3,7},... | collective-permute-start | bytes 491528 | tf_op jit(solution)/shard_map/ppermute | solution.py:559
  57.2 28.2 %collective-permute-start.14 = (bf16[2,2,32,640]{3,2,1,0:T(8,128)(2,1)}, bf16[2,2,32,640]{3,2,1,0:T(8,128)(2,1)S(1)}, u32[]{:S(2)}, u32[]{:S(2)}) collective-permute-start(bf16[2,2,32,640]{3,2,1,0:T(8,128)(2,1)} %pad_maximum_fusion.7), channel_id=1, source_target_pairs={{0,8},{2,10},{4,12},{6,14},{8,0},{10,2},{12,4},{14,6},{1,9},{3,11}... | collective-permute-start | bytes 491528 | tf_op jit(solution)/shard_map/ppermute | solution.py:559
  59.7 25.7 %collective-permute-start.15 = (bf16[2,2,32,640]{3,2,1,0:T(8,128)(2,1)}, bf16[2,2,32,640]{3,2,1,0:T(8,128)(2,1)S(1)}, u32[]{:S(2)}, u32[]{:S(2)}) collective-permute-start(bf16[2,2,32,640]{3,2,1,0:T(8,128)(2,1)} %pad_maximum_fusion.8), channel_id=1, source_target_pairs={{0,12},{2,14},{4,8},{6,10},{8,4},{10,6},{12,0},{14,2},{1,13},{3,15... | collective-permute-start | bytes 491528 | tf_op jit(solution)/shard_map/ppermute | solution.py:559
  62.9 33.1 %collective-permute-start.3 = (bf16[2,2,32,640]{3,2,1,0:T(8,128)(2,1)}, bf16[2,2,32,640]{3,2,1,0:T(8,128)(2,1)}, u32[]{:S(2)}, u32[]{:S(2)}) collective-permute-start(bf16[2,2,32,640]{3,2,1,0:T(8,128)(2,1)} %pad_maximum_fusion.3), channel_id=1, source_target_pairs={{0,8},{2,10},{4,12},{6,14},{8,0},{10,2},{12,4},{14,6},{1,9},{3,11}... | collective-permute-start | bytes 491528 | tf_op jit(solution)/shard_map/ppermute | solution.py:559
  63.9 22.4 %copy-start.14 = (bf16[1,2,32,640]{3,2,1,0:T(8,128)(2,1)S(1)}, bf16[1,2,32,640]{3,2,1,0:T(8,128)(2,1)}, u32[]{:S(2)}) copy-start(bf16[1,2,32,640]{3,2,1,0:T(8,128)(2,1)} %get-tuple-element.57) | copy-start | bytes 245764
  69.4 1.3 copy-start.1
  85.4 0.9 copy-start.12
  85.4 2.5 %copy-start.13 = (bf16[1,2,32,640]{3,2,1,0:T(8,128)(2,1)S(1)}, bf16[1,2,32,640]{3,2,1,0:T(8,128)(2,1)}, u32[]{:S(2)}) copy-start(bf16[1,2,32,640]{3,2,1,0:T(8,128)(2,1)} %get-tuple-element.60) | copy-start | bytes 245764
  85.4 3.2 %copy-start = (bf16[1280,1024]{1,0:T(8,128)(2,1)S(1)}, bf16[1280,1024]{1,0:T(8,128)(2,1)}, u32[]{:S(2)}) copy-start(bf16[1280,1024]{1,0:T(8,128)(2,1)} %proj_weight.3) | copy-start | bytes 7864324
  85.4 3.2 %copy-start.7 = (f32[1024]{0:T(1024)S(1)}, f32[1024]{0:T(1024)}, u32[]{:S(2)}) copy-start(f32[1024]{0:T(1024)} %param.17) | copy-start | bytes 12292
  86.2 2.3 %collective-permute-start.16 = (bf16[256,640]{1,0:T(8,128)(2,1)S(1)}, bf16[256,640]{1,0:T(8,128)(2,1)S(1)}, u32[]{:S(2)}, u32[]{:S(2)}) collective-permute-start(bf16[256,640]{1,0:T(8,128)(2,1)S(1)} %get-tuple-element.32), channel_id=1, source_target_pairs={{0,1},{1,0},{2,3},{3,2},{4,5},{5,4},{6,7},{7,6},{8,9},{9,8},{10,11... | collective-permute-start | bytes 983048 | tf_op jit(solution)/shard_map/ppermute | solution.py:559
  86.4 9.7 %collective-permute-start.4 = (bf16[2,2,32,640]{3,2,1,0:T(8,128)(2,1)S(1)}, bf16[2,2,32,640]{3,2,1,0:T(8,128)(2,1)S(1)}, u32[]{:S(2)}, u32[]{:S(2)}) collective-permute-start(bf16[2,2,32,640]{3,2,1,0:T(8,128)(2,1)S(1)} %pad_maximum_fusion.4), channel_id=1, source_target_pairs={{0,12},{2,14},{4,8},{6,10},{8,4},{10,6},{12,0},{14,2},{1,13},{3,15... | collective-permute-start | bytes 491528 | tf_op jit(solution)/shard_map/ppermute | solution.py:559
  90.9 5.1 %copy-start.10 = (bf16[2,2,32,640]{3,2,1,0:T(8,128)(2,1)}, bf16[2,2,32,640]{3,2,1,0:T(8,128)(2,1)S(1)}, u32[]{:S(2)}) copy-start(bf16[2,2,32,640]{3,2,1,0:T(8,128)(2,1)S(1)} %collective-permute-done.2.refs_1_.refs_2_) | copy-start | bytes 491524
  96.0 0.7 copy-start.11
  96.7 21.3 %all-to-all-start.1 = ((bf16[8,4,8,1024]{3,2,1,0:T(8,128)(2,1)}), bf16[8,4,8,1024]{3,2,1,0:T(8,128)(2,1)S(1)}, u32[]{:S(2)}, u32[]{:S(2)}) async-start(bf16[8,4,8,1024]{3,2,1,0:T(8,128)(2,1)} %bitcast.113), calls=%async_computation.1 | async-start | bytes 1048576 | tf_op jit(solution)/shard_map/all_to_all | solution.py:563
  103.3 1.6 %copy-start.2 = (bf16[4,512,512]{2,1,0:T(8,128)(2,1)S(1)}, bf16[4,512,512]{2,1,0:T(8,128)(2,1)}, u32[]{:S(2)}) copy-start(bf16[4,512,512]{2,1,0:T(8,128)(2,1)} %copy-done.1) | copy-start | bytes 6291460
  106.8 1.7 %collective-permute-start.5 = (bf16[256,640]{1,0:T(8,128)(2,1)S(1)}, bf16[256,640]{1,0:T(8,128)(2,1)S(1)}, u32[]{:S(2)}, u32[]{:S(2)}) collective-permute-start(bf16[256,640]{1,0:T(8,128)(2,1)S(1)} %get-tuple-element.21), channel_id=1, source_target_pairs={{0,1},{1,0},{2,3},{3,2},{4,5},{5,4},{6,7},{7,6},{8,9},{9,8},{10,11... | collective-permute-start | bytes 983048 | tf_op jit(solution)/shard_map/ppermute | solution.py:559
  110.8 10.4 %collective-permute-start.6 = (bf16[1,32,1024]{2,1,0:T(8,128)(2,1)}, bf16[1,32,1024]{2,1,0:T(8,128)(2,1)S(1)}, u32[]{:S(2)}, u32[]{:S(2)}) collective-permute-start(bf16[1,32,1024]{2,1,0:T(8,128)(2,1)} %get-tuple-element.23), channel_id=1, source_target_pairs={{0,2},{2,0},{4,6},{6,4},{8,10},{10,8},{12,14},{14,12},{1,3},{3,1},... | collective-permute-start | bytes 196616 | tf_op jit(solution)/shard_map/ppermute | solution.py:559
  112.8 9.9 %collective-permute-start.7 = (bf16[1,32,1024]{2,1,0:T(8,128)(2,1)}, bf16[1,32,1024]{2,1,0:T(8,128)(2,1)S(1)}, u32[]{:S(2)}, u32[]{:S(2)}) collective-permute-start(bf16[1,32,1024]{2,1,0:T(8,128)(2,1)} %get-tuple-element.24), channel_id=1, source_target_pairs={{0,4},{2,6},{4,0},{6,2},{8,12},{10,14},{12,8},{14,10},{1,5},{3,7},... | collective-permute-start | bytes 196616 | tf_op jit(solution)/shard_map/ppermute | solution.py:559
  114.3 10.5 %collective-permute-start.8 = (bf16[1,32,1024]{2,1,0:T(8,128)(2,1)}, bf16[1,32,1024]{2,1,0:T(8,128)(2,1)S(1)}, u32[]{:S(2)}, u32[]{:S(2)}) collective-permute-start(bf16[1,32,1024]{2,1,0:T(8,128)(2,1)} %get-tuple-element.25), channel_id=1, source_target_pairs={{0,6},{2,4},{4,2},{6,0},{8,14},{10,12},{12,10},{14,8},{1,7},{3,5},... | collective-permute-start | bytes 196616 | tf_op jit(solution)/shard_map/ppermute | solution.py:559
  114.3 22.8 %copy-start.6 = (bf16[3,3,256,256]{3,2,1,0:T(8,128)(2,1)S(1)}, bf16[3,3,256,256]{3,2,1,0:T(8,128)(2,1)}, u32[]{:S(2)}) copy-start(bf16[3,3,256,256]{3,2,1,0:T(8,128)(2,1)} %param.18) | copy-start | bytes 3538948
  114.3 22.8 %copy-start.8 = (f32[256]{0:T(256)S(1)}, f32[256]{0:T(256)}, u32[]{:S(2)}) copy-start(f32[256]{0:T(256)} %param.19) | copy-start | bytes 3076
  114.3 22.8 %copy-start.9 = (f32[256]{0:T(256)S(1)}, f32[256]{0:T(256)}, u32[]{:S(2)}) copy-start(f32[256]{0:T(256)} %param.21) | copy-start | bytes 3076
  114.3 13.8 %collective-permute-start.9 = (bf16[1,32,1024]{2,1,0:T(8,128)(2,1)S(1)}, bf16[1,32,1024]{2,1,0:T(8,128)(2,1)S(1)}, u32[]{:S(2)}, u32[]{:S(2)}) collective-permute-start(bf16[1,32,1024]{2,1,0:T(8,128)(2,1)S(1)} %get-tuple-element.26), channel_id=1, source_target_pairs={{0,8},{2,10},{4,12},{6,14},{8,0},{10,2},{12,4},{14,6},{1,9},{3,11}... | collective-permute-start | bytes 196616 | tf_op jit(solution)/shard_map/ppermute | solution.py:559
  118.0 17.3 %collective-permute-start.17 = (bf16[2,4,8,1024]{3,2,1,0:T(8,128)(2,1)S(1)}, bf16[2,4,8,1024]{3,2,1,0:T(8,128)(2,1)S(1)}, u32[]{:S(2)}, u32[]{:S(2)}) collective-permute-start(bf16[2,4,8,1024]{3,2,1,0:T(8,128)(2,1)S(1)} %get-tuple-element.62), channel_id=1, source_target_pairs={{0,2},{2,4},{4,6},{6,8},{8,10},{10,12},{12,14},{1,3},{3,5},{5,7},{... | collective-permute-start | bytes 393224 | tf_op jit(solution)/shard_map/ppermute | solution.py:555
  121.2 14.1 %collective-permute-start.18 = (bf16[2,4,8,1024]{3,2,1,0:T(8,128)(2,1)S(1)}, bf16[2,4,8,1024]{3,2,1,0:T(8,128)(2,1)S(1)}, u32[]{:S(2)}, u32[]{:S(2)}) collective-permute-start(bf16[2,4,8,1024]{3,2,1,0:T(8,128)(2,1)S(1)} %get-tuple-element.61), channel_id=1, source_target_pairs={{2,0},{4,2},{6,4},{8,6},{10,8},{12,10},{14,12},{3,1},{5,3},{7,5},{... | collective-permute-start | bytes 393224 | tf_op jit(solution)/shard_map/ppermute | solution.py:555
  122.7 10.2 %collective-permute-start.10 = (bf16[1,32,1024]{2,1,0:T(8,128)(2,1)S(1)}, bf16[1,32,1024]{2,1,0:T(8,128)(2,1)S(1)}, u32[]{:S(2)}, u32[]{:S(2)}) collective-permute-start(bf16[1,32,1024]{2,1,0:T(8,128)(2,1)S(1)} %get-tuple-element.27), channel_id=1, source_target_pairs={{0,10},{2,8},{4,14},{6,12},{8,2},{10,0},{12,6},{14,4},{1,11},{3,9}... | collective-permute-start | bytes 196616 | tf_op jit(solution)/shard_map/ppermute | solution.py:559
  124.8 8.1 %collective-permute-start.11 = (bf16[1,32,1024]{2,1,0:T(8,128)(2,1)S(1)}, bf16[1,32,1024]{2,1,0:T(8,128)(2,1)S(1)}, u32[]{:S(2)}, u32[]{:S(2)}) collective-permute-start(bf16[1,32,1024]{2,1,0:T(8,128)(2,1)S(1)} %get-tuple-element.28), channel_id=1, source_target_pairs={{0,12},{2,14},{4,8},{6,10},{8,4},{10,6},{12,0},{14,2},{1,13},{3,15... | collective-permute-start | bytes 196616 | tf_op jit(solution)/shard_map/ppermute | solution.py:559
  128.1 7.1 %collective-permute-start.12 = (bf16[1,32,1024]{2,1,0:T(8,128)(2,1)S(1)}, bf16[1,32,1024]{2,1,0:T(8,128)(2,1)S(1)}, u32[]{:S(2)}, u32[]{:S(2)}) collective-permute-start(bf16[1,32,1024]{2,1,0:T(8,128)(2,1)S(1)} %get-tuple-element.29), channel_id=1, source_target_pairs={{0,14},{2,12},{4,10},{6,8},{8,6},{10,4},{12,2},{14,0},{1,15},{3,13... | collective-permute-start | bytes 196616 | tf_op jit(solution)/shard_map/ppermute | solution.py:559
  135.2 1.3 collective-permute-start.20
  135.4 1.4 collective-permute-start.19

commit v7 on v6

--- a/solution.py
+++ b/solution.py
@@ -17,7 +17,7 @@
 EDGE = 16
 PIECE = 8
 SPAN = 2 * LANES
-VMEM_BYTES = 16 * 1024 * 1024
+VMEM_BYTES = 12 * 1024 * 1024
 
 
 def params(steps=0, size=VMEM_BYTES):

time: 146 us -> 146 us (level)
  no operation moved by 1% of the time
where the time goes in v7:
time: 146 us
  waiting for transfers between devices  54.8 us (38%)
  starting transfers between devices  44.3 us (30%)
  Pallas kernels  29.1 us (20%)
  local copies, waits for them, and re-layouts  10.3 us (7%)
  other arithmetic  6.78 us (5%)
    ppermute x19, waiting for transfers between devices, swapped(): lax.ppermute(value, axis, [(i, i ^ by) for i in range(lax.axis_size(axis))])  54.1 us
    ppermute x19, starting transfers between devices, swapped(): lax.ppermute(value, axis, [(i, i ^ by) for i in range(lax.axis_size(axis))])  25.6 us
    all_to_all x2, starting transfers between devices, exchanged(): return lax.all_to_all(value, axes, split_axis=0, concat_axis=0, tiled=True)  14 us
    pallas_call x1, Pallas kernels, convolve_twice(): pl.pallas_call(functools.partial(conv_kernel, rows, cols, len(middles)),...  8.59 us
    unnamed x30, local copies, waits for them, and re-layouts  7.56 us
    pallas_call x1, Pallas kernels, index_weights(): pl.pallas_call(functools.partial(weights_kernel, tokens), grid=(parts, he...  5.5 us
    ppermute x2, starting transfers between devices, shifted(): return lax.ppermute(value, axis, pairs)  4.65 us
    pallas_call x2, Pallas kernels, project(): pl.pallas_call(functools.partial(project_kernel, places, inner), in_specs...  4.59 us
  transfers between devices with their start and end apart: 23, of which 11 were waited for; matrix products, arithmetic and copies ran while one was open for 6% of the time, Pallas kernels for 12%

profile of v7, /device:TPU:0, one launch (start us, length us, event | category | flops | bytes accessed | tf_op | source)
XLA Modules:
  0.0 145.9 jit_solution(2598983410808123286)
XLA Ops:
  0.0 3.0 %shard_map.109 = bf16[8,2,2,2,32,640]{5,4,3,2,1,0:T(8,128)(2,1)} custom-call(bf16[4,128,1280]{2,1,0:T(8,128)(2,1)} %bitcast.114, bf16[4,128,1280]{2,1,0:T(8,128)(2,1)} %bitcast.115), custom_call_target="tpu_custom_call" | custom-call | tf_op jit(solution)/shard_map/pallas_call | solution.py:131
  3.0 7.4 %all-to-all-start = ((bf16[16,2,2,32,640]{4,3,2,1,0:T(8,128)(2,1)}), bf16[16,2,2,32,640]{4,3,2,1,0:T(8,128)(2,1)S(1)}, u32[]{:S(2)}, u32[]{:S(2)}) async-start(bf16[16,2,2,32,640]{4,3,2,1,0:T(8,128)(2,1)} %bitcast.112), calls=%async_computation | async-start | bytes 5242880 | tf_op jit(solution)/shard_map/all_to_all | solution.py:563
  10.4 1.3 copy-done.3
  11.7 1.3 copy-done.4
  13.1 1.3 copy-done.5
  14.4 4.5 %shard_map.111 = bf16[2,4,128,640]{3,2,1,0:T(8,128)(2,1)S(1)} custom-call(bf16[4,128,1280]{2,1,0:T(8,128)(2,1)S(1)} %bitcast.88, bf16[4,128,1280]{2,1,0:T(8,128)(2,1)S(1)} %bitcast.89, bf16[4,128,1280]{2,1,0:T(8,128)(2,1)S(1)} %bitcast.90), custom_call_target="tpu_custom_call" | custom-call | tf_op jit(solution)/shard_map/pallas_call | solution.py:83
  18.9 1.0 constant_dynamic-slice_fusion
  19.9 0.4 collective-permute-start
  20.3 2.1 %collective-permute-done = bf16[4,128,640]{2,1,0:T(8,128)(2,1)} collective-permute-done((bf16[4,128,640]{2,1,0:T(8,128)(2,1)}, bf16[4,128,640]{2,1,0:T(8,128)(2,1)}, u32[]{:S(2)}, u32[]{:S(2)}) %collective-permute-start) | collective-permute-done | bytes 655392 | tf_op jit(solution)/shard_map/ppermute | solution.py:559
  22.4 1.0 fusion.8
  23.3 1.2 fusion.14
  24.6 0.1 maximum_bitcast_fusion.2
  24.6 0.1 maximum_bitcast_fusion
  24.7 0.2 pad_maximum_fusion
  24.9 0.1 dynamic-slice_bitcast_fusion.1
  25.1 2.0 %collective-permute-start.1 = (bf16[4,2,2,4,8,640]{5,4,3,2,1,0:T(8,128)(2,1)S(1)}, bf16[4,2,2,4,8,640]{5,4,3,2,1,0:T(8,128)(2,1)S(1)}, u32[]{:S(2)}, u32[]{:S(2)}) collective-permute-start(bf16[4,2,2,4,8,640]{5,4,3,2,1,0:T(8,128)(2,1)S(1)} %get-tuple-element.34), channel_id=1, source_target_pairs={{0,2},{2,0},{4,6},{6,4},{8,10},{10,8},{12,14},{14,12},{1,3},{3,1},... | collective-permute-start | bytes 1966088 | tf_op jit(solution)/shard_map/ppermute | solution.py:559
  27.0 0.7 slice_bitcast_fusion.1
  27.7 24.5 %collective-permute-done.1 = bf16[4,2,2,4,8,640]{5,4,3,2,1,0:T(8,128)(2,1)S(1)} collective-permute-done((bf16[4,2,2,4,8,640]{5,4,3,2,1,0:T(8,128)(2,1)S(1)}, bf16[4,2,2,4,8,640]{5,4,3,2,1,0:T(8,128)(2,1)S(1)}, u32[]{:S(2)}, u32[]{:S(2)}) %collective-permute-start.1) | collective-permute-done | bytes 655392 | tf_op jit(solution)/shard_map/ppermute | solution.py:559
  52.2 0.7 slice_bitcast_fusion
  53.0 0.7 pad_maximum_fusion.2
  53.6 2.1 %collective-permute-start.2 = (bf16[2,2,32,640]{3,2,1,0:T(8,128)(2,1)}, bf16[2,2,32,640]{3,2,1,0:T(8,128)(2,1)S(1)}, u32[]{:S(2)}, u32[]{:S(2)}) collective-permute-start(bf16[2,2,32,640]{3,2,1,0:T(8,128)(2,1)} %pad_maximum_fusion.2), channel_id=1, source_target_pairs={{0,4},{2,6},{4,0},{6,2},{8,12},{10,14},{12,8},{14,10},{1,5},{3,7},... | collective-permute-start | bytes 491528 | tf_op jit(solution)/shard_map/ppermute | solution.py:559
  55.8 0.7 pad_maximum_fusion.6
  56.5 0.7 pad_maximum_fusion.7
  57.2 1.9 %collective-permute-start.14 = (bf16[2,2,32,640]{3,2,1,0:T(8,128)(2,1)}, bf16[2,2,32,640]{3,2,1,0:T(8,128)(2,1)S(1)}, u32[]{:S(2)}, u32[]{:S(2)}) collective-permute-start(bf16[2,2,32,640]{3,2,1,0:T(8,128)(2,1)} %pad_maximum_fusion.7), channel_id=1, source_target_pairs={{0,8},{2,10},{4,12},{6,14},{8,0},{10,2},{12,4},{14,6},{1,9},{3,11}... | collective-permute-start | bytes 491528 | tf_op jit(solution)/shard_map/ppermute | solution.py:559
  59.0 0.7 pad_maximum_fusion.8
  59.7 2.5 %collective-permute-start.15 = (bf16[2,2,32,640]{3,2,1,0:T(8,128)(2,1)}, bf16[2,2,32,640]{3,2,1,0:T(8,128)(2,1)S(1)}, u32[]{:S(2)}, u32[]{:S(2)}) collective-permute-start(bf16[2,2,32,640]{3,2,1,0:T(8,128)(2,1)} %pad_maximum_fusion.8), channel_id=1, source_target_pairs={{0,12},{2,14},{4,8},{6,10},{8,4},{10,6},{12,0},{14,2},{1,13},{3,15... | collective-permute-start | bytes 491528 | tf_op jit(solution)/shard_map/ppermute | solution.py:559
  62.2 0.7 pad_maximum_fusion.3
  62.9 1.0 collective-permute-start.3
  63.9 5.5 %shard_map.110 = (bf16[4,512,512]{2,1,0:T(8,128)(2,1)S(1)}, bf16[4,512,512]{2,1,0:T(8,128)(2,1)S(1)}) custom-call(s32[1]{0:T(128)} %bitcast.core, bf16[8,2,2,2,32,640]{5,4,3,2,1,0:T(8,128)(2,1)S(1)} %bitcast.87), custom_call_target="tpu_custom_call" | custom-call | tf_op jit(solution)/shard_map/pallas_call | solution.py:187
  69.4 1.3 copy-done.1
  70.8 2.9 %collective-permute-done.13.refs_1_ = bf16[2,2,32,640]{3,2,1,0:T(8,128)(2,1)S(1)} collective-permute-done((bf16[2,2,32,640]{3,2,1,0:T(8,128)(2,1)}, bf16[2,2,32,640]{3,2,1,0:T(8,128)(2,1)S(1)}, u32[]{:S(2)}, u32[]{:S(2)}) %collective-permute-start.13) | collective-permute-done | bytes 163872 | tf_op jit(solution)/shard_map/ppermute | solution.py:559
  73.7 11.7 %collective-permute-done.14.refs_2_ = bf16[2,2,32,640]{3,2,1,0:T(8,128)(2,1)S(1)} collective-permute-done((bf16[2,2,32,640]{3,2,1,0:T(8,128)(2,1)}, bf16[2,2,32,640]{3,2,1,0:T(8,128)(2,1)S(1)}, u32[]{:S(2)}, u32[]{:S(2)}) %collective-permute-start.14) | collective-permute-done | bytes 163872 | tf_op jit(solution)/shard_map/ppermute | solution.py:559
  85.4 0.8 shard_map.114
  86.2 0.1 collective-permute-start.16
  86.4 1.4 collective-permute-start.4
  87.8 0.1 pad_add_fusion.scalars
  87.9 0.7 pad_maximum_fusion.1.refs_0_.refs_1_
  88.6 2.3 %shard_map.115.refs_0_ = bf16[256,1024]{1,0:T(8,128)(2,1)} custom-call(s32[2]{0:T(128)S(1)} %pad_add_fusion.scalars, bf16[256,640]{1,0:T(8,128)(2,1)S(1)} %get-tuple-element.31.near, bf16[256,640]{1,0:T(8,128)(2,1)S(1)} %collective-permute-done.16.far, bf16[1280,1024]{1,0:T(8,128)(2,1)S(1)} %copy-done, f32[1,1024]{1,0:T(1,128)S(1)} %bitcast.108), custom_call_target="tpu_custom_call" | custom-call | tf_op jit(solution)/shard_map/pallas_call | solution.py:292
  90.9 5.1 %collective-permute-done.3.refs_2_.refs_3_ = bf16[2,2,32,640]{3,2,1,0:T(8,128)(2,1)} collective-permute-done((bf16[2,2,32,640]{3,2,1,0:T(8,128)(2,1)}, bf16[2,2,32,640]{3,2,1,0:T(8,128)(2,1)}, u32[]{:S(2)}, u32[]{:S(2)}) %collective-permute-start.3) | collective-permute-done | bytes 163872 | tf_op jit(solution)/shard_map/ppermute | solution.py:559
  96.0 0.7 copy-done.11
  96.7 6.6 %all-to-all-start.1 = ((bf16[8,4,8,1024]{3,2,1,0:T(8,128)(2,1)}), bf16[8,4,8,1024]{3,2,1,0:T(8,128)(2,1)S(1)}, u32[]{:S(2)}, u32[]{:S(2)}) async-start(bf16[8,4,8,1024]{3,2,1,0:T(8,128)(2,1)} %bitcast.113), calls=%async_computation.1 | async-start | bytes 1048576 | tf_op jit(solution)/shard_map/all_to_all | solution.py:563
  103.3 1.6 %copy-done.2 = bf16[4,512,512]{2,1,0:T(8,128)(2,1)S(1)} copy-done((bf16[4,512,512]{2,1,0:T(8,128)(2,1)S(1)}, bf16[4,512,512]{2,1,0:T(8,128)(2,1)}, u32[]{:S(2)}) %copy-start.2) | copy-done | bytes 2097176
  104.9 1.9 %shard_map.112 = (bf16[256,640]{1,0:T(8,128)(2,1)S(1)}, bf16[256,640]{1,0:T(8,128)(2,1)S(1)}) custom-call(s32[1]{0:T(128)} %bitcast.1.place, bf16[4,512,512]{2,1,0:T(8,128)(2,1)S(1)} %copy-done.2, bf16[2,2,32,640]{3,2,1,0:T(8,128)(2,1)} %pad_maximum_fusion.1.refs_0_.refs_1_, bf16[2,2,32,640]{3,2,1,0:T(8,128)(2,1)} %copy-done.10, ...), custom_call_target="tpu_custom_call" | custom-call | tf_op jit(solution)/shard_map/pallas_call | solution.py:250
  106.8 0.1 collective-permute-start.5
  106.9 1.6 %collective-permute-done.5.far = bf16[256,640]{1,0:T(8,128)(2,1)S(1)} collective-permute-done((bf16[256,640]{1,0:T(8,128)(2,1)S(1)}, bf16[256,640]{1,0:T(8,128)(2,1)S(1)}, u32[]{:S(2)}, u32[]{:S(2)}) %collective-permute-start.5) | collective-permute-done | bytes 327712 | tf_op jit(solution)/shard_map/ppermute | solution.py:559
  108.5 2.2 %shard_map.113 = (bf16[1,32,1024]{2,1,0:T(8,128)(2,1)S(1)}, bf16[1,32,1024]{2,1,0:T(8,128)(2,1)}, bf16[1,32,1024]{2,1,0:T(8,128)(2,1)}, bf16[1,32,1024]{2,1,0:T(...) custom-call(s32[2]{0:T(128)S(1)} %pad_add_fusion.scalars, ...), custom_call_target="tpu_custom_call" | custom-call | tf_op jit(solution)/shard_map/pallas_call | solution.py:292
  110.8 2.0 %collective-permute-start.6 = (bf16[1,32,1024]{2,1,0:T(8,128)(2,1)}, bf16[1,32,1024]{2,1,0:T(8,128)(2,1)S(1)}, u32[]{:S(2)}, u32[]{:S(2)}) collective-permute-start(bf16[1,32,1024]{2,1,0:T(8,128)(2,1)} %get-tuple-element.23), channel_id=1, source_target_pairs={{0,2},{2,0},{4,6},{6,4},{8,10},{10,8},{12,14},{14,12},{1,3},{3,1},... | collective-permute-start | bytes 196616 | tf_op jit(solution)/shard_map/ppermute | solution.py:559
  112.8 1.5 %collective-permute-start.7 = (bf16[1,32,1024]{2,1,0:T(8,128)(2,1)}, bf16[1,32,1024]{2,1,0:T(8,128)(2,1)S(1)}, u32[]{:S(2)}, u32[]{:S(2)}) collective-permute-start(bf16[1,32,1024]{2,1,0:T(8,128)(2,1)} %get-tuple-element.24), channel_id=1, source_target_pairs={{0,4},{2,6},{4,0},{6,2},{8,12},{10,14},{12,8},{14,10},{1,5},{3,7},... | collective-permute-start | bytes 196616 | tf_op jit(solution)/shard_map/ppermute | solution.py:559
  114.3 2.9 %collective-permute-start.9 = (bf16[1,32,1024]{2,1,0:T(8,128)(2,1)S(1)}, bf16[1,32,1024]{2,1,0:T(8,128)(2,1)S(1)}, u32[]{:S(2)}, u32[]{:S(2)}) collective-permute-start(bf16[1,32,1024]{2,1,0:T(8,128)(2,1)S(1)} %get-tuple-element.26), channel_id=1, source_target_pairs={{0,8},{2,10},{4,12},{6,14},{8,0},{10,2},{12,4},{14,6},{1,9},{3,11}... | collective-permute-start | bytes 196616 | tf_op jit(solution)/shard_map/ppermute | solution.py:559
  117.2 0.8 all-to-all-done.1.refs_1_.refs_8_
  118.0 3.2 %collective-permute-start.17 = (bf16[2,4,8,1024]{3,2,1,0:T(8,128)(2,1)S(1)}, bf16[2,4,8,1024]{3,2,1,0:T(8,128)(2,1)S(1)}, u32[]{:S(2)}, u32[]{:S(2)}) collective-permute-start(bf16[2,4,8,1024]{3,2,1,0:T(8,128)(2,1)S(1)} %get-tuple-element.62), channel_id=1, source_target_pairs={{0,2},{2,4},{4,6},{6,8},{8,10},{10,12},{12,14},{1,3},{3,5},{5,7},{... | collective-permute-start | bytes 393224 | tf_op jit(solution)/shard_map/ppermute | solution.py:555
  121.2 1.5 %collective-permute-start.18 = (bf16[2,4,8,1024]{3,2,1,0:T(8,128)(2,1)S(1)}, bf16[2,4,8,1024]{3,2,1,0:T(8,128)(2,1)S(1)}, u32[]{:S(2)}, u32[]{:S(2)}) collective-permute-start(bf16[2,4,8,1024]{3,2,1,0:T(8,128)(2,1)S(1)} %get-tuple-element.61), channel_id=1, source_target_pairs={{2,0},{4,2},{6,4},{8,6},{10,8},{12,10},{14,12},{3,1},{5,3},{7,5},{... | collective-permute-start | bytes 393224 | tf_op jit(solution)/shard_map/ppermute | solution.py:555
  122.7 2.1 %collective-permute-start.10 = (bf16[1,32,1024]{2,1,0:T(8,128)(2,1)S(1)}, bf16[1,32,1024]{2,1,0:T(8,128)(2,1)S(1)}, u32[]{:S(2)}, u32[]{:S(2)}) collective-permute-start(bf16[1,32,1024]{2,1,0:T(8,128)(2,1)S(1)} %get-tuple-element.27), channel_id=1, source_target_pairs={{0,10},{2,8},{4,14},{6,12},{8,2},{10,0},{12,6},{14,4},{1,11},{3,9}... | collective-permute-start | bytes 196616 | tf_op jit(solution)/shard_map/ppermute | solution.py:559
  124.8 3.3 %collective-permute-start.11 = (bf16[1,32,1024]{2,1,0:T(8,128)(2,1)S(1)}, bf16[1,32,1024]{2,1,0:T(8,128)(2,1)S(1)}, u32[]{:S(2)}, u32[]{:S(2)}) collective-permute-start(bf16[1,32,1024]{2,1,0:T(8,128)(2,1)S(1)} %get-tuple-element.28), channel_id=1, source_target_pairs={{0,12},{2,14},{4,8},{6,10},{8,4},{10,6},{12,0},{14,2},{1,13},{3,15... | collective-permute-start | bytes 196616 | tf_op jit(solution)/shard_map/ppermute | solution.py:559
  128.1 1.8 %collective-permute-start.12 = (bf16[1,32,1024]{2,1,0:T(8,128)(2,1)S(1)}, bf16[1,32,1024]{2,1,0:T(8,128)(2,1)S(1)}, u32[]{:S(2)}, u32[]{:S(2)}) collective-permute-start(bf16[1,32,1024]{2,1,0:T(8,128)(2,1)S(1)} %get-tuple-element.29), channel_id=1, source_target_pairs={{0,14},{2,12},{4,10},{6,8},{8,6},{10,4},{12,2},{14,0},{1,15},{3,13... | collective-permute-start | bytes 196616 | tf_op jit(solution)/shard_map/ppermute | solution.py:559
  129.9 3.0 %collective-permute-done.10 = bf16[1,32,1024]{2,1,0:T(8,128)(2,1)S(1)} collective-permute-done((bf16[1,32,1024]{2,1,0:T(8,128)(2,1)S(1)}, bf16[1,32,1024]{2,1,0:T(8,128)(2,1)S(1)}, u32[]{:S(2)}, u32[]{:S(2)}) %collective-permute-start.10) | collective-permute-done | bytes 65568 | tf_op jit(solution)/shard_map/ppermute | solution.py:559
  132.9 2.2 %collective-permute-done.12 = bf16[1,32,1024]{2,1,0:T(8,128)(2,1)S(1)} collective-permute-done((bf16[1,32,1024]{2,1,0:T(8,128)(2,1)S(1)}, bf16[1,32,1024]{2,1,0:T(8,128)(2,1)S(1)}, u32[]{:S(2)}, u32[]{:S(2)}) %collective-permute-start.12) | collective-permute-done | bytes 65568 | tf_op jit(solution)/shard_map/ppermute | solution.py:559
  135.2 0.1 collective-permute-start.20
  135.3 0.1 shard_map.117
  135.4 0.5 collective-permute-start.19
  136.0 0.5 collective-permute-done.20.refs_12_
  136.5 0.4 collective-permute-done.19.refs_11_
  136.8 0.2 broadcast_in_dim.21.refs_13_
  137.1 8.6 %shard_map.119 = bf16[2048,256]{1,0:T(8,128)(2,1)} custom-call(s32[2]{0:T(128)S(1)} %pad_add_fusion.scalars, bf16[1,4,8,1024]{3,2,1,0:T(8,128)(2,1)S(1)} %bitcast.93, bf16[1,4,8,1024]{3,2,1,0:T(8,128)(2,1)S(1)} %bitcast.95, bf16[1,4,8,1024]{3,2,1,0:T(8,128)(2,1)S(1)} %bitcast.97, bf16[1,4,8,1024]{3,2,1,0:T(8,128)(2,1)S(1)} %bitcast.99, ...), custom_call_target="tpu_custom_call" | custom-call | tf_op jit(solution)/shard_map/pallas_call | solution.py:506
  (44 shorter events, 0.2 us)
Async XLA Ops:
  3.0 60.9 %all-to-all-start = ((bf16[16,2,2,32,640]{4,3,2,1,0:T(8,128)(2,1)}), bf16[16,2,2,32,640]{4,3,2,1,0:T(8,128)(2,1)S(1)}, u32[]{:S(2)}, u32[]{:S(2)}) async-start(bf16[16,2,2,32,640]{4,3,2,1,0:T(8,128)(2,1)} %bitcast.112), calls=%async_computation | async-start | bytes 5242880 | tf_op jit(solution)/shard_map/all_to_all | solution.py:563
  10.4 1.3 copy-start.3
  11.7 1.3 copy-start.4
  13.1 1.3 copy-start.5
  19.9 2.5 %collective-permute-start = (bf16[4,128,640]{2,1,0:T(8,128)(2,1)}, bf16[4,128,640]{2,1,0:T(8,128)(2,1)}, u32[]{:S(2)}, u32[]{:S(2)}) collective-permute-start(bf16[4,128,640]{2,1,0:T(8,128)(2,1)} %get-tuple-element.44), channel_id=1, source_target_pairs={{0,1},{1,0},{2,3},{3,2},{4,5},{5,4},{6,7},{7,6},{8,9},{9,8},{10,11... | collective-permute-start | bytes 1966088 | tf_op jit(solution)/shard_map/ppermute | solution.py:559
  25.1 27.2 %collective-permute-start.1 = (bf16[4,2,2,4,8,640]{5,4,3,2,1,0:T(8,128)(2,1)S(1)}, bf16[4,2,2,4,8,640]{5,4,3,2,1,0:T(8,128)(2,1)S(1)}, u32[]{:S(2)}, u32[]{:S(2)}) collective-permute-start(bf16[4,2,2,4,8,640]{5,4,3,2,1,0:T(8,128)(2,1)S(1)} %get-tuple-element.34), channel_id=1, source_target_pairs={{0,2},{2,0},{4,6},{6,4},{8,10},{10,8},{12,14},{14,12},{1,3},{3,1},... | collective-permute-start | bytes 1966088 | tf_op jit(solution)/shard_map/ppermute | solution.py:559
  53.6 37.3 %collective-permute-start.2 = (bf16[2,2,32,640]{3,2,1,0:T(8,128)(2,1)}, bf16[2,2,32,640]{3,2,1,0:T(8,128)(2,1)S(1)}, u32[]{:S(2)}, u32[]{:S(2)}) collective-permute-start(bf16[2,2,32,640]{3,2,1,0:T(8,128)(2,1)} %pad_maximum_fusion.2), channel_id=1, source_target_pairs={{0,4},{2,6},{4,0},{6,2},{8,12},{10,14},{12,8},{14,10},{1,5},{3,7},... | collective-permute-start | bytes 491528 | tf_op jit(solution)/shard_map/ppermute | solution.py:559
  56.4 17.3 %collective-permute-start.13 = (bf16[2,2,32,640]{3,2,1,0:T(8,128)(2,1)}, bf16[2,2,32,640]{3,2,1,0:T(8,128)(2,1)S(1)}, u32[]{:S(2)}, u32[]{:S(2)}) collective-permute-start(bf16[2,2,32,640]{3,2,1,0:T(8,128)(2,1)} %pad_maximum_fusion.6), channel_id=1, source_target_pairs={{0,4},{2,6},{4,0},{6,2},{8,12},{10,14},{12,8},{14,10},{1,5},{3,7},... | collective-permute-start | bytes 491528 | tf_op jit(solution)/shard_map/ppermute | solution.py:559
  57.2 28.2 %collective-permute-start.14 = (bf16[2,2,32,640]{3,2,1,0:T(8,128)(2,1)}, bf16[2,2,32,640]{3,2,1,0:T(8,128)(2,1)S(1)}, u32[]{:S(2)}, u32[]{:S(2)}) collective-permute-start(bf16[2,2,32,640]{3,2,1,0:T(8,128)(2,1)} %pad_maximum_fusion.7), channel_id=1, source_target_pairs={{0,8},{2,10},{4,12},{6,14},{8,0},{10,2},{12,4},{14,6},{1,9},{3,11}... | collective-permute-start | bytes 491528 | tf_op jit(solution)/shard_map/ppermute | solution.py:559
  59.7 25.7 %collective-permute-start.15 = (bf16[2,2,32,640]{3,2,1,0:T(8,128)(2,1)}, bf16[2,2,32,640]{3,2,1,0:T(8,128)(2,1)S(1)}, u32[]{:S(2)}, u32[]{:S(2)}) collective-permute-start(bf16[2,2,32,640]{3,2,1,0:T(8,128)(2,1)} %pad_maximum_fusion.8), channel_id=1, source_target_pairs={{0,12},{2,14},{4,8},{6,10},{8,4},{10,6},{12,0},{14,2},{1,13},{3,15... | collective-permute-start | bytes 491528 | tf_op jit(solution)/shard_map/ppermute | solution.py:559
  62.9 33.1 %collective-permute-start.3 = (bf16[2,2,32,640]{3,2,1,0:T(8,128)(2,1)}, bf16[2,2,32,640]{3,2,1,0:T(8,128)(2,1)}, u32[]{:S(2)}, u32[]{:S(2)}) collective-permute-start(bf16[2,2,32,640]{3,2,1,0:T(8,128)(2,1)} %pad_maximum_fusion.3), channel_id=1, source_target_pairs={{0,8},{2,10},{4,12},{6,14},{8,0},{10,2},{12,4},{14,6},{1,9},{3,11}... | collective-permute-start | bytes 491528 | tf_op jit(solution)/shard_map/ppermute | solution.py:559
  63.9 22.4 %copy-start.14 = (bf16[1,2,32,640]{3,2,1,0:T(8,128)(2,1)S(1)}, bf16[1,2,32,640]{3,2,1,0:T(8,128)(2,1)}, u32[]{:S(2)}) copy-start(bf16[1,2,32,640]{3,2,1,0:T(8,128)(2,1)} %get-tuple-element.57) | copy-start | bytes 245764
  69.4 1.3 copy-start.1
  85.4 0.9 copy-start.12
  85.4 2.5 %copy-start.13 = (bf16[1,2,32,640]{3,2,1,0:T(8,128)(2,1)S(1)}, bf16[1,2,32,640]{3,2,1,0:T(8,128)(2,1)}, u32[]{:S(2)}) copy-start(bf16[1,2,32,640]{3,2,1,0:T(8,128)(2,1)} %get-tuple-element.60) | copy-start | bytes 245764
  85.4 3.2 %copy-start = (bf16[1280,1024]{1,0:T(8,128)(2,1)S(1)}, bf16[1280,1024]{1,0:T(8,128)(2,1)}, u32[]{:S(2)}) copy-start(bf16[1280,1024]{1,0:T(8,128)(2,1)} %proj_weight.3) | copy-start | bytes 7864324
  85.4 3.2 %copy-start.7 = (f32[1024]{0:T(1024)S(1)}, f32[1024]{0:T(1024)}, u32[]{:S(2)}) copy-start(f32[1024]{0:T(1024)} %param.17) | copy-start | bytes 12292
  86.2 2.3 %collective-permute-start.16 = (bf16[256,640]{1,0:T(8,128)(2,1)S(1)}, bf16[256,640]{1,0:T(8,128)(2,1)S(1)}, u32[]{:S(2)}, u32[]{:S(2)}) collective-permute-start(bf16[256,640]{1,0:T(8,128)(2,1)S(1)} %get-tuple-element.32), channel_id=1, source_target_pairs={{0,1},{1,0},{2,3},{3,2},{4,5},{5,4},{6,7},{7,6},{8,9},{9,8},{10,11... | collective-permute-start | bytes 983048 | tf_op jit(solution)/shard_map/ppermute | solution.py:559
  86.4 9.7 %collective-permute-start.4 = (bf16[2,2,32,640]{3,2,1,0:T(8,128)(2,1)S(1)}, bf16[2,2,32,640]{3,2,1,0:T(8,128)(2,1)S(1)}, u32[]{:S(2)}, u32[]{:S(2)}) collective-permute-start(bf16[2,2,32,640]{3,2,1,0:T(8,128)(2,1)S(1)} %pad_maximum_fusion.4), channel_id=1, source_target_pairs={{0,12},{2,14},{4,8},{6,10},{8,4},{10,6},{12,0},{14,2},{1,13},{3,15... | collective-permute-start | bytes 491528 | tf_op jit(solution)/shard_map/ppermute | solution.py:559
  90.9 5.1 %copy-start.10 = (bf16[2,2,32,640]{3,2,1,0:T(8,128)(2,1)}, bf16[2,2,32,640]{3,2,1,0:T(8,128)(2,1)S(1)}, u32[]{:S(2)}) copy-start(bf16[2,2,32,640]{3,2,1,0:T(8,128)(2,1)S(1)} %collective-permute-done.2.refs_1_.refs_2_) | copy-start | bytes 491524
  96.0 0.7 copy-start.11
  96.7 21.3 %all-to-all-start.1 = ((bf16[8,4,8,1024]{3,2,1,0:T(8,128)(2,1)}), bf16[8,4,8,1024]{3,2,1,0:T(8,128)(2,1)S(1)}, u32[]{:S(2)}, u32[]{:S(2)}) async-start(bf16[8,4,8,1024]{3,2,1,0:T(8,128)(2,1)} %bitcast.113), calls=%async_computation.1 | async-start | bytes 1048576 | tf_op jit(solution)/shard_map/all_to_all | solution.py:563
  103.3 1.6 %copy-start.2 = (bf16[4,512,512]{2,1,0:T(8,128)(2,1)S(1)}, bf16[4,512,512]{2,1,0:T(8,128)(2,1)}, u32[]{:S(2)}) copy-start(bf16[4,512,512]{2,1,0:T(8,128)(2,1)} %copy-done.1) | copy-start | bytes 6291460
  106.8 1.7 %collective-permute-start.5 = (bf16[256,640]{1,0:T(8,128)(2,1)S(1)}, bf16[256,640]{1,0:T(8,128)(2,1)S(1)}, u32[]{:S(2)}, u32[]{:S(2)}) collective-permute-start(bf16[256,640]{1,0:T(8,128)(2,1)S(1)} %get-tuple-element.21), channel_id=1, source_target_pairs={{0,1},{1,0},{2,3},{3,2},{4,5},{5,4},{6,7},{7,6},{8,9},{9,8},{10,11... | collective-permute-start | bytes 983048 | tf_op jit(solution)/shard_map/ppermute | solution.py:559
  110.8 10.4 %collective-permute-start.6 = (bf16[1,32,1024]{2,1,0:T(8,128)(2,1)}, bf16[1,32,1024]{2,1,0:T(8,128)(2,1)S(1)}, u32[]{:S(2)}, u32[]{:S(2)}) collective-permute-start(bf16[1,32,1024]{2,1,0:T(8,128)(2,1)} %get-tuple-element.23), channel_id=1, source_target_pairs={{0,2},{2,0},{4,6},{6,4},{8,10},{10,8},{12,14},{14,12},{1,3},{3,1},... | collective-permute-start | bytes 196616 | tf_op jit(solution)/shard_map/ppermute | solution.py:559
  112.8 9.9 %collective-permute-start.7 = (bf16[1,32,1024]{2,1,0:T(8,128)(2,1)}, bf16[1,32,1024]{2,1,0:T(8,128)(2,1)S(1)}, u32[]{:S(2)}, u32[]{:S(2)}) collective-permute-start(bf16[1,32,1024]{2,1,0:T(8,128)(2,1)} %get-tuple-element.24), channel_id=1, source_target_pairs={{0,4},{2,6},{4,0},{6,2},{8,12},{10,14},{12,8},{14,10},{1,5},{3,7},... | collective-permute-start | bytes 196616 | tf_op jit(solution)/shard_map/ppermute | solution.py:559
  114.3 10.5 %collective-permute-start.8 = (bf16[1,32,1024]{2,1,0:T(8,128)(2,1)}, bf16[1,32,1024]{2,1,0:T(8,128)(2,1)S(1)}, u32[]{:S(2)}, u32[]{:S(2)}) collective-permute-start(bf16[1,32,1024]{2,1,0:T(8,128)(2,1)} %get-tuple-element.25), channel_id=1, source_target_pairs={{0,6},{2,4},{4,2},{6,0},{8,14},{10,12},{12,10},{14,8},{1,7},{3,5},... | collective-permute-start | bytes 196616 | tf_op jit(solution)/shard_map/ppermute | solution.py:559
  114.3 22.8 %copy-start.6 = (bf16[3,3,256,256]{3,2,1,0:T(8,128)(2,1)S(1)}, bf16[3,3,256,256]{3,2,1,0:T(8,128)(2,1)}, u32[]{:S(2)}) copy-start(bf16[3,3,256,256]{3,2,1,0:T(8,128)(2,1)} %param.18) | copy-start | bytes 3538948
  114.3 22.8 %copy-start.8 = (f32[256]{0:T(256)S(1)}, f32[256]{0:T(256)}, u32[]{:S(2)}) copy-start(f32[256]{0:T(256)} %param.19) | copy-start | bytes 3076
  114.3 22.8 %copy-start.9 = (f32[256]{0:T(256)S(1)}, f32[256]{0:T(256)}, u32[]{:S(2)}) copy-start(f32[256]{0:T(256)} %param.21) | copy-start | bytes 3076
  114.3 13.8 %collective-permute-start.9 = (bf16[1,32,1024]{2,1,0:T(8,128)(2,1)S(1)}, bf16[1,32,1024]{2,1,0:T(8,128)(2,1)S(1)}, u32[]{:S(2)}, u32[]{:S(2)}) collective-permute-start(bf16[1,32,1024]{2,1,0:T(8,128)(2,1)S(1)} %get-tuple-element.26), channel_id=1, source_target_pairs={{0,8},{2,10},{4,12},{6,14},{8,0},{10,2},{12,4},{14,6},{1,9},{3,11}... | collective-permute-start | bytes 196616 | tf_op jit(solution)/shard_map/ppermute | solution.py:559
  118.0 17.3 %collective-permute-start.17 = (bf16[2,4,8,1024]{3,2,1,0:T(8,128)(2,1)S(1)}, bf16[2,4,8,1024]{3,2,1,0:T(8,128)(2,1)S(1)}, u32[]{:S(2)}, u32[]{:S(2)}) collective-permute-start(bf16[2,4,8,1024]{3,2,1,0:T(8,128)(2,1)S(1)} %get-tuple-element.62), channel_id=1, source_target_pairs={{0,2},{2,4},{4,6},{6,8},{8,10},{10,12},{12,14},{1,3},{3,5},{5,7},{... | collective-permute-start | bytes 393224 | tf_op jit(solution)/shard_map/ppermute | solution.py:555
  121.2 14.1 %collective-permute-start.18 = (bf16[2,4,8,1024]{3,2,1,0:T(8,128)(2,1)S(1)}, bf16[2,4,8,1024]{3,2,1,0:T(8,128)(2,1)S(1)}, u32[]{:S(2)}, u32[]{:S(2)}) collective-permute-start(bf16[2,4,8,1024]{3,2,1,0:T(8,128)(2,1)S(1)} %get-tuple-element.61), channel_id=1, source_target_pairs={{2,0},{4,2},{6,4},{8,6},{10,8},{12,10},{14,12},{3,1},{5,3},{7,5},{... | collective-permute-start | bytes 393224 | tf_op jit(solution)/shard_map/ppermute | solution.py:555
  122.7 10.2 %collective-permute-start.10 = (bf16[1,32,1024]{2,1,0:T(8,128)(2,1)S(1)}, bf16[1,32,1024]{2,1,0:T(8,128)(2,1)S(1)}, u32[]{:S(2)}, u32[]{:S(2)}) collective-permute-start(bf16[1,32,1024]{2,1,0:T(8,128)(2,1)S(1)} %get-tuple-element.27), channel_id=1, source_target_pairs={{0,10},{2,8},{4,14},{6,12},{8,2},{10,0},{12,6},{14,4},{1,11},{3,9}... | collective-permute-start | bytes 196616 | tf_op jit(solution)/shard_map/ppermute | solution.py:559
  124.8 8.1 %collective-permute-start.11 = (bf16[1,32,1024]{2,1,0:T(8,128)(2,1)S(1)}, bf16[1,32,1024]{2,1,0:T(8,128)(2,1)S(1)}, u32[]{:S(2)}, u32[]{:S(2)}) collective-permute-start(bf16[1,32,1024]{2,1,0:T(8,128)(2,1)S(1)} %get-tuple-element.28), channel_id=1, source_target_pairs={{0,12},{2,14},{4,8},{6,10},{8,4},{10,6},{12,0},{14,2},{1,13},{3,15... | collective-permute-start | bytes 196616 | tf_op jit(solution)/shard_map/ppermute | solution.py:559
  128.1 7.1 %collective-permute-start.12 = (bf16[1,32,1024]{2,1,0:T(8,128)(2,1)S(1)}, bf16[1,32,1024]{2,1,0:T(8,128)(2,1)S(1)}, u32[]{:S(2)}, u32[]{:S(2)}) collective-permute-start(bf16[1,32,1024]{2,1,0:T(8,128)(2,1)S(1)} %get-tuple-element.29), channel_id=1, source_target_pairs={{0,14},{2,12},{4,10},{6,8},{8,6},{10,4},{12,2},{14,0},{1,15},{3,13... | collective-permute-start | bytes 196616 | tf_op jit(solution)/shard_map/ppermute | solution.py:559
  135.2 1.3 collective-permute-start.20
  135.4 1.4 collective-permute-start.19
